TPU v7x, 32 devices: a whole 2x2x4 slice. The times are simulated.
32 devices in a mesh: mesh: 8 (over y, x, core), four: 4 (over z).
Axes of the slice: x: 2, y: 2, z: 4, core: 2. Of those that a mesh axis runs over, the one named last changes fastest.
Arguments:
- adj_modes: float32 [3, 256, 64, 2048], P(None, 'four', None, 'mesh'), may hold values from -1 to 1
- base_flow: bfloat16 [12, 256, 64, 2048], P(None, None, 'four', 'mesh'), may hold values from -6 to 6
- geometry: float32 [4, 64, 2048], P(None, None, 'mesh'), may hold values from -1 to 1
- mass: float32 [64, 2048], P(None, 'mesh'), may hold values from 0.2 to 2
- connect: int32 [64, 2048], P(None, 'mesh'), may hold values from 0 to 12824, as said below
- edge_nodes: int32 [8, 2, 225], P('mesh'), may hold values from 0 to 12824, as said below
Outputs:
- adj_next: float32 [3, 256, 64, 2048], P(None, 'four', None, 'mesh')
Inputs may be any that keep to these rules, and one draw needn't show every extreme that they name: `connect`: columns p * 256 to (p + 1) * 256 - 1 form partition p. Each partition numbers its 12825 nodes from 0; element nodes at the same place share an id, and every id is used. edge_nodes[p, 1] lists the ids of partition p's nodes that coincide with nodes of partition p + 1 (mod 8), in the same order in which edge_nodes[p + 1, 0] lists them; the two lists of a partition are disjoint, and no other node is shared between partitions.
All inputs are finite; a program needn't handle non-finite values.
Results may differ from a plain program's by a relative error of at most 0.0003.
Values sent between devices are 32-bit elements; how exact they have to be, the bound alone decides.
No kernel may reach another device: no remote copies, remote signals or barrier semaphores. Data moves between devices by JAX's collectives and lax.ppermute only.
A program may use at most 256 MiB of HBM per device.

v0:
```python
import math

import jax
import jax.numpy as jnp
from jax import lax
from jax.sharding import PartitionSpec as P

NP = 8
PLANES = 256
UNIQUE = 12825


STEP_SIZE = 0.1
HIGH = lax.Precision.HIGHEST


def padded(shard, sides, width):
    for axis, dim in sides:
        count, length = (lax.axis_size(axis), shard.shape[dim])
        up = [(i, (i + 1) % count) for i in range(count)]
        down = [(j, i) for i, j in up]
        last = lax.slice_in_dim(shard, length - width, length, axis=dim)
        leading = lax.slice_in_dim(shard, 0, width, axis=dim)
        before = lax.ppermute(last, axis, up)
        after = lax.ppermute(leading, axis, down)
        shard = jnp.concatenate([before, shard, after], axis=dim)
    return shard


def legendre_values(degree, point):
    before = 1.0
    current = point
    for order in range(1, degree):
        after = ((2 * order + 1) * point * current - order * before) / (order + 1)
        before = current
        current = after
    return (current, before)


def gll_derivative(points_n):
    degree = points_n - 1
    points = []
    for index in range(points_n):
        point = -math.cos(math.pi * index / degree)
        for sweep in range(100):
            top_val, below_val = legendre_values(degree, point)
            point = point - (point * top_val - below_val) / (points_n * top_val)
        points.append(point)
    values = [legendre_values(degree, point)[0] for point in points]
    deriv_rows = []
    for row_index in range(points_n):
        row_vals = []
        for col_index in range(points_n):
            if row_index != col_index:
                row_vals.append(
                    values[row_index]
                    / (values[col_index] * (points[row_index] - points[col_index]))
                )
            else:
                row_vals.append(0.0)
        deriv_rows.append(row_vals)
    deriv_rows[0][0] = -degree * (degree + 1) / 4.0
    deriv_rows[degree][degree] = degree * (degree + 1) / 4.0
    deriv_table = jnp.asarray(deriv_rows, jnp.float32)
    identity = jnp.eye(points_n, dtype=jnp.float32)
    return (jnp.kron(deriv_table, identity), jnp.kron(identity, deriv_table))


def plane_tables(planes):
    plane_idx = jnp.arange(planes, dtype=jnp.int32)
    wave_idx = plane_idx // 2
    phase = (plane_idx[:, None] * wave_idx[None, :] % planes).astype(jnp.float32) * (
        2.0 * math.pi / planes
    )
    is_sine = plane_idx % 2 == 1
    synth = jnp.where(is_sine[None, :], jnp.sin(phase), jnp.cos(phase))
    alternate = (1 - 2 * (plane_idx % 2)).astype(jnp.float32)
    synth = synth.at[:, 1].set(alternate)
    scales = jnp.where(wave_idx == 0, 1.0 / planes, 2.0 / planes).astype(jnp.float32)
    analysis = synth.T * scales[:, None]
    return (synth, analysis)


def axial(coef, wave):
    pairs = coef.reshape(coef.shape[0], coef.shape[1] // 2, 2, coef.shape[2], coef.shape[3])
    factor = wave[None, :, None, None]
    return jnp.stack([factor * pairs[:, :, 1], -factor * pairs[:, :, 0]], axis=2).reshape(
        coef.shape
    )


def gradients(coef, geometry, deriv_r, deriv_s):
    along_r = jnp.einsum("mn,fpne->fpme", deriv_r, coef, precision=HIGH)
    along_s = jnp.einsum("mn,fpne->fpme", deriv_s, coef, precision=HIGH)
    grad_x = geometry[0] * along_r + geometry[1] * along_s
    grad_y = geometry[2] * along_r + geometry[3] * along_s
    return (grad_x, grad_y)


def advect(physical, base):
    pieces = []
    for component in range(3):
        total = jnp.zeros(physical.shape[1:], jnp.float32)
        for direction in range(3):
            total = (
                total
                - base[direction].astype(jnp.float32) * physical[3 + 3 * direction + component]
                + physical[direction] * base[3 + 3 * component + direction].astype(jnp.float32)
            )
        pieces.append(total)
    return jnp.stack(pieces)


def assemble(weighted, mass, connect, edges):
    fields_n, planes_dev, points_n, elems_n = weighted.shape
    node_ids = connect.reshape(-1)
    rows = jnp.concatenate([weighted.reshape(fields_n * planes_dev, -1), mass.reshape(1, -1)])
    summed = jnp.zeros((rows.shape[0], UNIQUE), jnp.float32).at[:, node_ids].add(rows)
    lower = edges[0]
    upper = edges[1]
    rims = jnp.stack([summed[:, lower], summed[:, upper]])
    widened = padded(rims, (("mesh", 0),), 1)
    summed = summed.at[:, lower].set(widened[1] + widened[0])
    summed = summed.at[:, upper].set(widened[2] + widened[3])
    spread_back = summed[:, node_ids]
    result = spread_back[:-1] / spread_back[-1:]
    return result.reshape(weighted.shape)


def body(adj_modes, base_flow, geometry, mass, connect, edge_nodes):
    deriv_r, deriv_s = gll_derivative(NP)
    synth, analysis = plane_tables(PLANES)
    planes_dev = adj_modes.shape[1]
    grad_x, grad_y = gradients(adj_modes, geometry, deriv_r, deriv_s)
    pair_first = lax.axis_index("four") * (planes_dev // 2)
    wave = (pair_first + jnp.arange(planes_dev // 2, dtype=jnp.int32)).astype(jnp.float32) * (
        2.0 / PLANES
    )
    grad_z = axial(adj_modes, wave)
    packed = jnp.concatenate([adj_modes, grad_x, grad_y, grad_z])
    spread = lax.all_to_all(packed, "four", split_axis=2, concat_axis=1, tiled=True)
    physical = jnp.einsum("jm,fmne->fjne", synth, spread, precision=HIGH)
    forcing = advect(physical, base_flow)
    forcing_modes = jnp.einsum("mj,fjne->fmne", analysis, forcing, precision=HIGH)
    returned = lax.all_to_all(forcing_modes, "four", split_axis=1, concat_axis=2, tiled=True)
    weighted = mass * (adj_modes + STEP_SIZE * returned)
    return assemble(weighted, mass, connect, edge_nodes[0])


def solution(mesh):
    return jax.shard_map(
        body,
        mesh=mesh,
        in_specs=(
            P(None, "four", None, "mesh"),
            P(None, None, "four", "mesh"),
            P(None, None, "mesh"),
            P(None, "mesh"),
            P(None, "mesh"),
            P("mesh", None, None),
        ),
        out_specs=P(None, "four", None, "mesh"),
        check_vma=False,
    )
```

profile of v0, /device:TPU:9, one launch (start us, length us, event | category | flops | bytes accessed | tf_op | source)
XLA Modules:
  0.0 2037.4 jit_solution(12220155417862914626)
XLA Ops:
  2.1 16.8 fusion.60
  18.9 9.5 slice_multiply_fusion.1
  28.3 9.4 pad_maximum_fusion.1
  37.8 23.4 %add_bitcast_fusion.1 = (f32[3,64,64,256]{3,2,1,0:T(8,128)}, f32[3,64,64,256]{3,2,1,0:T(8,128)}) fusion(f32[64,3,64,256]{3,0,2,1:T(8,128)} %fusion.60, f32[64,256]{1,0:T(8,128)S(1)} %get-tuple-element.34, f32[64,256]{1,0:T(8,128)S(1)} %get-tuple-element.33, f32[64,256]{1,0:T(8,128)S(1)} %get-tuple-element.35, f32[64,256]{1,0:T(8,128)S(1)} %get-tuple-element.36, ...), kind=kOutput, calls=%fused_computation.26 | convolution fusion | flops 2434793472 | bytes 50610176 | tf_op jit(solution)/shard_map/mn,fpne->fpme/dot_general | solution.py:93
  61.2 33.7 %pad_maximum_fusion = f32[12,64,64,256]{3,2,1,0:T(8,128)} fusion(f32[3,64,64,256]{3,2,1,0:T(8,128)} %bitcast.114, f32[3,64,64,256]{3,2,1,0:T(8,128)} %get-tuple-element.30, f32[3,64,64,256]{3,2,1,0:T(8,128)} %get-tuple-element.29, f32[3,64,64,256]{3,2,1,0:T(8,128)} %param.9), kind=kLoop, calls=%fused_computation.6 | loop fusion | flops 37748736 | bytes 100663296 | tf_op jit(solution)/shard_map/concatenate | solution.py:140
  94.9 46.1 %copy.105 = f32[12,64,64,256]{3,1,0,2:T(8,128)} copy(f32[12,64,64,256]{3,2,1,0:T(8,128)} %pad_maximum_fusion) | data formatting | bytes 100663296 | tf_op jit(solution)/shard_map/concatenate | solution.py:140
  141.0 12.1 all-to-all-start
  153.2 18.0 fusion.69
  224.6 1007.1 %all-to-all-done = f32[12,64,64,256]{3,1,0,2:T(8,128)} async-done(((f32[12,64,64,256]{3,1,0,2:T(8,128)}), f32[12,64,64,256]{3,1,0,2:T(8,128)}, u32[]{:S(2)}, u32[]{:S(2)}) %all-to-all-start) | async-done | bytes 50331680 | tf_op jit(solution)/shard_map/all_to_all | solution.py:141
  1231.7 45.9 %copy.107 = f32[12,4,64,16,256]{4,3,2,1,0:T(8,128)} copy(f32[12,4,64,16,256]{4,2,0,3,1:T(8,128)} %bitcast.13) | data formatting | bytes 100663296 | tf_op jit(solution)/shard_map/all_to_all | solution.py:141
  1277.6 99.8 %fusion.2 = f32[12,256,16,256]{1,3,2,0:T(8,128)} fusion(f32[12,256,16,256]{3,2,1,0:T(8,128)} %bitcast.111, f32[256,256]{1,0:T(8,128)S(1)} %scatter.19), kind=kOutput, calls=%fused_computation.9 | convolution fusion | flops 38654705664 | bytes 100925440 | tf_op jit(solution)/shard_map/jm,fmne->fjne/dot_general | solution.py:142
  1377.5 11.2 fusion.24
  1388.7 14.1 fusion.30
  1402.8 13.3 fusion.36
  1416.0 15.1 fusion.16
  1431.1 12.8 copy.120
  1444.0 9.7 all-to-all-start.1
  1458.9 263.5 %all-to-all-done.1 = f32[3,256,16,256]{3,2,0,1:T(8,128)} async-done(((f32[3,256,16,256]{3,2,0,1:T(8,128)}), f32[3,256,16,256]{3,2,0,1:T(8,128)}, u32[]{:S(2)}, u32[]{:S(2)}) %all-to-all-start.1) | async-done | bytes 12582944 | tf_op jit(solution)/shard_map/all_to_all | solution.py:145
  1722.4 11.5 copy_multiply_fusion
  1733.9 11.4 copy.122
  1745.3 14.8 fusion.14
  1760.1 20.2 copy.144
  1780.2 14.9 copy.123
  1795.2 98.0 %scatter_custom_fusion = f32[193,12825]{0,1:T(8,128)} fusion(s32[16384]{0:T(1024)S(1)} %bitcast.124, f32[1,16384]{0,1:T(8,128)} %copy.146, f32[]{:T(128)} %constant.108, f32[192,16384]{0,1:T(8,128)} %copy.123, f32[]{:T(128)} %constant.91.clone.1), kind=kCustom, calls=%fused_computation.11 | custom fusion | flops 6324224 | bytes 22549356 | tf_op jit(solution)/shard_map/scatter-add | solution.py:118
  1893.2 5.6 gather_fusion.1
  1902.0 5.6 gather_fusion
  1907.7 10.7 scatter_custom_fusion.1
  1918.4 10.7 scatter_custom_fusion.2
  1929.2 67.1 %gather_fusion.2 = f32[16384,193]{1,0:T(8,128)} fusion(f32[193,12825]{0,1:T(8,128)} %scatter_custom_fusion.2, s32[16384]{0:T(1024)S(1)} %broadcast_clamp_fusion), kind=kCustom, calls=%fused_computation.2 | custom fusion | bytes 25362432 | tf_op jit(solution)/shard_map/gather | solution.py:125
  1996.2 15.1 copy.125
  2012.5 10.6 slice_divide_fusion
  2023.1 14.1 copy.147
  (52 shorter events, 64.9 us)
Async XLA Ops:
  141.0 1090.7 %all-to-all-start = ((f32[12,64,64,256]{3,1,0,2:T(8,128)}), f32[12,64,64,256]{3,1,0,2:T(8,128)}, u32[]{:S(2)}, u32[]{:S(2)}) async-start(f32[12,64,64,256]{3,1,0,2:T(8,128)} %copy.105), calls=%async_computation | async-start | bytes 100663296 | tf_op jit(solution)/shard_map/all_to_all | solution.py:141
  1277.6 99.8 %copy-start = (bf16[1,256,16,256]{1,3,2,0:T(8,128)(2,1)S(1)}, bf16[1,256,16,256]{1,3,2,0:T(8,128)(2,1)}, u32[]{:S(2)}) copy-start(bf16[1,256,16,256]{1,3,2,0:T(8,128)(2,1)} %copy.133) | copy-start | bytes 6291460
  1277.6 99.8 %copy-start.1 = (bf16[1,256,16,256]{1,3,2,0:T(8,128)(2,1)S(1)}, bf16[1,256,16,256]{1,3,2,0:T(8,128)(2,1)}, u32[]{:S(2)}) copy-start(bf16[1,256,16,256]{1,3,2,0:T(8,128)(2,1)} %copy.135) | copy-start | bytes 6291460
  1277.6 99.8 %copy-start.2 = (bf16[1,256,16,256]{1,3,2,0:T(8,128)(2,1)S(1)}, bf16[1,256,16,256]{1,3,2,0:T(8,128)(2,1)}, u32[]{:S(2)}) copy-start(bf16[1,256,16,256]{1,3,2,0:T(8,128)(2,1)} %copy.132) | copy-start | bytes 6291460
  1388.7 14.1 copy-start.3
  1444.0 9.7 copy-start.5
  1444.0 9.8 copy-start.4
  1444.0 278.5 %all-to-all-start.1 = ((f32[3,256,16,256]{3,2,0,1:T(8,128)}), f32[3,256,16,256]{3,2,0,1:T(8,128)}, u32[]{:S(2)}, u32[]{:S(2)}) async-start(f32[3,256,16,256]{3,2,0,1:T(8,128)} %copy.120), calls=%async_computation.1 | async-start | bytes 25165824 | tf_op jit(solution)/shard_map/all_to_all | solution.py:145
  1453.9 4.9 copy-start.6
  1898.8 8.9 collective-permute-start
  1907.6 10.8 collective-permute-start.1
where the time goes:
time: 2050 us; the launch traced here: 2040 us
  waiting for transfers between devices  1270 us (62%)
  local copies, waits for them, and re-layouts  335 us (16%)
  other arithmetic  251 us (12%)
  matrix products  155 us (8%)
  starting transfers between devices  25.1 us (1%)
    all_to_all x1, waiting for transfers between devices, body(): lax.all_to_all(packed, 'four', split_axis=2, concat_axis=1, tiled=True)  1010 us
    all_to_all x1, waiting for transfers between devices, body(): lax.all_to_all(forcing_modes, 'four', split_axis=1, concat_axis=2, tiled=...  264 us
    dot_general x1, matrix products, body(): physical = jnp.einsum('jm,fmne->fjne', synth, spread, precision=HIGH)  99.8 us
    scatter-add x1, other arithmetic, assemble(): jnp.zeros((rows.shape[0], UNIQUE), jnp.float32).at[:, node_ids].add(rows)  98 us
    unnamed x30, local copies, waits for them, and re-layouts  84.7 us
    gather x2, local copies, waits for them, and re-layouts, assemble(): spread_back = summed[:, node_ids]  82.2 us
    concatenate x1, local copies, waits for them, and re-layouts, body(): packed = jnp.concatenate([adj_modes, grad_x, grad_y, grad_z])  46.1 us
    all_to_all x1, local copies, waits for them, and re-layouts, body(): lax.all_to_all(packed, 'four', split_axis=2, concat_axis=1, tiled=True)  45.9 us
  transfers between devices with their start and end apart: 4, of which 2 were waited for; matrix products, arithmetic and copies ran while one was open for 5% of the time, Pallas kernels for 0%

commit v1 on v0

v1 whole, which is shorter than its diff:
```python
import functools
import math

import jax
import jax.numpy as jnp
import numpy as np
from jax import lax
from jax.experimental import pallas as pl
from jax.experimental.pallas import tpu as pltpu
from jax.sharding import PartitionSpec as P

NP = 8
PLANES = 256
UNIQUE = 12825
STEP_SIZE = 0.1
HIGH = lax.Precision.HIGHEST
LANES = 128
BATCH = 8
VMEM_LIMIT = 56 * 1024 * 1024


def legendre_values(degree, point):
    before = 1.0
    current = point
    for order in range(1, degree):
        after = ((2 * order + 1) * point * current - order * before) / (order + 1)
        before = current
        current = after
    return (current, before)


def gll_derivative(points_n):
    degree = points_n - 1
    points = []
    for index in range(points_n):
        point = -math.cos(math.pi * index / degree)
        for sweep in range(100):
            top_val, below_val = legendre_values(degree, point)
            point = point - (point * top_val - below_val) / (points_n * top_val)
        points.append(point)
    values = [legendre_values(degree, point)[0] for point in points]
    deriv_rows = []
    for row_index in range(points_n):
        row_vals = []
        for col_index in range(points_n):
            if row_index != col_index:
                row_vals.append(
                    values[row_index]
                    / (values[col_index] * (points[row_index] - points[col_index]))
                )
            else:
                row_vals.append(0.0)
        deriv_rows.append(row_vals)
    deriv_rows[0][0] = -degree * (degree + 1) / 4.0
    deriv_rows[degree][degree] = degree * (degree + 1) / 4.0
    return deriv_rows


def plane_tables(planes):
    plane = np.arange(planes)
    wave = plane // 2
    phase = ((plane[:, None] * wave[None, :]) % planes) * (2.0 * math.pi / planes)
    synth = np.where((plane % 2 == 1)[None, :], np.sin(phase), np.cos(phase))
    synth[:, 1] = 1 - 2 * (plane % 2)
    scales = np.where(wave == 0, 1.0 / planes, 2.0 / planes)
    analysis = synth.T * scales[:, None]
    number = wave * (2.0 / planes)
    along = np.zeros_like(synth)
    along[:, 1::2] = number[1::2] * synth[:, 0::2]
    along[:, 0::2] = -number[0::2] * synth[:, 1::2]
    along[:, :2] = 0.0
    return tuple(jnp.asarray(t, jnp.float32) for t in (synth, along, analysis))


def params(**kw):
    return pltpu.CompilerParams(vmem_limit_bytes=VMEM_LIMIT, **kw)


def derivative(x, groups):
    a_n, c_n, l_n, m_n, e_n = x.shape
    deriv = gll_derivative(NP)
    rows = 8

    def kernel(x_ref, o_ref):
        for line in groups:
            vals = [x_ref[a, 0, l] for a, l in line]
            for i, (a, l) in enumerate(line):
                total = deriv[i][0] * vals[0]
                for k in range(1, NP):
                    if deriv[i][k] != 0.0:
                        total = total + deriv[i][k] * vals[k]
                o_ref[a, 0, l] = total

    spec = pl.BlockSpec((a_n, 1, l_n, rows, e_n), lambda c, m: (0, c, 0, m, 0))
    return pl.pallas_call(
        kernel,
        grid=(c_n, m_n // rows),
        in_specs=[spec],
        out_specs=spec,
        out_shape=jax.ShapeDtypeStruct(x.shape, jnp.float32),
        compiler_params=params(),
        cost_estimate=pl.CostEstimate(flops=16 * x.size, bytes_accessed=8 * x.size, transcendentals=0),
        name="line_derivative",
    )(x)


def base_products(synth, along, u, us, base, geo):
    s_n, c_n, l_n, m_n, e_n = u.shape
    p_n = base.shape[2]

    def kernel(synth_ref, along_ref, u_ref, us_ref, b_ref, g_ref, vr_ref, part_ref):
        l = pl.program_id(0)
        s_mat = synth_ref[...]
        z_mat = along_ref[...]
        field = lambda i: b_ref[i, 0].astype(jnp.float32)
        dot = functools.partial(jnp.dot, precision=HIGH, preferred_element_type=jnp.float32)
        g = [g_ref[i, pl.ds(l, 1), :] for i in range(4)]
        ux, uy = field(0), field(1)
        vr_ref[0] = ux * g[0] + uy * g[2]
        vs = ux * g[1] + uy * g[3]
        uz = field(2)
        phys = []
        for c in range(3):
            coef = u_ref[:, c, 0].reshape(s_n * m_n, e_n)
            phys.append(dot(s_mat, coef))
            dz = dot(z_mat, coef)
            ds = dot(s_mat, us_ref[:, c, 0].reshape(s_n * m_n, e_n))
            part_ref[c, 0] = -(vs * ds) - uz * dz
        for c in range(3):
            part_ref[c, 0] += phys[0] * field(3 + 3 * c) + phys[1] * field(4 + 3 * c) + phys[2] * field(5 + 3 * c)

    whole = pl.BlockSpec((p_n, p_n), lambda l: (0, 0))
    coefs = pl.BlockSpec((s_n, 3, 1, m_n, e_n), lambda l: (0, 0, l, 0, 0))
    return pl.pallas_call(
        kernel,
        grid=(l_n,),
        in_specs=[
            whole,
            whole,
            coefs,
            coefs,
            pl.BlockSpec((12, 1, p_n, e_n), lambda l: (0, l, 0, 0)),
            pl.BlockSpec((4, l_n, e_n), lambda l: (0, 0, 0)),
        ],
        out_specs=[
            pl.BlockSpec((1, p_n, e_n), lambda l: (l, 0, 0)),
            pl.BlockSpec((3, 1, p_n, e_n), lambda l: (0, l, 0, 0)),
        ],
        out_shape=[
            jax.ShapeDtypeStruct((l_n, p_n, e_n), jnp.float32),
            jax.ShapeDtypeStruct((3, l_n, p_n, e_n), jnp.float32),
        ],
        compiler_params=params(),
        cost_estimate=pl.CostEstimate(
            flops=9 * 2 * 6 * l_n * p_n * p_n * e_n, bytes_accessed=l_n * p_n * e_n * 64, transcendentals=0
        ),
        name="base_products",
    )(synth, along, u, us, base, geo)


def forcing_modes(synth, analysis, ur, vr, part, mass, first):
    s_n, c_n, l_n, m_n, e_n = ur.shape
    p_n = vr.shape[1]

    def kernel(synth_ref, analysis_ref, ur_ref, vr_ref, part_ref, mass_ref, o_ref):
        l = pl.program_id(1)
        dot = functools.partial(jnp.dot, precision=HIGH, preferred_element_type=jnp.float32)
        dr = dot(synth_ref[...], ur_ref[:, 0, 0].reshape(s_n * m_n, e_n))
        forcing = part_ref[0, 0] - vr_ref[0] * dr
        modes = dot(analysis_ref[...], forcing) * (STEP_SIZE * mass_ref[pl.ds(l, 1), :])
        o_ref[:, 0, 0] = modes.reshape(s_n, m_n, e_n)

    whole = pl.BlockSpec((p_n, p_n), lambda c, l: (0, 0))
    coefs = pl.BlockSpec((s_n, 1, 1, m_n, e_n), lambda c, l: (0, c, l, 0, 0))
    return pl.pallas_call(
        kernel,
        grid=(c_n, l_n),
        in_specs=[
            whole,
            whole,
            coefs,
            pl.BlockSpec((1, p_n, e_n), lambda c, l: (l, 0, 0)),
            pl.BlockSpec((1, 1, p_n, e_n), lambda c, l: (first + c, l, 0, 0)),
            pl.BlockSpec((l_n, e_n), lambda c, l: (0, 0)),
        ],
        out_specs=coefs,
        out_shape=jax.ShapeDtypeStruct(ur.shape, jnp.float32),
        compiler_params=params(),
        cost_estimate=pl.CostEstimate(
            flops=2 * 2 * 6 * c_n * l_n * p_n * p_n * e_n,
            bytes_accessed=c_n * l_n * p_n * e_n * 16,
            transcendentals=0,
        ),
        name="forcing_modes",
    )(synth, analysis, ur, vr, part, mass)


def local_sums(modes, u, mass, pairs, edge_reps, first):
    s_n, c_n, l_n, m_n, e_n = modes.shape
    nodes_n = s_n * l_n
    rows_n = nodes_n * e_n
    step = min(8, l_n)
    per = l_n // step
    close_k, close_r, close_n, far_k, far_r, far_n = pairs
    edges_n = edge_reps.shape[1]
    feats = c_n * m_n

    def kernel(ck, cr, cn, fk, fr, fn, er, f_ref, u_ref, mass_ref, o_ref, e_ref):
        b = pl.program_id(0)

        def fill(t, _):
            node = b * step + t
            weight = mass_ref[pl.ds(node, 1), :]
            rows = [f_ref[0, c, t] + weight * u_ref[0, c, t] for c in range(c_n)]
            if feats < LANES:
                rows.append(jnp.zeros((LANES - feats, e_n), jnp.float32))
            table = jnp.concatenate(rows, axis=0)
            o_ref[pl.ds(pl.multiple_of(node * e_n, e_n), e_n), :] = table.T
            return 0

        lax.fori_loop(0, step, fill, 0)

        @pl.when(b == pl.num_programs(0) - 1)
        def _():
            o_ref[pl.ds(rows_n, 8), :] = jnp.zeros((8, LANES), jnp.float32)

            def close(i, _):
                heads = [cr[i * BATCH + t] for t in range(BATCH)]
                others = [ck[i * BATCH + t] for t in range(BATCH)]
                sums = [o_ref[pl.ds(r, 1), :] + o_ref[pl.ds(k, 1), :] for r, k in zip(heads, others)]
                for r, total in zip(heads, sums):
                    o_ref[pl.ds(r, 1), :] = total
                return 0

            lax.fori_loop(0, pl.cdiv(cn[0], BATCH), close, 0)

            def far(i, _):
                r = fr[i]
                o_ref[pl.ds(r, 1), :] = o_ref[pl.ds(r, 1), :] + o_ref[pl.ds(fk[i], 1), :]
                return 0

            lax.fori_loop(0, fn[0], far, 0)

            def edge(i, _):
                for side in range(2):
                    for t in range(BATCH):
                        e_ref[side, pl.ds(i * BATCH + t, 1), :] = o_ref[pl.ds(er[side, i * BATCH + t], 1), :]
                return 0

            lax.fori_loop(0, edges_n // BATCH, edge, 0)

    smem = pl.BlockSpec(memory_space=pltpu.SMEM)
    where = lambda b: (b // per, 0, b % per, 0, 0)
    where_u = lambda b: (b // per, first // c_n, b % per, 0, 0)
    return pl.pallas_call(
        kernel,
        grid=(nodes_n // step,),
        in_specs=[smem] * 7
        + [
            pl.BlockSpec((1, c_n, step, m_n, e_n), where),
            pl.BlockSpec((1, c_n, step, m_n, e_n), where_u),
            pl.BlockSpec((nodes_n, e_n), lambda b: (0, 0)),
        ],
        out_specs=[
            pl.BlockSpec((rows_n + 8, LANES), lambda b: (0, 0)),
            pl.BlockSpec((2, edges_n, LANES), lambda b: (0, 0, 0)),
        ],
        out_shape=[
            jax.ShapeDtypeStruct((rows_n + 8, LANES), jnp.float32),
            jax.ShapeDtypeStruct((2, edges_n, LANES), jnp.float32),
        ],
        compiler_params=params(),
        cost_estimate=pl.CostEstimate(
            flops=rows_n * LANES * 400, bytes_accessed=rows_n * LANES * 12, transcendentals=0
        ),
        name="local_sums",
    )(close_k, close_r, close_n, far_k, far_r, far_n, edge_reps, modes, u, mass)


def spread(table, came, edge_reps, back_k, back_r, inverse, held, shape, first, c_n):
    _, m_n, nodes_n, e_n = shape
    rows_n = nodes_n * e_n
    step = 8
    edges_n = edge_reps.shape[1]
    pairs_n = back_k.shape[0]

    def kernel(er, bk, br, t_ref, came_ref, inv_ref, *rest):
        o_ref, work = rest[-2], t_ref
        b = pl.program_id(0)

        @pl.when(b == 0)
        def _():
            def edge(i, _):
                for side in range(2):
                    spots = [er[side, i * BATCH + t] for t in range(BATCH)]
                    sums = [
                        work[pl.ds(r, 1), :] + came_ref[side, pl.ds(i * BATCH + t, 1), :]
                        for t, r in enumerate(spots)
                    ]
                    for r, total in zip(spots, sums):
                        work[pl.ds(r, 1), :] = total
                return 0

            lax.fori_loop(0, edges_n // BATCH, edge, 0)

            def back(i, _):
                got = [work[pl.ds(br[i * BATCH + t], 1), :] for t in range(BATCH)]
                for t, row in enumerate(got):
                    work[pl.ds(bk[i * BATCH + t], 1), :] = row
                return 0

            lax.fori_loop(0, pairs_n // BATCH, back, 0)

        stage = rest[-1]

        def node(t, _):
            n = b * step + t
            rows = work[pl.ds(pl.multiple_of(n * e_n, e_n), e_n), :].T
            scaled = rows * inv_ref[pl.ds(n, 1), :]
            for c in range(c_n):
                stage[c, t] = scaled[c * m_n : (c + 1) * m_n]
            return 0

        lax.fori_loop(0, step, node, 0)
        for c in range(c_n):
            o_ref[c] = jnp.swapaxes(stage[c], 0, 1)

    smem = pl.BlockSpec(memory_space=pltpu.SMEM)
    in_specs = [smem] * 3 + [
        pl.BlockSpec((rows_n + 8, LANES), lambda b: (0, 0)),
        pl.BlockSpec((2, edges_n, LANES), lambda b: (0, 0, 0)),
        pl.BlockSpec((nodes_n, e_n), lambda b: (0, 0)),
    ]
    args = [edge_reps, back_k, back_r, table, came, inverse]
    aliases = {}
    if held is not None:
        in_specs.append(pl.BlockSpec(memory_space=pl.ANY))
        args.append(held)
        aliases = {len(args) - 1: 0}
    return pl.pallas_call(
        kernel,
        grid=(nodes_n // step,),
        in_specs=in_specs,
        out_specs=pl.BlockSpec((c_n, m_n, step, e_n), lambda b: (first // c_n, 0, b, 0)),
        out_shape=jax.ShapeDtypeStruct(shape, jnp.float32),
        scratch_shapes=[pltpu.VMEM((c_n, step, m_n, e_n), jnp.float32)],
        input_output_aliases=aliases,
        compiler_params=params(),
        cost_estimate=pl.CostEstimate(
            flops=rows_n * LANES * 400, bytes_accessed=rows_n * LANES * 12, transcendentals=0
        ),
        name="spread",
    )(*args)


def fill_up(values, multiple, filler):
    short = -values.shape[-1] % multiple
    pad = [(0, 0)] * (values.ndim - 1) + [(0, short)]
    return jnp.pad(values, pad, constant_values=filler)


def pair_lists(ids, edges):
    rows_n = ids.shape[0]
    place = jnp.arange(rows_n, dtype=jnp.int32)
    ids_sorted, member = lax.sort((ids, place), num_keys=1)
    head = jnp.concatenate([jnp.ones((1,), bool), ids_sorted[1:] != ids_sorted[:-1]])
    code = lax.cummax(jnp.where(head, place * rows_n + member, 0))
    rep = code % rows_n
    rank = place - code // rows_n
    group = jnp.where(rank == 0, 2, jnp.where(rank == 1, 0, 1)).astype(jnp.int32)
    _, member_l, rep_l = lax.sort((group, member, rep), num_keys=1)
    pairs_n = rows_n - UNIQUE
    member_l = member_l[:pairs_n]
    rep_l = rep_l[:pairs_n]
    close_n = jnp.sum(group == 0, dtype=jnp.int32)
    far_n = pairs_n - close_n
    spot = jnp.arange(pairs_n, dtype=jnp.int32)
    close_k = fill_up(jnp.where(spot < close_n, member_l, rows_n), BATCH, rows_n)
    close_r = fill_up(jnp.where(spot < close_n, rep_l, rows_n), BATCH, rows_n)
    far_k = jnp.roll(member_l, -close_n)
    far_r = jnp.roll(rep_l, -close_n)
    back_k = fill_up(member_l, BATCH, rows_n)
    back_r = fill_up(rep_l, BATCH, rows_n)
    flat = edges.reshape(-1)
    start = jnp.sum(ids_sorted[None, :] < flat[:, None], axis=1, dtype=jnp.int32)
    edge_reps = fill_up(member[start].reshape(edges.shape), BATCH, rows_n)
    pairs = (close_k, close_r, close_n.reshape(1), far_k, far_r, far_n.reshape(1))
    return pairs, (back_k, back_r), edge_reps


def swap_edges(sums):
    count = lax.axis_size("mesh")
    up = [(i, (i + 1) % count) for i in range(count)]
    down = [(j, i) for i, j in up]
    return jnp.stack([lax.ppermute(sums[1], "mesh", up), lax.ppermute(sums[0], "mesh", down)])


def inverse_mass(mass, ids, edges):
    summed = jnp.zeros((UNIQUE,), jnp.float32).at[ids].add(mass.reshape(-1))
    came = swap_edges(summed[edges])
    summed = summed.at[edges.reshape(-1)].add(came.reshape(-1))
    return (1.0 / summed[ids]).reshape(mass.shape)


def exchange(x):
    return lax.all_to_all(x, "four", split_axis=0, concat_axis=0, tiled=True)


def body(adj_modes, base_flow, geometry, mass, connect, edge_nodes):
    comps, m_n, nodes_n, e_n = adj_modes.shape
    parts = lax.axis_size("four")
    l_n = nodes_n // parts
    mine = lax.axis_index("four") * l_n
    synth, along, analysis = plane_tables(PLANES)
    ids = connect.reshape(-1)
    edges = edge_nodes[0]

    u = adj_modes.reshape(comps, m_n, parts, l_n, e_n).transpose(2, 0, 3, 1, 4)
    u_here = exchange(u)
    spot = lambda n: (n // l_n, n % l_n)
    ur = derivative(u, [[spot(NP * i + j) for i in range(NP)] for j in range(NP)])
    if l_n % NP == 0:
        lines = [[(a, l + j) for j in range(NP)] for a in range(parts) for l in range(0, l_n, NP)]
        us_here = derivative(u_here, lines)
    else:
        us_here = exchange(derivative(u, [[spot(NP * i + j) for j in range(NP)] for i in range(NP)]))
    ur_here_a = exchange(ur[:, :2])
    ur_here_b = exchange(ur[:, 2:])

    base = base_flow.transpose(0, 2, 1, 3)
    geo = lax.dynamic_slice_in_dim(geometry, mine, l_n, 1)
    mass_here = lax.dynamic_slice_in_dim(mass, mine, l_n, 0)
    pairs, backs, edge_reps = pair_lists(ids, edges)
    inverse = inverse_mass(mass, ids, edges)

    vr, part = base_products(synth, along, u_here, us_here, base, geo)
    modes_a = exchange(forcing_modes(synth, analysis, ur_here_a, vr, part, mass_here, 0))
    modes_b = exchange(forcing_modes(synth, analysis, ur_here_b, vr, part, mass_here, 2))

    table_a, rims_a = local_sums(modes_a, u, mass, pairs, edge_reps, 0)
    out = spread(table_a, swap_edges(rims_a), edge_reps, *backs, inverse, None, adj_modes.shape, 0, 2)
    table_b, rims_b = local_sums(modes_b, u, mass, pairs, edge_reps, 2)
    return spread(table_b, swap_edges(rims_b), edge_reps, *backs, inverse, out, adj_modes.shape, 2, 1)


def solution(mesh):
    return jax.shard_map(
        body,
        mesh=mesh,
        in_specs=(
            P(None, "four", None, "mesh"),
            P(None, None, "four", "mesh"),
            P(None, None, "mesh"),
            P(None, "mesh"),
            P(None, "mesh"),
            P("mesh", None, None),
        ),
        out_specs=P(None, "four", None, "mesh"),
        check_vma=False,
    )
```

time: 2050 us -> 1040 us (0.51)
  waiting for transfers between devices: 1270 us -> 387 us
  Pallas kernels: 0 us -> 228 us
  local copies, waits for them, and re-layouts: 335 us -> 155 us
  matrix products: 155 us -> 0 us
  other arithmetic: 251 us -> 114 us
  blocking collectives: 0 us -> 95.1 us
    all_to_all x2 -> x4, waiting for transfers between devices: 1270 us -> 385 us  [exchange(): return lax.all_to_all(x, 'four', split_axis=0, concat_axis=0, tiled=True)]
    pallas_call x0 -> x9, Pallas kernels: none -> 228 us  [the longest x2 59.2 us: forcing_modes(): pl.pallas_call(kernel, grid=(c_n, l_n), in_specs=[whole, whole, coefs, pl...]
    dot_general x4 -> x0, matrix products: 155 us -> none  [the longest x1 99.8 us: body(): physical = jnp.einsum('jm,fmne->fjne', synth, spread, precision=HIGH)]
    all_to_all x0 -> x1, blocking collectives: none -> 95.1 us  [exchange(): return lax.all_to_all(x, 'four', split_axis=0, concat_axis=0, tiled=True)]
    unnamed x30 -> x16, local copies, waits for them, and re-layouts: 84.7 us -> 23.5 us
    concatenate x1 -> x0, local copies, waits for them, and re-layouts: 46.1 us -> none  [body(): packed = jnp.concatenate([adj_modes, grad_x, grad_y, grad_z])]
    all_to_all x1 -> x0, local copies, waits for them, and re-layouts: 45.9 us -> none  [body(): lax.all_to_all(packed, 'four', split_axis=2, concat_axis=1, tiled=True)]
    add x3 -> x0, other arithmetic: 38.5 us -> none  [advect(): total - base[direction].astype(jnp.float32) * physical[3 + 3 * direction...]
  transfers between devices with their start and end apart: 4 -> 10, of which waited for: 2 -> 4; matrix products, arithmetic and copies ran while one was open for 5% -> 24% of each run, Pallas kernels for 0% -> 17%
where the time goes in v1:
time: 1040 us; the launch traced here: 1030 us
  waiting for transfers between devices  387 us (37%)
  Pallas kernels  228 us (22%)
  local copies, waits for them, and re-layouts  155 us (15%)
  other arithmetic  114 us (11%)
  blocking collectives  95.1 us (9%)
  starting transfers between devices  44.1 us (4%)
    all_to_all x4, waiting for transfers between devices, exchange(): return lax.all_to_all(x, 'four', split_axis=0, concat_axis=0, tiled=True)  385 us
    all_to_all x1, blocking collectives, exchange(): return lax.all_to_all(x, 'four', split_axis=0, concat_axis=0, tiled=True)  95.1 us
    gather x1, local copies, waits for them, and re-layouts, inverse_mass(): return (1.0 / summed[ids]).reshape(mass.shape)  90.5 us
    scatter-add x1, other arithmetic, inverse_mass(): summed = jnp.zeros((UNIQUE,), jnp.float32).at[ids].add(mass.reshape(-1))  85.8 us
    pallas_call x2, Pallas kernels, forcing_modes(): pl.pallas_call(kernel, grid=(c_n, l_n), in_specs=[whole, whole, coefs, pl...  59.2 us
    pallas_call x2, Pallas kernels, local_sums(): pl.pallas_call(kernel, grid=(nodes_n // step,), in_specs=[smem] * 7 + [pl...  50.8 us
    pallas_call x2, Pallas kernels, derivative(): pl.pallas_call(kernel, grid=(c_n, m_n // rows), in_specs=[spec], out_spec...  39.7 us
    pallas_call x1, Pallas kernels, base_products(): pl.pallas_call(kernel, grid=(l_n,), in_specs=[whole, whole, coefs, coefs,...  39.5 us
  transfers between devices with their start and end apart: 10, of which 4 were waited for; matrix products, arithmetic and copies ran while one was open for 24% of the time, Pallas kernels for 17%

profile of v1, /device:TPU:9, one launch (start us, length us, event | category | flops | bytes accessed | tf_op | source)
XLA Modules:
  0.0 1025.8 jit_solution(16320822575402262746)
XLA Ops:
  0.0 18.0 %copy.29 = f32[3,64,4,16,256]{4,1,3,0,2:T(8,128)} copy(f32[3,64,4,16,256]{4,3,2,1,0:T(8,128)} %bitcast.74) | data formatting | bytes 25165824 | tf_op jit(solution)/shard_map/reshape | solution.py:418
  18.0 19.9 %line_derivative.2 = f32[4,3,16,64,256]{4,3,2,1,0:T(8,128)} custom-call(f32[4,3,16,64,256]{4,3,2,1,0:T(8,128)} %bitcast.69), custom_call_target="tpu_custom_call" | custom-call | flops 50331648 | bytes 25165824 | tf_op jit(solution)/shard_map/line_derivative/pallas_call | solution.py:95
  37.9 2.5 slice.75
  40.4 95.1 %all_to_all.25.ur_ref = f32[4,1,16,64,256]{4,3,2,1,0:T(8,128)} all-to-all(f32[4,1,16,64,256]{4,3,2,1,0:T(8,128)S(1)} %slice.75), channel_id=1, replica_groups=mesh['mesh'=8,'four'=4] {'four'}, dimensions={0} | all-to-all | bytes 8388608 | tf_op jit(solution)/shard_map/all_to_all | solution.py:406
  135.5 8.1 all-to-all-start.1
  143.6 7.7 slice.76
  151.3 260.4 %all-to-all-done.1.x_ref.u_ref = f32[4,3,16,64,256]{4,3,2,1,0:T(8,128)} async-done(((f32[4,3,16,64,256]{4,3,2,1,0:T(8,128)}), f32[4,3,16,64,256]{4,3,2,1,0:T(8,128)}, u32[]{:S(2)}, u32[]{:S(2)}) %all-to-all-start.1) | async-done | bytes 12582944 | tf_op jit(solution)/shard_map/all_to_all | solution.py:406
  411.7 10.2 all-to-all-start.3
  421.9 23.4 %copy.28 = bf16[12,256,16,256]{3,1,2,0:T(8,128)(2,1)} copy(bf16[12,256,16,256]{3,2,1,0:T(8,128)(2,1)} %param.12) | data formatting | bytes 50331648 | tf_op args[1]
  446.5 19.8 %line_derivative.3.us_ref = f32[4,3,16,64,256]{4,3,2,1,0:T(8,128)} custom-call(f32[4,3,16,64,256]{4,3,2,1,0:T(8,128)} %all-to-all-done.1.x_ref.u_ref), custom_call_target="tpu_custom_call" | custom-call | flops 50331648 | bytes 25165824 | tf_op jit(solution)/shard_map/line_derivative/pallas_call | solution.py:95
  466.4 39.5 %base_products.1 = (f32[16,256,256]{2,1,0:T(8,128)}, f32[3,16,256,256]{3,2,1,0:T(8,128)}) custom-call(f32[256,256]{1,0:T(8,128)} %constant.86.clone.synth_ref, f32[256,256]{1,0:T(8,128)} %constant.87.clone.along_ref, f32[4,3,16,64,256]{4,3,2,1,0:T(8,128)} %all-to-all-done.1.x_ref.u_ref, f32[4,3,16,64,256]{4,3,2,1,0:T(8,128)} %line_derivative.3.us_ref, ...), custom_call_target="tpu_custom_call" | custom-call | flops 28991029248 | bytes 67108864 | tf_op jit(solution)/shard_map/base_products/pallas_call | solution.py:134
  505.8 20.4 %forcing_modes.2 = f32[4,1,16,64,256]{4,3,2,1,0:T(8,128)} custom-call(f32[256,256]{1,0:T(8,128)} %constant.86.clone.synth_ref, f32[256,256]{1,0:T(8,128)} %constant.88.clone.analysis_ref, f32[4,1,16,64,256]{4,3,2,1,0:T(8,128)} %all_to_all.25.ur_ref, f32[16,256,256]{2,1,0:T(8,128)} %get-tuple-element.23.vr_ref, ...), custom_call_target="tpu_custom_call" | custom-call | flops 6442450944 | bytes 16777216 | tf_op jit(solution)/shard_map/forcing_modes/pallas_call | solution.py:175
  526.2 74.2 %all-to-all-done.3.ur_ref = f32[4,2,16,64,256]{4,3,2,1,0:T(8,128)} async-done(((f32[4,2,16,64,256]{4,3,2,1,0:T(8,128)}), f32[4,2,16,64,256]{4,3,2,1,0:T(8,128)}, u32[]{:S(2)}, u32[]{:S(2)}) %all-to-all-start.3) | async-done | bytes 8388640 | tf_op jit(solution)/shard_map/all_to_all | solution.py:406
  600.5 8.8 all-to-all-start.2
  609.3 38.8 %forcing_modes.3 = f32[4,2,16,64,256]{4,3,2,1,0:T(8,128)} custom-call(f32[256,256]{1,0:T(8,128)} %constant.86.clone.synth_ref, f32[256,256]{1,0:T(8,128)} %constant.88.clone.analysis_ref, f32[4,2,16,64,256]{4,3,2,1,0:T(8,128)} %all-to-all-done.3.ur_ref, f32[16,256,256]{2,1,0:T(8,128)} %get-tuple-element.23.vr_ref, ...), custom_call_target="tpu_custom_call" | custom-call | flops 12884901888 | bytes 33554432 | tf_op jit(solution)/shard_map/forcing_modes/pallas_call | solution.py:175
  648.1 49.9 %all-to-all-done.2.f_ref = f32[4,1,16,64,256]{4,3,2,1,0:T(8,128)} async-done(((f32[4,1,16,64,256]{4,3,2,1,0:T(8,128)}), f32[4,1,16,64,256]{4,3,2,1,0:T(8,128)}, u32[]{:S(2)}, u32[]{:S(2)}) %all-to-all-start.2) | async-done | bytes 4194336 | tf_op jit(solution)/shard_map/all_to_all | solution.py:406
  698.0 9.6 all-to-all-start.4
  707.9 85.8 %scatter_custom_fusion = f32[12825]{0:T(1024)S(1)} fusion(s32[16384]{0:T(1024)S(1)} %bitcast.78, f32[16384]{0:T(1024)S(1)} %bitcast.86, f32[]{:T(128)} %constant.84.clone.1), kind=kCustom, calls=%fused_computation.47 | custom fusion | flops 16384 | bytes 51304 | tf_op jit(solution)/shard_map/scatter-add | solution.py:399
  793.8 3.1 gather_fusion.1
  797.0 2.8 collective-permute-start.2
  800.1 7.1 sort.46
  809.7 8.7 sort.47
  820.4 4.0 convert_reduce_fusion
  826.8 3.1 gather_fusion
  830.8 3.3 scatter_fusion
  834.0 90.5 %gather_fusion.2 = f32[16384]{0:T(1024)S(1)} fusion(f32[12825]{0:T(1024)S(1)} %scatter_fusion, s32[16384]{0:T(1024)S(1)} %broadcast_clamp_fusion), kind=kCustom, calls=%fused_computation.2 | custom fusion | bytes 196608 | tf_op jit(solution)/shard_map/gather | solution.py:402
  924.6 24.8 %local_sums.2 = (f32[16392,128]{1,0:T(8,128)}, f32[2,232,128]{2,1,0:T(8,128)}) custom-call(s32[3560]{0:T(1024)} %pad.20.ck, s32[3560]{0:T(1024)} %pad.21.cr, s32[1]{0:T(128)} %bitcast.4.cn, s32[3559]{0:T(1024)} %fusion.10.fk, s32[3559]{0:T(1024)} %fusion.9.fr, s32[1]{0:T(128)} %bitcast.5.fn, s32[2,232]{1,0:T(2,128)} %pad.17.er, ...), custom_call_target="tpu_custom_call" | custom-call | flops 838860800 | bytes 25165824 | tf_op jit(solution)/shard_map/local_sums/pallas_call | solution.py:255
  952.1 26.0 %local_sums.3 = (f32[16392,128]{1,0:T(8,128)}, f32[2,232,128]{2,1,0:T(8,128)}) custom-call(s32[3560]{0:T(1024)} %pad.20.ck, s32[3560]{0:T(1024)} %pad.21.cr, s32[1]{0:T(128)} %bitcast.4.cn, s32[3559]{0:T(1024)} %fusion.10.fk, s32[3559]{0:T(1024)} %fusion.9.fr, s32[1]{0:T(128)} %bitcast.5.fn, s32[2,232]{1,0:T(2,128)} %pad.17.er, ...), custom_call_target="tpu_custom_call" | custom-call | flops 838860800 | bytes 25165824 | tf_op jit(solution)/shard_map/local_sums/pallas_call | solution.py:255
  979.1 1.8 collective-permute-start.4
  983.0 2.7 collective-permute-done.5
  986.5 20.4 %spread.2.rest_0_ = f32[3,64,64,256]{3,2,1,0:T(8,128)} custom-call(s32[2,232]{1,0:T(2,128)} %pad.17.er, s32[3560]{0:T(1024)} %get-tuple-element.42.bk, s32[3560]{0:T(1024)} %get-tuple-element.41.br, f32[16392,128]{1,0:T(8,128)} %get-tuple-element.27.t_ref, f32[2,232,128]{2,1,0:T(8,128)} %pad_maximum_fusion.1.came_ref, f32[64,256]{1,0:T(8,128)} %div.40.inv_ref), custom_call_target="tpu_custom_call" | custom-call | flops 838860800 | bytes 25165824 | tf_op jit(solution)/shard_map/spread/pallas_call | solution.py:340
  1006.9 18.5 %spread.3 = f32[3,64,64,256]{3,2,1,0:T(8,128)} custom-call(s32[2,232]{1,0:T(2,128)} %pad.17.er, s32[3560]{0:T(1024)} %get-tuple-element.42.bk, s32[3560]{0:T(1024)} %get-tuple-element.41.br, f32[16392,128]{1,0:T(8,128)} %get-tuple-element.25.t_ref, f32[2,232,128]{2,1,0:T(8,128)} %pad_maximum_fusion.came_ref, ...), custom_call_target="tpu_custom_call", output_to_operand_aliasing={{}: (6, {})} | custom-call | flops 838860800 | bytes 25165824 | tf_op jit(solution)/shard_map/spread/pallas_call | solution.py:340
  (67 shorter events, 14.8 us)
Async XLA Ops:
  0.0 445.9 %copy-start = (f32[4,64,256]{2,1,0:T(8,128)S(1)}, f32[4,64,256]{2,1,0:T(8,128)}, u32[]{:S(2)}) copy-start(f32[4,64,256]{2,1,0:T(8,128)} %param.13) | copy-start | bytes 786436
  135.5 276.3 %all-to-all-start.1 = ((f32[4,3,16,64,256]{4,3,2,1,0:T(8,128)}), f32[4,3,16,64,256]{4,3,2,1,0:T(8,128)}, u32[]{:S(2)}, u32[]{:S(2)}) async-start(f32[4,3,16,64,256]{4,3,2,1,0:T(8,128)} %bitcast.70), calls=%async_computation.1 | async-start | bytes 25165824 | tf_op jit(solution)/shard_map/all_to_all | solution.py:406
  411.7 188.7 %all-to-all-start.3 = ((f32[4,2,16,64,256]{4,3,2,1,0:T(8,128)}), f32[4,2,16,64,256]{4,3,2,1,0:T(8,128)}, u32[]{:S(2)}, u32[]{:S(2)}) async-start(f32[4,2,16,64,256]{4,3,2,1,0:T(8,128)} %slice.76), calls=%async_computation.3 | async-start | bytes 16777216 | tf_op jit(solution)/shard_map/all_to_all | solution.py:406
  421.9 23.4 %copy-start.2 = (f32[64,256]{1,0:T(8,128)S(1)}, f32[64,256]{1,0:T(8,128)}, u32[]{:S(2)}) copy-start(f32[64,256]{1,0:T(8,128)} %mass_ref.3) | copy-start | bytes 196612
  600.5 97.6 %all-to-all-start.2 = ((f32[4,1,16,64,256]{4,3,2,1,0:T(8,128)}), f32[4,1,16,64,256]{4,3,2,1,0:T(8,128)}, u32[]{:S(2)}, u32[]{:S(2)}) async-start(f32[4,1,16,64,256]{4,3,2,1,0:T(8,128)} %forcing_modes.2), calls=%async_computation.2 | async-start | bytes 8388608 | tf_op jit(solution)/shard_map/all_to_all | solution.py:406
  648.1 59.5 %copy-start.3 = (s32[64,256]{1,0:T(8,128)S(1)}, s32[64,256]{1,0:T(8,128)}, u32[]{:S(2)}) copy-start(s32[64,256]{1,0:T(8,128)} %param.15) | copy-start | bytes 196612
  648.1 59.6 %copy-start.4 = (s32[1,2,225]{2,1,0:T(2,128)S(1)}, s32[1,2,225]{2,1,0:T(2,128)}, u32[]{:S(2)}) copy-start(s32[1,2,225]{2,1,0:T(2,128)} %param.16) | copy-start | bytes 5404
  648.1 176.3 %copy-start.5 = (pred[3560]{0:T(1024)(128)(4,1)S(1)}, pred[3560]{0:T(1024)(128)(4,1)}, u32[]{:S(2)}) copy-start(pred[3560]{0:T(1024)(128)(4,1)} %constant.70.clone.1) | copy-start | bytes 10684
  698.0 254.1 %all-to-all-start.4 = ((f32[4,2,16,64,256]{4,3,2,1,0:T(8,128)}), f32[4,2,16,64,256]{4,3,2,1,0:T(8,128)}, u32[]{:S(2)}, u32[]{:S(2)}) async-start(f32[4,2,16,64,256]{4,3,2,1,0:T(8,128)} %forcing_modes.3), calls=%async_computation.4 | async-start | bytes 16777216 | tf_op jit(solution)/shard_map/all_to_all | solution.py:406
  797.0 33.7 %collective-permute-start.2 = (f32[225]{0:T(256)S(1)}, f32[225]{0:T(256)S(1)}, u32[]{:S(2)}, u32[]{:S(2)}) collective-permute-start(f32[225]{0:T(256)S(1)} %get-tuple-element.43), channel_id=1, source_target_pairs={{0,4},{4,8},{8,12},{12,16},{16,20},{20,24},{24,28},{28,0},{1,5},{5... | collective-permute-start | bytes 2708 | tf_op jit(solution)/shard_map/ppermute | solution.py:395
  799.8 30.8 %collective-permute-start.3 = (f32[225]{0:T(256)S(1)}, f32[225]{0:T(256)S(1)}, u32[]{:S(2)}, u32[]{:S(2)}) collective-permute-start(f32[225]{0:T(256)S(1)} %get-tuple-element.44), channel_id=1, source_target_pairs={{4,0},{8,4},{12,8},{16,12},{20,16},{24,20},{28,24},{0,28},{5,1},{9... | collective-permute-start | bytes 2708 | tf_op jit(solution)/shard_map/ppermute | solution.py:395
  950.3 32.0 %collective-permute-start = (f32[232,128]{1,0:T(8,128)S(1)}, f32[232,128]{1,0:T(8,128)S(1)}, u32[]{:S(2)}, u32[]{:S(2)}) collective-permute-start(f32[232,128]{1,0:T(8,128)S(1)} %get-tuple-element.33), channel_id=1, source_target_pairs={{0,4},{4,8},{8,12},{12,16},{16,20},{20,24},{24,28},{28,0},{1,5},{5... | collective-permute-start | bytes 356360 | tf_op jit(solution)/shard_map/ppermute | solution.py:395
  952.1 30.2 %collective-permute-start.1 = (f32[232,128]{1,0:T(8,128)S(1)}, f32[232,128]{1,0:T(8,128)S(1)}, u32[]{:S(2)}, u32[]{:S(2)}) collective-permute-start(f32[232,128]{1,0:T(8,128)S(1)} %get-tuple-element.34), channel_id=1, source_target_pairs={{4,0},{8,4},{12,8},{16,12},{20,16},{24,20},{28,24},{0,28},{5,1},{9... | collective-permute-start | bytes 356360 | tf_op jit(solution)/shard_map/ppermute | solution.py:395
  979.1 3.9 collective-permute-start.4
  980.9 4.9 collective-permute-start.5
  1006.9 18.5 %copy-start.1 = (f32[4,64,256]{2,1,0:T(8,128)S(1)}, f32[4,64,256]{2,1,0:T(8,128)}, u32[]{:S(2)}) copy-start(f32[4,64,256]{2,1,0:T(8,128)} %param.13) | copy-start | bytes 786436

commit v2 on v1

--- a/solution.py
+++ b/solution.py
@@ -76,8 +76,30 @@
     return pltpu.CompilerParams(vmem_limit_bytes=VMEM_LIMIT, **kw)
 
 
-def derivative(x, groups):
-    a_n, c_n, l_n, m_n, e_n = x.shape
+def node_major(x, parts):
+    c_n, m_n, n_n, e_n = x.shape
+    l_n = n_n // parts
+    rows = 16
+    wide = min(LANES, e_n)
+
+    def kernel(x_ref, o_ref):
+        for n in range(n_n):
+            o_ref[n // l_n, 0, n % l_n] = x_ref[0, pl.ds(n, rows, stride=n_n), :]
+
+    return pl.pallas_call(
+        kernel,
+        grid=(c_n, m_n // rows, e_n // wide),
+        in_specs=[pl.BlockSpec((1, rows * n_n, wide), lambda c, m, e: (c, m, e))],
+        out_specs=pl.BlockSpec((parts, 1, l_n, rows, wide), lambda c, m, e: (0, c, 0, m, e)),
+        out_shape=jax.ShapeDtypeStruct((parts, c_n, l_n, m_n, e_n), jnp.float32),
+        compiler_params=params(),
+        cost_estimate=pl.CostEstimate(flops=x.size, bytes_accessed=8 * x.size, transcendentals=0),
+        name="node_major",
+    )(x.reshape(c_n, m_n * n_n, e_n))
+
+
+def derivative(x, groups, first=0, c_n=3):
+    a_n, _, l_n, m_n, e_n = x.shape
     deriv = gll_derivative(NP)
     rows = 8
 
@@ -91,15 +113,16 @@
                         total = total + deriv[i][k] * vals[k]
                 o_ref[a, 0, l] = total
 
-    spec = pl.BlockSpec((a_n, 1, l_n, rows, e_n), lambda c, m: (0, c, 0, m, 0))
+    block = (a_n, 1, l_n, rows, e_n)
+    size = a_n * c_n * l_n * m_n * e_n
     return pl.pallas_call(
         kernel,
         grid=(c_n, m_n // rows),
-        in_specs=[spec],
-        out_specs=spec,
-        out_shape=jax.ShapeDtypeStruct(x.shape, jnp.float32),
-        compiler_params=params(),
-        cost_estimate=pl.CostEstimate(flops=16 * x.size, bytes_accessed=8 * x.size, transcendentals=0),
+        in_specs=[pl.BlockSpec(block, lambda c, m: (0, first + c, 0, m, 0))],
+        out_specs=pl.BlockSpec(block, lambda c, m: (0, c, 0, m, 0)),
+        out_shape=jax.ShapeDtypeStruct((a_n, c_n, l_n, m_n, e_n), jnp.float32),
+        compiler_params=params(),
+        cost_estimate=pl.CostEstimate(flops=16 * size, bytes_accessed=8 * size, transcendentals=0),
         name="line_derivative",
     )(x)
 
@@ -412,33 +435,47 @@
     l_n = nodes_n // parts
     mine = lax.axis_index("four") * l_n
     synth, along, analysis = plane_tables(PLANES)
+    together = lax.optimization_barrier
+    u = node_major(adj_modes, parts)
+    u, connect, edge_nodes, mass, base_flow = together((u, connect, edge_nodes, mass, base_flow))
+    u_here = exchange(u)
+
     ids = connect.reshape(-1)
     edges = edge_nodes[0]
-
-    u = adj_modes.reshape(comps, m_n, parts, l_n, e_n).transpose(2, 0, 3, 1, 4)
-    u_here = exchange(u)
     spot = lambda n: (n // l_n, n % l_n)
-    ur = derivative(u, [[spot(NP * i + j) for i in range(NP)] for j in range(NP)])
+    along_r = [[spot(NP * i + j) for i in range(NP)] for j in range(NP)]
+    ur_a, ur_b = derivative(u, along_r, 0, 2), derivative(u, along_r, 2, 1)
+    pairs, backs, edge_reps = pair_lists(ids, edges)
+    inverse = inverse_mass(mass, ids, edges)
+    base = base_flow.transpose(0, 2, 1, 3)
+    ur_a, ur_b, u_here, pairs, backs, edge_reps, inverse, base = together(
+        (ur_a, ur_b, u_here, pairs, backs, edge_reps, inverse, base)
+    )
+
+    ur_here_a = exchange(ur_a)
     if l_n % NP == 0:
         lines = [[(a, l + j) for j in range(NP)] for a in range(parts) for l in range(0, l_n, NP)]
         us_here = derivative(u_here, lines)
     else:
         us_here = exchange(derivative(u, [[spot(NP * i + j) for j in range(NP)] for i in range(NP)]))
-    ur_here_a = exchange(ur[:, :2])
-    ur_here_b = exchange(ur[:, 2:])
-
-    base = base_flow.transpose(0, 2, 1, 3)
     geo = lax.dynamic_slice_in_dim(geometry, mine, l_n, 1)
     mass_here = lax.dynamic_slice_in_dim(mass, mine, l_n, 0)
-    pairs, backs, edge_reps = pair_lists(ids, edges)
-    inverse = inverse_mass(mass, ids, edges)
-
     vr, part = base_products(synth, along, u_here, us_here, base, geo)
-    modes_a = exchange(forcing_modes(synth, analysis, ur_here_a, vr, part, mass_here, 0))
-    modes_b = exchange(forcing_modes(synth, analysis, ur_here_b, vr, part, mass_here, 2))
-
+    ur_b, ur_here_a, vr, part = together((ur_b, ur_here_a, vr, part))
+
+    ur_here_b = exchange(ur_b)
+    f_a = forcing_modes(synth, analysis, ur_here_a, vr, part, mass_here, 0)
+    f_a, ur_here_b = together((f_a, ur_here_b))
+
+    modes_a = exchange(f_a)
+    f_b = forcing_modes(synth, analysis, ur_here_b, vr, part, mass_here, 2)
+    f_b, modes_a = together((f_b, modes_a))
+
+    modes_b = exchange(f_b)
     table_a, rims_a = local_sums(modes_a, u, mass, pairs, edge_reps, 0)
     out = spread(table_a, swap_edges(rims_a), edge_reps, *backs, inverse, None, adj_modes.shape, 0, 2)
+    modes_b, out = together((modes_b, out))
+
     table_b, rims_b = local_sums(modes_b, u, mass, pairs, edge_reps, 2)
     return spread(table_b, swap_edges(rims_b), edge_reps, *backs, inverse, out, adj_modes.shape, 2, 1)
 

time: 1040 us -> 928 us (0.89)
  blocking collectives: 95.1 us -> 0 us
  local copies, waits for them, and re-layouts: 155 us -> 127 us
  Pallas kernels: 228 us -> 250 us
    all_to_all x1 -> x0, blocking collectives: 95.1 us -> none  [exchange(): return lax.all_to_all(x, 'four', split_axis=0, concat_axis=0, tiled=True)]
    unnamed x16 -> x15, local copies, waits for them, and re-layouts: 23.5 us -> 0.16 us
    optimization_barrier x0 -> x1, local copies, waits for them, and re-layouts: none -> 23.3 us  [body(): together((u, connect, edge_nodes, mass, base_flow))]
    pallas_call x2 -> x4, Pallas kernels: 39.7 us -> 61.4 us  [the longest x3 41 us: derivative(): pl.pallas_call(kernel, grid=(c_n, m_n // rows), in_specs=[pl.BlockSpec(bl...]
    reshape x2 -> x1, local copies, waits for them, and re-layouts: 18.1 us -> 0.09 us  [the longest x1 18 us: body(): u = adj_modes.reshape(comps, m_n, parts, l_n, e_n).transpose(2, 0, 3, 1, 4)]
    all_to_all x4 -> x5, waiting for transfers between devices: 385 us -> 368 us  [exchange(): return lax.all_to_all(x, 'four', split_axis=0, concat_axis=0, tiled=True)]
    all_to_all x4 -> x5, starting transfers between devices: 36.7 us -> 42.5 us  [exchange(): return lax.all_to_all(x, 'four', split_axis=0, concat_axis=0, tiled=True)]
  transfers between devices with their start and end apart: 10 -> 11, of which waited for: 4 -> 9; matrix products, arithmetic and copies ran while one was open for 24% -> 26% of each run, Pallas kernels for 17% -> 20%
where the time goes in v2:
time: 928 us; the launch traced here: 920 us
  waiting for transfers between devices  377 us (41%)
  Pallas kernels  250 us (27%)
  local copies, waits for them, and re-layouts  127 us (14%)
  other arithmetic  114 us (12%)
  starting transfers between devices  50.7 us (5%)
    all_to_all x5, waiting for transfers between devices, exchange(): return lax.all_to_all(x, 'four', split_axis=0, concat_axis=0, tiled=True)  368 us
    gather x1, local copies, waits for them, and re-layouts, inverse_mass(): return (1.0 / summed[ids]).reshape(mass.shape)  90.5 us
    scatter-add x1, other arithmetic, inverse_mass(): summed = jnp.zeros((UNIQUE,), jnp.float32).at[ids].add(mass.reshape(-1))  85.8 us
    pallas_call x2, Pallas kernels, forcing_modes(): pl.pallas_call(kernel, grid=(c_n, l_n), in_specs=[whole, whole, coefs, pl...  59.2 us
    pallas_call x2, Pallas kernels, local_sums(): pl.pallas_call(kernel, grid=(nodes_n // step,), in_specs=[smem] * 7 + [pl...  50.9 us
    all_to_all x5, starting transfers between devices, exchange(): return lax.all_to_all(x, 'four', split_axis=0, concat_axis=0, tiled=True)  42.5 us
    pallas_call x3, Pallas kernels, derivative(): pl.pallas_call(kernel, grid=(c_n, m_n // rows), in_specs=[pl.BlockSpec(bl...  41 us
    pallas_call x1, Pallas kernels, base_products(): pl.pallas_call(kernel, grid=(l_n,), in_specs=[whole, whole, coefs, coefs,...  39.4 us
  transfers between devices with their start and end apart: 11, of which 9 were waited for; matrix products, arithmetic and copies ran while one was open for 26% of the time, Pallas kernels for 20%

profile of v2, /device:TPU:9, one launch (start us, length us, event | category | flops | bytes accessed | tf_op | source)
XLA Modules:
  0.0 920.3 jit_solution(721774833598227289)
XLA Ops:
  0.0 20.4 %node_major.1.x_ref.u_ref = f32[4,3,16,64,256]{4,3,2,1,0:T(8,128)} custom-call(f32[3,4096,256]{2,1,0:T(8,128)} %bitcast.67), custom_call_target="tpu_custom_call" | custom-call | flops 3145728 | bytes 25165824 | tf_op jit(solution)/shard_map/node_major/pallas_call | solution.py:89
  20.4 6.5 all-to-all-start
  27.2 85.8 %scatter_custom_fusion = f32[12825]{0:T(1024)S(1)} fusion(s32[16384]{0:T(1024)S(1)} %bitcast.71, f32[16384]{0:T(1024)S(1)} %bitcast.79, f32[]{:T(128)} %constant.81.clone.1), kind=kCustom, calls=%fused_computation.46 | custom fusion | flops 16384 | bytes 51304 | tf_op jit(solution)/shard_map/scatter-add | solution.py:422
  113.0 3.1 gather_fusion.1
  118.4 7.1 sort.46
  128.0 8.7 sort.47
  136.7 13.7 %line_derivative.3 = f32[4,2,16,64,256]{4,3,2,1,0:T(8,128)} custom-call(f32[4,3,16,64,256]{4,3,2,1,0:T(8,128)} %node_major.1.x_ref.u_ref), custom_call_target="tpu_custom_call" | custom-call | flops 33554432 | bytes 16777216 | tf_op jit(solution)/shard_map/line_derivative/pallas_call | solution.py:118
  150.4 4.0 convert_reduce_fusion
  157.1 7.5 line_derivative.4
  166.3 3.1 gather_fusion
  170.2 23.3 %copy.25 = bf16[12,256,16,256]{3,1,2,0:T(8,128)(2,1)} copy(bf16[12,256,16,256]{3,2,1,0:T(8,128)(2,1)} %param.12) | data formatting | bytes 50331648 | tf_op jit(solution)/shard_map/optimization_barrier | solution.py:440
  193.6 3.3 scatter_fusion
  196.9 90.5 %gather_fusion.2 = f32[16384]{0:T(1024)S(1)} fusion(f32[12825]{0:T(1024)S(1)} %scatter_fusion, s32[16384]{0:T(1024)S(1)} %broadcast_clamp_fusion), kind=kCustom, calls=%fused_computation.2 | custom fusion | bytes 196608 | tf_op jit(solution)/shard_map/gather | solution.py:425
  288.1 8.4 all-to-all-done.x_ref.u_ref
  296.5 8.9 all-to-all-start.1
  306.0 19.7 %line_derivative.5.us_ref = f32[4,3,16,64,256]{4,3,2,1,0:T(8,128)} custom-call(f32[4,3,16,64,256]{4,3,2,1,0:T(8,128)} %all-to-all-done.x_ref.u_ref), custom_call_target="tpu_custom_call" | custom-call | flops 50331648 | bytes 25165824 | tf_op jit(solution)/shard_map/line_derivative/pallas_call | solution.py:118
  325.7 39.4 %base_products.1 = (f32[16,256,256]{2,1,0:T(8,128)}, f32[3,16,256,256]{3,2,1,0:T(8,128)}) custom-call(f32[256,256]{1,0:T(8,128)} %constant.86.clone.synth_ref, f32[256,256]{1,0:T(8,128)} %constant.87.clone.along_ref, f32[4,3,16,64,256]{4,3,2,1,0:T(8,128)} %all-to-all-done.x_ref.u_ref, f32[4,3,16,64,256]{4,3,2,1,0:T(8,128)} %line_derivative.5.us_ref, ...), custom_call_target="tpu_custom_call" | custom-call | flops 28991029248 | bytes 67108864 | tf_op jit(solution)/shard_map/base_products/pallas_call | solution.py:157
  365.2 119.0 %all-to-all-done.1.ur_ref = f32[4,2,16,64,256]{4,3,2,1,0:T(8,128)} async-done(((f32[4,2,16,64,256]{4,3,2,1,0:T(8,128)}), f32[4,2,16,64,256]{4,3,2,1,0:T(8,128)}, u32[]{:S(2)}, u32[]{:S(2)}) %all-to-all-start.1) | async-done | bytes 8388640 | tf_op jit(solution)/shard_map/all_to_all | solution.py:429
  484.2 8.6 all-to-all-start.2
  493.4 38.8 %forcing_modes.2 = f32[4,2,16,64,256]{4,3,2,1,0:T(8,128)} custom-call(f32[256,256]{1,0:T(8,128)} %constant.86.clone.synth_ref, f32[256,256]{1,0:T(8,128)} %constant.88.clone.analysis_ref, f32[4,2,16,64,256]{4,3,2,1,0:T(8,128)} %all-to-all-done.1.ur_ref, f32[16,256,256]{2,1,0:T(8,128)} %get-tuple-element.73.vr_ref, ...), custom_call_target="tpu_custom_call" | custom-call | flops 12884901888 | bytes 33554432 | tf_op jit(solution)/shard_map/forcing_modes/pallas_call | solution.py:198
  532.2 49.3 %all-to-all-done.2.ur_ref = f32[4,1,16,64,256]{4,3,2,1,0:T(8,128)} async-done(((f32[4,1,16,64,256]{4,3,2,1,0:T(8,128)}), f32[4,1,16,64,256]{4,3,2,1,0:T(8,128)}, u32[]{:S(2)}, u32[]{:S(2)}) %all-to-all-start.2) | async-done | bytes 4194336 | tf_op jit(solution)/shard_map/all_to_all | solution.py:429
  581.5 9.6 %all-to-all-start.3 = ((f32[4,2,16,64,256]{4,3,2,1,0:T(8,128)}), f32[4,2,16,64,256]{4,3,2,1,0:T(8,128)}, u32[]{:S(2)}, u32[]{:S(2)}) async-start(f32[4,2,16,64,256]{4,3,2,1,0:T(8,128)} %forcing_modes.2), calls=%async_computation.3 | async-start | bytes 16777216 | tf_op jit(solution)/shard_map/all_to_all | solution.py:429
  591.1 20.4 %forcing_modes.3 = f32[4,1,16,64,256]{4,3,2,1,0:T(8,128)} custom-call(f32[256,256]{1,0:T(8,128)} %constant.86.clone.synth_ref, f32[256,256]{1,0:T(8,128)} %constant.88.clone.analysis_ref, f32[4,1,16,64,256]{4,3,2,1,0:T(8,128)} %all-to-all-done.2.ur_ref, f32[16,256,256]{2,1,0:T(8,128)} %get-tuple-element.73.vr_ref, ...), custom_call_target="tpu_custom_call" | custom-call | flops 6442450944 | bytes 16777216 | tf_op jit(solution)/shard_map/forcing_modes/pallas_call | solution.py:198
  611.5 158.2 %all-to-all-done.3.f_ref = f32[4,2,16,64,256]{4,3,2,1,0:T(8,128)} async-done(((f32[4,2,16,64,256]{4,3,2,1,0:T(8,128)}), f32[4,2,16,64,256]{4,3,2,1,0:T(8,128)}, u32[]{:S(2)}, u32[]{:S(2)}) %all-to-all-start.3) | async-done | bytes 8388640 | tf_op jit(solution)/shard_map/all_to_all | solution.py:429
  769.7 8.9 all-to-all-start.4
  778.6 26.2 %local_sums.2 = (f32[16392,128]{1,0:T(8,128)}, f32[2,232,128]{2,1,0:T(8,128)}) custom-call(s32[3560]{0:T(1024)} %pad.17.ck, s32[3560]{0:T(1024)} %pad.18.cr, s32[1]{0:T(128)} %bitcast.3.cn, s32[3559]{0:T(1024)} %fusion.10.fk, s32[3559]{0:T(1024)} %fusion.9.fr, s32[1]{0:T(128)} %bitcast.4.fn, s32[2,232]{1,0:T(2,128)} %pad.21.er, ...), custom_call_target="tpu_custom_call" | custom-call | flops 838860800 | bytes 25165824 | tf_op jit(solution)/shard_map/local_sums/pallas_call | solution.py:278
  810.3 3.3 collective-permute-done.3
  814.3 20.4 %spread.2.rest_0_ = f32[3,64,64,256]{3,2,1,0:T(8,128)} custom-call(s32[2,232]{1,0:T(2,128)} %pad.21.er, s32[3560]{0:T(1024)} %get-tuple-element.58.bk, s32[3560]{0:T(1024)} %get-tuple-element.59.br, f32[16392,128]{1,0:T(8,128)} %get-tuple-element.80.t_ref, f32[2,232,128]{2,1,0:T(8,128)} %pad_maximum_fusion.came_ref, f32[64,256]{1,0:T(8,128)} %div.40.inv_ref), custom_call_target="tpu_custom_call" | custom-call | flops 838860800 | bytes 25165824 | tf_op jit(solution)/shard_map/spread/pallas_call | solution.py:363
  834.7 32.6 %all-to-all-done.4.f_ref = f32[4,1,16,64,256]{4,3,2,1,0:T(8,128)} async-done(((f32[4,1,16,64,256]{4,3,2,1,0:T(8,128)}), f32[4,1,16,64,256]{4,3,2,1,0:T(8,128)}, u32[]{:S(2)}, u32[]{:S(2)}) %all-to-all-start.4) | async-done | bytes 4194336 | tf_op jit(solution)/shard_map/all_to_all | solution.py:429
  867.3 24.7 %local_sums.3 = (f32[16392,128]{1,0:T(8,128)}, f32[2,232,128]{2,1,0:T(8,128)}) custom-call(s32[3560]{0:T(1024)} %pad.17.ck, s32[3560]{0:T(1024)} %pad.18.cr, s32[1]{0:T(128)} %bitcast.3.cn, s32[3559]{0:T(1024)} %fusion.10.fk, s32[3559]{0:T(1024)} %fusion.9.fr, s32[1]{0:T(128)} %bitcast.4.fn, s32[2,232]{1,0:T(2,128)} %pad.21.er, ...), custom_call_target="tpu_custom_call" | custom-call | flops 838860800 | bytes 25165824 | tf_op jit(solution)/shard_map/local_sums/pallas_call | solution.py:278
  893.0 3.4 collective-permute-start.4
  901.8 18.4 %spread.3 = f32[3,64,64,256]{3,2,1,0:T(8,128)} custom-call(s32[2,232]{1,0:T(2,128)} %pad.21.er, s32[3560]{0:T(1024)} %get-tuple-element.58.bk, s32[3560]{0:T(1024)} %get-tuple-element.59.br, f32[16392,128]{1,0:T(8,128)} %get-tuple-element.84.t_ref, f32[2,232,128]{2,1,0:T(8,128)} %pad_maximum_fusion.1.came_ref, ...), custom_call_target="tpu_custom_call", output_to_operand_aliasing={{}: (6, {})} | custom-call | flops 838860800 | bytes 25165824 | tf_op jit(solution)/shard_map/spread/pallas_call | solution.py:363
  (67 shorter events, 23.5 us)
Async XLA Ops:
  0.0 305.4 %copy-start = (f32[4,64,256]{2,1,0:T(8,128)S(1)}, f32[4,64,256]{2,1,0:T(8,128)}, u32[]{:S(2)}) copy-start(f32[4,64,256]{2,1,0:T(8,128)} %param.13) | copy-start | bytes 786436
  20.4 6.5 copy-start.2
  20.4 6.5 copy-start.3
  20.4 6.6 copy-start.4
  20.4 276.1 %all-to-all-start = ((f32[4,3,16,64,256]{4,3,2,1,0:T(8,128)}), f32[4,3,16,64,256]{4,3,2,1,0:T(8,128)}, u32[]{:S(2)}, u32[]{:S(2)}) async-start(f32[4,3,16,64,256]{4,3,2,1,0:T(8,128)} %node_major.1.x_ref.u_ref), calls=%async_computation | async-start | bytes 25165824 | tf_op jit(solution)/shard_map/all_to_all | solution.py:429
  113.0 43.4 %copy-start.5 = (pred[3560]{0:T(1024)(128)(4,1)S(1)}, pred[3560]{0:T(1024)(128)(4,1)}, u32[]{:S(2)}) copy-start(pred[3560]{0:T(1024)(128)(4,1)} %constant.79.clone.1) | copy-start | bytes 10684
  116.3 77.2 %collective-permute-start = (f32[225]{0:T(256)S(1)}, f32[225]{0:T(256)S(1)}, u32[]{:S(2)}, u32[]{:S(2)}) collective-permute-start(f32[225]{0:T(256)S(1)} %get-tuple-element.101), channel_id=1, source_target_pairs={{0,4},{4,8},{8,12},{12,16},{16,20},{20,24},{24,28},{28,0},{1,5},{5... | collective-permute-start | bytes 2708 | tf_op jit(solution)/shard_map/ppermute | solution.py:418
  118.4 75.1 %collective-permute-start.1 = (f32[225]{0:T(256)S(1)}, f32[225]{0:T(256)S(1)}, u32[]{:S(2)}, u32[]{:S(2)}) collective-permute-start(f32[225]{0:T(256)S(1)} %get-tuple-element.102), channel_id=1, source_target_pairs={{4,0},{8,4},{12,8},{16,12},{20,16},{24,20},{28,24},{0,28},{5,1},{9... | collective-permute-start | bytes 2708 | tf_op jit(solution)/shard_map/ppermute | solution.py:418
  296.5 187.7 %all-to-all-start.1 = ((f32[4,2,16,64,256]{4,3,2,1,0:T(8,128)}), f32[4,2,16,64,256]{4,3,2,1,0:T(8,128)}, u32[]{:S(2)}, u32[]{:S(2)}) async-start(f32[4,2,16,64,256]{4,3,2,1,0:T(8,128)} %line_derivative.3), calls=%async_computation.1 | async-start | bytes 16777216 | tf_op jit(solution)/shard_map/all_to_all | solution.py:429
  484.2 97.3 %all-to-all-start.2 = ((f32[4,1,16,64,256]{4,3,2,1,0:T(8,128)}), f32[4,1,16,64,256]{4,3,2,1,0:T(8,128)}, u32[]{:S(2)}, u32[]{:S(2)}) async-start(f32[4,1,16,64,256]{4,3,2,1,0:T(8,128)} %line_derivative.4), calls=%async_computation.2 | async-start | bytes 8388608 | tf_op jit(solution)/shard_map/all_to_all | solution.py:429
  581.5 188.2 %all-to-all-start.3 = ((f32[4,2,16,64,256]{4,3,2,1,0:T(8,128)}), f32[4,2,16,64,256]{4,3,2,1,0:T(8,128)}, u32[]{:S(2)}, u32[]{:S(2)}) async-start(f32[4,2,16,64,256]{4,3,2,1,0:T(8,128)} %forcing_modes.2), calls=%async_computation.3 | async-start | bytes 16777216 | tf_op jit(solution)/shard_map/all_to_all | solution.py:429
  769.7 97.6 %all-to-all-start.4 = ((f32[4,1,16,64,256]{4,3,2,1,0:T(8,128)}), f32[4,1,16,64,256]{4,3,2,1,0:T(8,128)}, u32[]{:S(2)}, u32[]{:S(2)}) async-start(f32[4,1,16,64,256]{4,3,2,1,0:T(8,128)} %forcing_modes.3), calls=%async_computation.4 | async-start | bytes 8388608 | tf_op jit(solution)/shard_map/all_to_all | solution.py:429
  805.8 4.6 collective-permute-start.2
  808.5 5.1 collective-permute-start.3
  893.0 5.2 collective-permute-start.4
  896.4 4.7 collective-permute-start.5
  901.8 18.4 %copy-start.1 = (f32[4,64,256]{2,1,0:T(8,128)S(1)}, f32[4,64,256]{2,1,0:T(8,128)}, u32[]{:S(2)}) copy-start(f32[4,64,256]{2,1,0:T(8,128)} %param.13) | copy-start | bytes 786436

commit v3 on v2

--- a/solution.py
+++ b/solution.py
@@ -426,7 +426,15 @@
 
 
 def exchange(x):
-    return lax.all_to_all(x, "four", split_axis=0, concat_axis=0, tiled=True)
+    count = lax.axis_size("four")
+    me = lax.axis_index("four")
+    came = []
+    for step in range(1, count):
+        piece = lax.dynamic_index_in_dim(x, (me + step) % count, 0, keepdims=False)
+        came.append(lax.ppermute(piece, "four", [(i, (i + step) % count) for i in range(count)]))
+    for step, piece in enumerate(came, 1):
+        x = lax.dynamic_update_index_in_dim(x, piece, (me - step) % count, 0)
+    return x
 
 
 def body(adj_modes, base_flow, geometry, mass, connect, edge_nodes):

time: 928 us -> 1060 us (1.14)
  local copies, waits for them, and re-layouts: 127 us -> 271 us
  starting transfers between devices: 50.7 us -> 23.3 us
  other arithmetic: 114 us -> 127 us
    all_to_all x5 -> x0, waiting for transfers between devices: 368 us -> none  [exchange(): return lax.all_to_all(x, 'four', split_axis=0, concat_axis=0, tiled=True)]
    ppermute x0 -> x15, waiting for transfers between devices: none -> 365 us  [exchange(): lax.ppermute(piece, 'four', [(i, (i + step) % count) for i in range(count)])]
    gather x1, local copies, waits for them, and re-layouts: 90.5 us -> 160 us  [inverse_mass(): return (1.0 / summed[ids]).reshape(mass.shape)]
    all_to_all x5 -> x0, starting transfers between devices: 42.5 us -> none  [exchange(): return lax.all_to_all(x, 'four', split_axis=0, concat_axis=0, tiled=True)]
    squeeze x0 -> x10, local copies, waits for them, and re-layouts: none -> 25.6 us  [exchange(): piece = lax.dynamic_index_in_dim(x, (me + step) % count, 0, keepdims=False)]
    unnamed x15 -> x46, local copies, waits for them, and re-layouts: 0.16 us -> 21.1 us
    dynamic_update_slice x0 -> x10, local copies, waits for them, and re-layouts: none -> 19.1 us  [exchange(): x = lax.dynamic_update_index_in_dim(x, piece, (me - step) % count, 0)]
    ppermute x0 -> x15, starting transfers between devices: none -> 15.1 us  [exchange(): lax.ppermute(piece, 'four', [(i, (i + step) % count) for i in range(count)])]
  transfers between devices with their start and end apart: 11 -> 21, of which waited for: 9 -> 14; matrix products, arithmetic and copies ran while one was open for 26% -> 34% of each run, Pallas kernels for 20% -> 18%
where the time goes in v3:
time: 1060 us; the launch traced here: 1050 us
  waiting for transfers between devices  374 us (35%)
  local copies, waits for them, and re-layouts  271 us (26%)
  Pallas kernels  251 us (24%)
  other arithmetic  127 us (12%)
  starting transfers between devices  23.3 us (2%)
    ppermute x15, waiting for transfers between devices, exchange(): lax.ppermute(piece, 'four', [(i, (i + step) % count) for i in range(count)])  365 us
    gather x1, local copies, waits for them, and re-layouts, inverse_mass(): return (1.0 / summed[ids]).reshape(mass.shape)  160 us
    scatter-add x1, other arithmetic, inverse_mass(): summed = jnp.zeros((UNIQUE,), jnp.float32).at[ids].add(mass.reshape(-1))  85.9 us
    pallas_call x2, Pallas kernels, forcing_modes(): pl.pallas_call(kernel, grid=(c_n, l_n), in_specs=[whole, whole, coefs, pl...  59.2 us
    pallas_call x2, Pallas kernels, local_sums(): pl.pallas_call(kernel, grid=(nodes_n // step,), in_specs=[smem] * 7 + [pl...  50.9 us
    pallas_call x3, Pallas kernels, derivative(): pl.pallas_call(kernel, grid=(c_n, m_n // rows), in_specs=[pl.BlockSpec(bl...  41.5 us
    pallas_call x1, Pallas kernels, base_products(): pl.pallas_call(kernel, grid=(l_n,), in_specs=[whole, whole, coefs, coefs,...  39.7 us
    pallas_call x2, Pallas kernels, spread(): pl.pallas_call(kernel, grid=(nodes_n // step,), in_specs=in_specs, out_sp...  38.8 us
  transfers between devices with their start and end apart: 21, of which 14 were waited for; matrix products, arithmetic and copies ran while one was open for 34% of the time, Pallas kernels for 18%

profile of v3, /device:TPU:9, one launch (start us, length us, event | category | flops | bytes accessed | tf_op | source)
XLA Modules:
  0.0 1047.0 jit_solution(18357558765926597245)
XLA Ops:
  0.0 20.4 %node_major.1.x_ref.u_ref = f32[4,3,16,64,256]{4,3,2,1,0:T(8,128)} custom-call(f32[3,4096,256]{2,1,0:T(8,128)} %bitcast.127), custom_call_target="tpu_custom_call" | custom-call | flops 3145728 | bytes 25165824 | tf_op jit(solution)/shard_map/node_major/pallas_call | solution.py:89
  25.4 85.9 %scatter_custom_fusion = f32[12825]{0:T(1024)S(1)} fusion(s32[16384]{0:T(1024)} %bitcast.131, f32[16384]{0:T(1024)} %bitcast.139, f32[]{:T(128)} %constant.240.clone.1), kind=kCustom, calls=%fused_computation.76 | custom fusion | flops 16384 | bytes 51812 | tf_op jit(solution)/shard_map/scatter-add | solution.py:422
  117.2 11.6 %copy.26 = f32[4,3,16,64,256]{4,3,2,1,0:T(8,128)} copy(f32[4,3,16,64,256]{4,3,2,1,0:T(8,128)} %node_major.1.x_ref.u_ref) | data formatting | bytes 25165824
  130.1 8.6 sort.46
  151.4 7.9 dynamic-slice_bitcast_fusion
  164.1 9.4 sort.47
  173.5 7.7 line_derivative.4
  181.3 13.8 %line_derivative.3 = f32[4,2,16,64,256]{4,3,2,1,0:T(8,128)} custom-call(f32[4,3,16,64,256]{4,3,2,1,0:T(8,128)} %node_major.1.x_ref.u_ref), custom_call_target="tpu_custom_call" | custom-call | flops 33554432 | bytes 16777216 | tf_op jit(solution)/shard_map/line_derivative/pallas_call | solution.py:118
  195.1 3.8 convert_reduce_fusion
  209.2 23.3 %copy.25 = bf16[12,256,16,256]{3,1,2,0:T(8,128)(2,1)} copy(bf16[12,256,16,256]{3,2,1,0:T(8,128)(2,1)} %param.12) | data formatting | bytes 50331648 | tf_op jit(solution)/shard_map/optimization_barrier | solution.py:448
  236.6 160.3 %gather_fusion.2 = f32[16384]{0:T(1024)} fusion(f32[12825]{0:T(1024)S(1)} %scatter_fusion, s32[16384]{0:T(1024)S(1)} %copy-done.16), kind=kCustom, calls=%fused_computation.2 | custom fusion | bytes 196608 | tf_op jit(solution)/shard_map/gather | solution.py:425
  398.5 3.9 bitcast_dynamic-update-slice_fusion.1
  406.7 19.9 %line_derivative.5.us_ref = f32[4,3,16,64,256]{4,3,2,1,0:T(8,128)} custom-call(f32[4,3,16,64,256]{4,3,2,1,0:T(8,128)} %bitcast_dynamic-update-slice_fusion.x_ref.u_ref), custom_call_target="tpu_custom_call" | custom-call | flops 50331648 | bytes 25165824 | tf_op jit(solution)/shard_map/line_derivative/pallas_call | solution.py:118
  426.6 24.6 %collective-permute-done.5 = f32[2,16,64,256]{3,2,1,0:T(8,128)} collective-permute-done((f32[2,16,64,256]{3,2,1,0:T(8,128)S(1)}, f32[2,16,64,256]{3,2,1,0:T(8,128)}, u32[]{:S(2)}, u32[]{:S(2)}) %collective-permute-start.5) | collective-permute-done | bytes 2097184 | tf_op jit(solution)/shard_map/ppermute | solution.py:434
  451.2 5.0 dynamic-slice_bitcast_fusion.6
  459.1 39.7 %base_products.1 = (f32[16,256,256]{2,1,0:T(8,128)}, f32[3,16,256,256]{3,2,1,0:T(8,128)}) custom-call(f32[256,256]{1,0:T(8,128)} %constant.244.clone.synth_ref, f32[256,256]{1,0:T(8,128)} %constant.245.clone.along_ref, f32[4,3,16,64,256]{4,3,2,1,0:T(8,128)} %bitcast_dynamic-update-slice_fusion.x_ref.u_ref, f32[4,3,16,64,256]{4,3,2,1,0:T(8,128)} %line_derivative.5.us_ref, ...), custom_call_target="tpu_custom_call" | custom-call | flops 28991029248 | bytes 67108864 | tf_op jit(solution)/shard_map/base_products/pallas_call | solution.py:157
  498.8 91.7 %collective-permute-done.6 = f32[2,16,64,256]{3,2,1,0:T(8,128)S(1)} collective-permute-done((f32[2,16,64,256]{3,2,1,0:T(8,128)S(1)}, f32[2,16,64,256]{3,2,1,0:T(8,128)S(1)}, u32[]{:S(2)}, u32[]{:S(2)}) %collective-permute-start.6) | collective-permute-done | bytes 2097184 | tf_op jit(solution)/shard_map/ppermute | solution.py:434
  599.8 21.0 %collective-permute-done.8 = f32[1,16,64,256]{3,2,1,0:T(8,128)S(1)} collective-permute-done((f32[1,16,64,256]{3,2,1,0:T(8,128)S(1)}, f32[1,16,64,256]{3,2,1,0:T(8,128)S(1)}, u32[]{:S(2)}, u32[]{:S(2)}) %collective-permute-start.8) | collective-permute-done | bytes 1048608 | tf_op jit(solution)/shard_map/ppermute | solution.py:434
  625.2 38.8 %forcing_modes.2 = f32[4,2,16,64,256]{4,3,2,1,0:T(8,128)} custom-call(f32[256,256]{1,0:T(8,128)} %constant.244.clone.synth_ref, f32[256,256]{1,0:T(8,128)} %constant.246.clone.analysis_ref, f32[4,2,16,64,256]{4,3,2,1,0:T(8,128)} %bitcast_dynamic-update-slice_fusion.6.ur_ref, f32[16,256,256]{2,1,0:T(8,128)} %get-tuple-element.73.vr_ref, ...), custom_call_target="tpu_custom_call" | custom-call | flops 12884901888 | bytes 33554432 | tf_op jit(solution)/shard_map/forcing_modes/pallas_call | solution.py:198
  664.0 29.0 %collective-permute-done.9 = f32[1,16,64,256]{3,2,1,0:T(8,128)S(1)} collective-permute-done((f32[1,16,64,256]{3,2,1,0:T(8,128)}, f32[1,16,64,256]{3,2,1,0:T(8,128)S(1)}, u32[]{:S(2)}, u32[]{:S(2)}) %collective-permute-start.9) | collective-permute-done | bytes 1048608 | tf_op jit(solution)/shard_map/ppermute | solution.py:434
  694.1 3.8 dynamic-slice_bitcast_fusion.5
  697.9 46.7 %collective-permute-done.11 = f32[2,16,64,256]{3,2,1,0:T(8,128)S(1)} collective-permute-done((f32[2,16,64,256]{3,2,1,0:T(8,128)S(1)}, f32[2,16,64,256]{3,2,1,0:T(8,128)S(1)}, u32[]{:S(2)}, u32[]{:S(2)}) %collective-permute-start.11) | collective-permute-done | bytes 2097184 | tf_op jit(solution)/shard_map/ppermute | solution.py:434
  746.7 3.4 copy-done.7
  752.0 20.4 %forcing_modes.3 = f32[4,1,16,64,256]{4,3,2,1,0:T(8,128)} custom-call(f32[256,256]{1,0:T(8,128)} %constant.244.clone.synth_ref, f32[256,256]{1,0:T(8,128)} %constant.246.clone.analysis_ref, f32[4,1,16,64,256]{4,3,2,1,0:T(8,128)} %copy-done.5, f32[16,256,256]{2,1,0:T(8,128)} %get-tuple-element.73.vr_ref, f32[3,16,256,256]{3,2,1,0:T(8,128)} %get-tuple-element.74.part_ref, ...), custom_call_target="tpu_custom_call" | custom-call | flops 6442450944 | bytes 16777216 | tf_op jit(solution)/shard_map/forcing_modes/pallas_call | solution.py:198
  772.4 114.9 %collective-permute-done.12 = f32[2,16,64,256]{3,2,1,0:T(8,128)S(1)} collective-permute-done((f32[2,16,64,256]{3,2,1,0:T(8,128)}, f32[2,16,64,256]{3,2,1,0:T(8,128)S(1)}, u32[]{:S(2)}, u32[]{:S(2)}) %collective-permute-start.12) | collective-permute-done | bytes 2097184 | tf_op jit(solution)/shard_map/ppermute | solution.py:434
  895.2 24.2 %collective-permute-done.14 = f32[1,16,64,256]{3,2,1,0:T(8,128)S(1)} collective-permute-done((f32[1,16,64,256]{3,2,1,0:T(8,128)S(1)}, f32[1,16,64,256]{3,2,1,0:T(8,128)S(1)}, u32[]{:S(2)}, u32[]{:S(2)}) %collective-permute-start.14) | collective-permute-done | bytes 1048608 | tf_op jit(solution)/shard_map/ppermute | solution.py:434
  923.9 26.1 %local_sums.2 = (f32[16392,128]{1,0:T(8,128)}, f32[2,232,128]{2,1,0:T(8,128)}) custom-call(s32[3560]{0:T(1024)} %pad.17.ck, s32[3560]{0:T(1024)} %pad.18.cr, s32[1]{0:T(128)} %bitcast.9.cn, s32[3559]{0:T(1024)} %fusion.10.fk, s32[3559]{0:T(1024)} %fusion.9.fr, s32[1]{0:T(128)} %bitcast.10.fn, s32[2,232]{1,0:T(2,128)} %pad.21.er, ...), custom_call_target="tpu_custom_call" | custom-call | flops 838860800 | bytes 25165824 | tf_op jit(solution)/shard_map/local_sums/pallas_call | solution.py:278
  951.0 3.6 collective-permute-start.17
  959.6 20.4 %spread.2.rest_0_ = f32[3,64,64,256]{3,2,1,0:T(8,128)} custom-call(s32[2,232]{1,0:T(2,128)} %pad.21.er, s32[3560]{0:T(1024)} %get-tuple-element.58.bk, s32[3560]{0:T(1024)} %get-tuple-element.59.br, f32[16392,128]{1,0:T(8,128)} %get-tuple-element.80.t_ref, f32[2,232,128]{2,1,0:T(8,128)} %pad_maximum_fusion.came_ref, f32[64,256]{1,0:T(8,128)} %div.40.inv_ref), custom_call_target="tpu_custom_call" | custom-call | flops 838860800 | bytes 25165824 | tf_op jit(solution)/shard_map/spread/pallas_call | solution.py:363
  980.0 11.7 %collective-permute-done.15 = f32[1,16,64,256]{3,2,1,0:T(8,128)S(1)} collective-permute-done((f32[1,16,64,256]{3,2,1,0:T(8,128)}, f32[1,16,64,256]{3,2,1,0:T(8,128)S(1)}, u32[]{:S(2)}, u32[]{:S(2)}) %collective-permute-start.15) | collective-permute-done | bytes 1048608 | tf_op jit(solution)/shard_map/ppermute | solution.py:434
  994.8 24.8 %local_sums.3 = (f32[16392,128]{1,0:T(8,128)}, f32[2,232,128]{2,1,0:T(8,128)}) custom-call(s32[3560]{0:T(1024)} %pad.17.ck, s32[3560]{0:T(1024)} %pad.18.cr, s32[1]{0:T(128)} %bitcast.9.cn, s32[3559]{0:T(1024)} %fusion.10.fk, s32[3559]{0:T(1024)} %fusion.9.fr, s32[1]{0:T(128)} %bitcast.10.fn, s32[2,232]{1,0:T(2,128)} %pad.21.er, ...), custom_call_target="tpu_custom_call" | custom-call | flops 838860800 | bytes 25165824 | tf_op jit(solution)/shard_map/local_sums/pallas_call | solution.py:278
  1028.1 18.4 %spread.3 = f32[3,64,64,256]{3,2,1,0:T(8,128)} custom-call(s32[2,232]{1,0:T(2,128)} %pad.21.er, s32[3560]{0:T(1024)} %get-tuple-element.58.bk, s32[3560]{0:T(1024)} %get-tuple-element.59.br, f32[16392,128]{1,0:T(8,128)} %get-tuple-element.84.t_ref, f32[2,232,128]{2,1,0:T(8,128)} %pad_maximum_fusion.1.came_ref, ...), custom_call_target="tpu_custom_call", output_to_operand_aliasing={{}: (6, {})} | custom-call | flops 838860800 | bytes 25165824 | tf_op jit(solution)/shard_map/spread/pallas_call | solution.py:363
  (138 shorter events, 100.0 us)
Async XLA Ops:
  0.0 406.1 %copy-start = (f32[4,64,256]{2,1,0:T(8,128)S(1)}, f32[4,64,256]{2,1,0:T(8,128)}, u32[]{:S(2)}) copy-start(f32[4,64,256]{2,1,0:T(8,128)} %param.13) | copy-start | bytes 786436
  22.5 128.8 %collective-permute-start = (f32[3,16,64,256]{3,2,1,0:T(8,128)S(1)}, f32[3,16,64,256]{3,2,1,0:T(8,128)}, u32[]{:S(2)}, u32[]{:S(2)}) collective-permute-start(f32[3,16,64,256]{3,2,1,0:T(8,128)S(1)} %dynamic-slice_bitcast_fusion.2), channel_id=1, source_target_pairs={{0,1},{1,2},{2,3},{3,0},{4,5},{5,6},{6,7},{7,4},{8,9},{9,10},{10,1... | collective-permute-start | bytes 9437192 | tf_op jit(solution)/shard_map/ppermute | solution.py:434
  115.1 117.4 %collective-permute-start.3 = (f32[225]{0:T(256)}, f32[225]{0:T(256)}, u32[]{:S(2)}, u32[]{:S(2)}) collective-permute-start(f32[225]{0:T(256)} %get-tuple-element.116), channel_id=1, source_target_pairs={{0,4},{4,8},{8,12},{12,16},{16,20},{20,24},{24,28},{28,0},{1,5},{5... | collective-permute-start | bytes 2708 | tf_op jit(solution)/shard_map/ppermute | solution.py:418
  117.2 115.3 %collective-permute-start.4 = (f32[225]{0:T(256)}, f32[225]{0:T(256)}, u32[]{:S(2)}, u32[]{:S(2)}) collective-permute-start(f32[225]{0:T(256)} %get-tuple-element.117), channel_id=1, source_target_pairs={{4,0},{8,4},{12,8},{16,12},{20,16},{24,20},{28,24},{0,28},{5,1},{9... | collective-permute-start | bytes 2708 | tf_op jit(solution)/shard_map/ppermute | solution.py:418
  117.2 11.6 %copy-start.14 = (s32[64,256]{1,0:T(8,128)S(1)}, s32[64,256]{1,0:T(8,128)}, u32[]{:S(2)}) copy-start(s32[64,256]{1,0:T(8,128)} %param.15) | copy-start | bytes 196612
  151.4 10.5 %copy-start.11 = (s32[128,128]{1,0:T(8,128)S(1)}, s32[128,128]{1,0:T(8,128)}, u32[]{:S(2)}) copy-start(s32[128,128]{1,0:T(8,128)} %copy.19) | copy-start | bytes 196612
  159.2 239.2 %collective-permute-start.1 = (f32[3,16,64,256]{3,2,1,0:T(8,128)}, f32[3,16,64,256]{3,2,1,0:T(8,128)}, u32[]{:S(2)}, u32[]{:S(2)}) collective-permute-start(f32[3,16,64,256]{3,2,1,0:T(8,128)} %get-tuple-element.90), channel_id=1, source_target_pairs={{0,2},{1,3},{2,0},{3,1},{4,6},{5,7},{6,4},{7,5},{8,10},{9,11},{10,... | collective-permute-start | bytes 9437192 | tf_op jit(solution)/shard_map/ppermute | solution.py:434
  160.2 242.2 %collective-permute-start.2 = (f32[3,16,64,256]{3,2,1,0:T(8,128)}, f32[3,16,64,256]{3,2,1,0:T(8,128)S(1)}, u32[]{:S(2)}, u32[]{:S(2)}) collective-permute-start(f32[3,16,64,256]{3,2,1,0:T(8,128)} %get-tuple-element.89), channel_id=1, source_target_pairs={{0,3},{1,0},{2,1},{3,2},{4,7},{5,4},{6,5},{7,6},{8,11},{9,8},{10,9... | collective-permute-start | bytes 9437192 | tf_op jit(solution)/shard_map/ppermute | solution.py:434
  181.2 13.9 %copy-start.12 = (s32[16384]{0:T(1024)S(1)}, s32[16384]{0:T(1024)}, u32[]{:S(2)}) copy-start(s32[16384]{0:T(1024)} %get-tuple-element.50) | copy-start | bytes 196612
  181.2 17.7 %copy-start.18 = (s32[16384]{0:T(1024)S(1)}, s32[16384]{0:T(1024)}, u32[]{:S(2)}) copy-start(s32[16384]{0:T(1024)} %get-tuple-element.52) | copy-start | bytes 196612
  181.2 17.7 %copy-start.19 = (s32[16384]{0:T(1024)S(1)}, s32[16384]{0:T(1024)}, u32[]{:S(2)}) copy-start(s32[16384]{0:T(1024)} %get-tuple-element.53) | copy-start | bytes 196612
  181.2 20.3 %copy-start.20 = (pred[3560]{0:T(1024)(128)(4,1)S(1)}, pred[3560]{0:T(1024)(128)(4,1)}, u32[]{:S(2)}) copy-start(pred[3560]{0:T(1024)(128)(4,1)} %constant.238.clone.1) | copy-start | bytes 10684
  181.2 20.9 %copy-start.15 = (s32[16384,1]{0,1:T(1,128)S(1)}, s32[16384,1]{0,1:T(1,128)}, u32[]{:S(2)}) copy-start(s32[16384,1]{0,1:T(1,128)} %compare_select_fusion) | copy-start | bytes 196612
  406.0 45.2 %collective-permute-start.5 = (f32[2,16,64,256]{3,2,1,0:T(8,128)S(1)}, f32[2,16,64,256]{3,2,1,0:T(8,128)}, u32[]{:S(2)}, u32[]{:S(2)}) collective-permute-start(f32[2,16,64,256]{3,2,1,0:T(8,128)S(1)} %dynamic-slice_bitcast_fusion.8), channel_id=1, source_target_pairs={{0,1},{1,2},{2,3},{3,0},{4,5},{5,6},{6,7},{7,4},{8,9},{9,10},{10,1... | collective-permute-start | bytes 6291464 | tf_op jit(solution)/shard_map/ppermute | solution.py:434
  456.2 134.3 %collective-permute-start.6 = (f32[2,16,64,256]{3,2,1,0:T(8,128)S(1)}, f32[2,16,64,256]{3,2,1,0:T(8,128)S(1)}, u32[]{:S(2)}, u32[]{:S(2)}) collective-permute-start(f32[2,16,64,256]{3,2,1,0:T(8,128)S(1)} %get-tuple-element.96), channel_id=1, source_target_pairs={{0,2},{1,3},{2,0},{3,1},{4,6},{5,7},{6,4},{7,5},{8,10},{9,11},{10,... | collective-permute-start | bytes 6291464 | tf_op jit(solution)/shard_map/ppermute | solution.py:434
  457.0 138.1 %collective-permute-start.7 = (f32[2,16,64,256]{3,2,1,0:T(8,128)S(1)}, f32[2,16,64,256]{3,2,1,0:T(8,128)}, u32[]{:S(2)}, u32[]{:S(2)}) collective-permute-start(f32[2,16,64,256]{3,2,1,0:T(8,128)S(1)} %get-tuple-element.95), channel_id=1, source_target_pairs={{0,3},{1,0},{2,1},{3,2},{4,7},{5,4},{6,5},{7,6},{8,11},{9,8},{10,9... | collective-permute-start | bytes 6291464 | tf_op jit(solution)/shard_map/ppermute | solution.py:434
  598.4 22.4 %collective-permute-start.8 = (f32[1,16,64,256]{3,2,1,0:T(8,128)S(1)}, f32[1,16,64,256]{3,2,1,0:T(8,128)S(1)}, u32[]{:S(2)}, u32[]{:S(2)}) collective-permute-start(f32[1,16,64,256]{3,2,1,0:T(8,128)S(1)} %dynamic-slice_bitcast_fusion.14), channel_id=1, source_target_pairs={{0,1},{1,2},{2,3},{3,0},{4,5},{5,6},{6,7},{7,4},{8,9},{9,10},{10,1... | collective-permute-start | bytes 3145736 | tf_op jit(solution)/shard_map/ppermute | solution.py:434
  622.1 70.9 %collective-permute-start.9 = (f32[1,16,64,256]{3,2,1,0:T(8,128)}, f32[1,16,64,256]{3,2,1,0:T(8,128)S(1)}, u32[]{:S(2)}, u32[]{:S(2)}) collective-permute-start(f32[1,16,64,256]{3,2,1,0:T(8,128)} %get-tuple-element.102), channel_id=1, source_target_pairs={{0,2},{1,3},{2,0},{3,1},{4,6},{5,7},{6,4},{7,5},{8,10},{9,11},{10,... | collective-permute-start | bytes 3145736 | tf_op jit(solution)/shard_map/ppermute | solution.py:434
  625.2 68.8 %collective-permute-start.10 = (f32[1,16,64,256]{3,2,1,0:T(8,128)S(1)}, f32[1,16,64,256]{3,2,1,0:T(8,128)S(1)}, u32[]{:S(2)}, u32[]{:S(2)}) collective-permute-start(f32[1,16,64,256]{3,2,1,0:T(8,128)S(1)} %get-tuple-element.101), channel_id=1, source_target_pairs={{0,3},{1,0},{2,1},{3,2},{4,7},{5,4},{6,5},{7,6},{8,11},{9,8},{10,9... | collective-permute-start | bytes 3145736 | tf_op jit(solution)/shard_map/ppermute | solution.py:434
  693.0 51.6 %copy-start.6 = (f32[4,2,16,64,256]{4,3,2,1,0:T(8,128)S(1)}, f32[4,2,16,64,256]{4,3,2,1,0:T(8,128)}, u32[]{:S(2)}) copy-start(f32[4,2,16,64,256]{4,3,2,1,0:T(8,128)} %forcing_modes.2) | copy-start | bytes 25165828
  694.1 52.7 %copy-start.5 = (f32[4,1,16,64,256]{4,3,2,1,0:T(8,128)}, f32[4,1,16,64,256]{4,3,2,1,0:T(8,128)S(1)}, u32[]{:S(2)}) copy-start(f32[4,1,16,64,256]{4,3,2,1,0:T(8,128)S(1)} %bitcast_dynamic-update-slice_fusion.12.ur_ref) | copy-start | bytes 12582916
  697.8 46.8 %collective-permute-start.11 = (f32[2,16,64,256]{3,2,1,0:T(8,128)S(1)}, f32[2,16,64,256]{3,2,1,0:T(8,128)S(1)}, u32[]{:S(2)}, u32[]{:S(2)}) collective-permute-start(f32[2,16,64,256]{3,2,1,0:T(8,128)S(1)} %dynamic-slice_bitcast_fusion.5), channel_id=1, source_target_pairs={{0,1},{1,2},{2,3},{3,0},{4,5},{5,6},{6,7},{7,4},{8,9},{9,10},{10,1... | collective-permute-start | bytes 6291464 | tf_op jit(solution)/shard_map/ppermute | solution.py:434
  750.1 137.2 %collective-permute-start.12 = (f32[2,16,64,256]{3,2,1,0:T(8,128)}, f32[2,16,64,256]{3,2,1,0:T(8,128)S(1)}, u32[]{:S(2)}, u32[]{:S(2)}) collective-permute-start(f32[2,16,64,256]{3,2,1,0:T(8,128)} %get-tuple-element.93), channel_id=1, source_target_pairs={{0,2},{1,3},{2,0},{3,1},{4,6},{5,7},{6,4},{7,5},{8,10},{9,11},{10,... | collective-permute-start | bytes 6291464 | tf_op jit(solution)/shard_map/ppermute | solution.py:434
  752.0 139.9 %collective-permute-start.13 = (f32[2,16,64,256]{3,2,1,0:T(8,128)S(1)}, f32[2,16,64,256]{3,2,1,0:T(8,128)}, u32[]{:S(2)}, u32[]{:S(2)}) collective-permute-start(f32[2,16,64,256]{3,2,1,0:T(8,128)S(1)} %get-tuple-element.92), channel_id=1, source_target_pairs={{0,3},{1,0},{2,1},{3,2},{4,7},{5,4},{6,5},{7,6},{8,11},{9,8},{10,9... | collective-permute-start | bytes 6291464 | tf_op jit(solution)/shard_map/ppermute | solution.py:434
  895.2 24.3 %collective-permute-start.14 = (f32[1,16,64,256]{3,2,1,0:T(8,128)S(1)}, f32[1,16,64,256]{3,2,1,0:T(8,128)S(1)}, u32[]{:S(2)}, u32[]{:S(2)}) collective-permute-start(f32[1,16,64,256]{3,2,1,0:T(8,128)S(1)} %dynamic-slice_bitcast_fusion.11), channel_id=1, source_target_pairs={{0,1},{1,2},{2,3},{3,0},{4,5},{5,6},{6,7},{7,4},{8,9},{9,10},{10,1... | collective-permute-start | bytes 3145736 | tf_op jit(solution)/shard_map/ppermute | solution.py:434
  920.9 70.9 %collective-permute-start.15 = (f32[1,16,64,256]{3,2,1,0:T(8,128)}, f32[1,16,64,256]{3,2,1,0:T(8,128)S(1)}, u32[]{:S(2)}, u32[]{:S(2)}) collective-permute-start(f32[1,16,64,256]{3,2,1,0:T(8,128)} %get-tuple-element.99), channel_id=1, source_target_pairs={{0,2},{1,3},{2,0},{3,1},{4,6},{5,7},{6,4},{7,5},{8,10},{9,11},{10,... | collective-permute-start | bytes 3145736 | tf_op jit(solution)/shard_map/ppermute | solution.py:434
  923.9 68.8 %collective-permute-start.16 = (f32[1,16,64,256]{3,2,1,0:T(8,128)S(1)}, f32[1,16,64,256]{3,2,1,0:T(8,128)S(1)}, u32[]{:S(2)}, u32[]{:S(2)}) collective-permute-start(f32[1,16,64,256]{3,2,1,0:T(8,128)S(1)} %get-tuple-element.98), channel_id=1, source_target_pairs={{0,3},{1,0},{2,1},{3,2},{4,7},{5,4},{6,5},{7,6},{8,11},{9,8},{10,9... | collective-permute-start | bytes 3145736 | tf_op jit(solution)/shard_map/ppermute | solution.py:434
  951.0 5.9 collective-permute-start.17
  954.6 4.3 collective-permute-start.18
  1020.5 4.8 collective-permute-start.19
  1023.1 4.3 collective-permute-start.20
  1028.1 18.4 %copy-start.1 = (f32[4,64,256]{2,1,0:T(8,128)S(1)}, f32[4,64,256]{2,1,0:T(8,128)}, u32[]{:S(2)}) copy-start(f32[4,64,256]{2,1,0:T(8,128)} %param.13) | copy-start | bytes 786436
  (10 other events, 37.7 us)

commit v4 on v2

v4 whole, which is shorter than its diff:
```python
import math

import jax
import jax.numpy as jnp
import ml_dtypes
import numpy as np
from jax import lax
from jax.experimental import pallas as pl
from jax.experimental.pallas import tpu as pltpu
from jax.sharding import PartitionSpec as P

NP = 8
PLANES = 256
UNIQUE = 12825
STEP_SIZE = 0.1
LANES = 128
BATCH = 8
RANKS = 3
VMEM_LIMIT = 56 * 1024 * 1024


def legendre_values(degree, point):
    before = 1.0
    current = point
    for order in range(1, degree):
        after = ((2 * order + 1) * point * current - order * before) / (order + 1)
        before = current
        current = after
    return (current, before)


def gll_derivative(points_n):
    degree = points_n - 1
    points = []
    for index in range(points_n):
        point = -math.cos(math.pi * index / degree)
        for sweep in range(100):
            top_val, below_val = legendre_values(degree, point)
            point = point - (point * top_val - below_val) / (points_n * top_val)
        points.append(point)
    values = [legendre_values(degree, point)[0] for point in points]
    deriv_rows = []
    for row_index in range(points_n):
        row_vals = []
        for col_index in range(points_n):
            if row_index != col_index:
                row_vals.append(
                    values[row_index]
                    / (values[col_index] * (points[row_index] - points[col_index]))
                )
            else:
                row_vals.append(0.0)
        deriv_rows.append(row_vals)
    deriv_rows[0][0] = -degree * (degree + 1) / 4.0
    deriv_rows[degree][degree] = degree * (degree + 1) / 4.0
    return deriv_rows


def plane_tables(planes):
    plane = np.arange(planes)
    wave = plane // 2
    phase = ((plane[:, None] * wave[None, :]) % planes) * (2.0 * math.pi / planes)
    synth = np.where((plane % 2 == 1)[None, :], np.sin(phase), np.cos(phase))
    synth[:, 1] = 1 - 2 * (plane % 2)
    scales = np.where(wave == 0, 1.0 / planes, 2.0 / planes)
    analysis = synth.T * scales[:, None]
    number = wave * (2.0 / planes)
    along = np.zeros_like(synth)
    along[:, 1::2] = number[1::2] * synth[:, 0::2]
    along[:, 0::2] = -number[0::2] * synth[:, 1::2]
    along[:, :2] = 0.0
    return tuple(t.astype(np.float32) for t in (synth, along, analysis))


def params(**kw):
    return pltpu.CompilerParams(vmem_limit_bytes=VMEM_LIMIT, **kw)


def node_major(x, parts):
    c_n, m_n, n_n, e_n = x.shape
    l_n = n_n // parts
    rows = 16

    def kernel(x_ref, o_ref):
        for n in range(0, n_n, 8):
            turned = jnp.swapaxes(x_ref[0, :, n : n + 8, :], 0, 1)
            for t in range(8):
                o_ref[(n + t) // l_n, 0, (n + t) % l_n] = turned[t]

    return pl.pallas_call(
        kernel,
        grid=(c_n, m_n // rows),
        in_specs=[pl.BlockSpec((1, rows, n_n, e_n), lambda c, m: (c, m, 0, 0))],
        out_specs=pl.BlockSpec((parts, 1, l_n, rows, e_n), lambda c, m: (0, c, 0, m, 0)),
        out_shape=jax.ShapeDtypeStruct((parts, c_n, l_n, m_n, e_n), jnp.float32),
        compiler_params=params(),
        cost_estimate=pl.CostEstimate(flops=x.size, bytes_accessed=8 * x.size, transcendentals=0),
        name="node_major",
    )(x)


def derivative(x, groups, first=0, c_n=3):
    a_n, _, l_n, m_n, e_n = x.shape
    deriv = gll_derivative(NP)
    rows = 8

    def kernel(x_ref, o_ref):
        for line in groups:
            vals = [x_ref[a, 0, l] for a, l in line]
            for i, (a, l) in enumerate(line):
                total = deriv[i][0] * vals[0]
                for k in range(1, NP):
                    if deriv[i][k] != 0.0:
                        total = total + deriv[i][k] * vals[k]
                o_ref[a, 0, l] = total

    block = (a_n, 1, l_n, rows, e_n)
    size = a_n * c_n * l_n * m_n * e_n
    return pl.pallas_call(
        kernel,
        grid=(c_n, m_n // rows),
        in_specs=[pl.BlockSpec(block, lambda c, m: (0, first + c, 0, m, 0))],
        out_specs=pl.BlockSpec(block, lambda c, m: (0, c, 0, m, 0)),
        out_shape=jax.ShapeDtypeStruct((a_n, c_n, l_n, m_n, e_n), jnp.float32),
        compiler_params=params(),
        cost_estimate=pl.CostEstimate(flops=16 * size, bytes_accessed=8 * size, transcendentals=0),
        name="line_derivative",
    )(x)


def split(x):
    high = x.astype(jnp.bfloat16)
    return high, (x - high.astype(jnp.float32)).astype(jnp.bfloat16)


def left_form(table):
    high = table.astype(ml_dtypes.bfloat16)
    low = (table - high.astype(np.float32)).astype(ml_dtypes.bfloat16)
    return jnp.asarray(np.concatenate([high, high, low], axis=1))


def right_form(x):
    high, low = split(x)
    return jnp.concatenate([high, low, high], axis=0)


def product(left, right):
    return jnp.dot(left, right, preferred_element_type=jnp.float32)


def base_products(synth_along, synth, u_a, u_b, us_a, us_b, base, geo):
    s_n, _, l_n, m_n, e_n = u_a.shape
    p_n = base.shape[2]

    def kernel(both_ref, synth_ref, ua_ref, ub_ref, usa_ref, usb_ref, b_ref, g_ref, vr_ref, part_ref):
        l = pl.program_id(0)
        field = lambda i: b_ref[i, 0].astype(jnp.float32)
        g = [g_ref[i, pl.ds(l, 1), :] for i in range(4)]
        ux, uy = field(0), field(1)
        vr_ref[0] = ux * g[0] + uy * g[2]
        vs = ux * g[1] + uy * g[3]
        uz = field(2)
        phys = []
        for c in range(3):
            u_c = ua_ref[:, 0, 0] if c == 0 else ub_ref[:, c - 1, 0]
            us_c = usa_ref[:, 0, 0] if c == 0 else usb_ref[:, c - 1, 0]
            both = product(both_ref[...], right_form(u_c.reshape(s_n * m_n, e_n)))
            phys.append(both[:p_n])
            ds = product(synth_ref[...], right_form(us_c.reshape(s_n * m_n, e_n)))
            part_ref[c, 0] = -(vs * ds) - uz * both[p_n:]
        for c in range(3):
            part_ref[c, 0] += phys[0] * field(3 + 3 * c) + phys[1] * field(4 + 3 * c) + phys[2] * field(5 + 3 * c)

    one = pl.BlockSpec((s_n, 1, 1, m_n, e_n), lambda l: (0, 0, l, 0, 0))
    two = pl.BlockSpec((s_n, 2, 1, m_n, e_n), lambda l: (0, 0, l, 0, 0))
    return pl.pallas_call(
        kernel,
        grid=(l_n,),
        in_specs=[
            pl.BlockSpec((2 * p_n, 3 * p_n), lambda l: (0, 0)),
            pl.BlockSpec((p_n, 3 * p_n), lambda l: (0, 0)),
            one,
            two,
            one,
            two,
            pl.BlockSpec((12, 1, p_n, e_n), lambda l: (0, l, 0, 0)),
            pl.BlockSpec((4, l_n, e_n), lambda l: (0, 0, 0)),
        ],
        out_specs=[
            pl.BlockSpec((1, p_n, e_n), lambda l: (l, 0, 0)),
            pl.BlockSpec((3, 1, p_n, e_n), lambda l: (0, l, 0, 0)),
        ],
        out_shape=[
            jax.ShapeDtypeStruct((l_n, p_n, e_n), jnp.float32),
            jax.ShapeDtypeStruct((3, l_n, p_n, e_n), jnp.float32),
        ],
        compiler_params=params(),
        cost_estimate=pl.CostEstimate(
            flops=9 * 2 * 3 * l_n * p_n * p_n * e_n, bytes_accessed=l_n * p_n * e_n * 64, transcendentals=0
        ),
        name="base_products",
    )(synth_along, synth, u_a, u_b, us_a, us_b, base, geo)


def forcing_modes(synth, analysis, ur, vr, part, mass, held_at, first, c_n):
    s_n, _, l_n, m_n, e_n = ur.shape
    p_n = vr.shape[1]

    def kernel(synth_ref, analysis_ref, ur_ref, vr_ref, part_ref, mass_ref, o_ref):
        l = pl.program_id(1)
        dr = product(synth_ref[...], right_form(ur_ref[:, 0, 0].reshape(s_n * m_n, e_n)))
        forcing = part_ref[0, 0] - vr_ref[0] * dr
        modes = product(analysis_ref[...], right_form(forcing)) * (STEP_SIZE * mass_ref[pl.ds(l, 1), :])
        o_ref[:, 0, 0] = modes.reshape(s_n, m_n, e_n)

    whole = pl.BlockSpec((p_n, 3 * p_n), lambda c, l: (0, 0))
    block = (s_n, 1, 1, m_n, e_n)
    return pl.pallas_call(
        kernel,
        grid=(c_n, l_n),
        in_specs=[
            whole,
            whole,
            pl.BlockSpec(block, lambda c, l: (0, held_at + c, l, 0, 0)),
            pl.BlockSpec((1, p_n, e_n), lambda c, l: (l, 0, 0)),
            pl.BlockSpec((1, 1, p_n, e_n), lambda c, l: (first + c, l, 0, 0)),
            pl.BlockSpec((l_n, e_n), lambda c, l: (0, 0)),
        ],
        out_specs=pl.BlockSpec(block, lambda c, l: (0, c, l, 0, 0)),
        out_shape=jax.ShapeDtypeStruct((s_n, c_n, l_n, m_n, e_n), jnp.float32),
        compiler_params=params(),
        cost_estimate=pl.CostEstimate(
            flops=2 * 2 * 3 * c_n * l_n * p_n * p_n * e_n,
            bytes_accessed=c_n * l_n * p_n * e_n * 16,
            transcendentals=0,
        ),
        name="forcing_modes",
    )(synth, analysis, ur, vr, part, mass)


def local_sums(modes, u, mass, pairs, edge_reps, first):
    s_n, c_n, l_n, m_n, e_n = modes.shape
    nodes_n = s_n * l_n
    rows_n = nodes_n * e_n
    step = min(8, l_n)
    per = l_n // step
    members, reps, bounds = pairs
    edges_n = edge_reps.shape[1]
    feats = c_n * m_n

    def kernel(mem, rep, bnd, er, f_ref, u_ref, mass_ref, o_ref, low_ref, up_ref):
        b = pl.program_id(0)
        for t in range(step):
            node = b * step + t
            weight = mass_ref[pl.ds(node, 1), :]
            rows = [f_ref[0, c, t] + weight * u_ref[0, c, t] for c in range(c_n)]
            table = jnp.concatenate(rows, axis=0) if c_n > 1 else rows[0]
            o_ref[pl.ds(pl.multiple_of(node * e_n, e_n), e_n), :] = table.T

        @pl.when(b == pl.num_programs(0) - 1)
        def _():
            o_ref[pl.ds(rows_n, 8), :] = jnp.zeros((8, feats), jnp.float32)

            for rank in range(RANKS):

                def close(i, _):
                    at = bnd[2 * rank] + i * BATCH
                    heads = [rep[at + t] for t in range(BATCH)]
                    others = [mem[at + t] for t in range(BATCH)]
                    sums = [o_ref[pl.ds(r, 1), :] + o_ref[pl.ds(k, 1), :] for r, k in zip(heads, others)]
                    for r, total in zip(heads, sums):
                        o_ref[pl.ds(r, 1), :] = total
                    return 0

                lax.fori_loop(0, pl.cdiv(bnd[2 * rank + 1], BATCH), close, 0)

            def far(i, _):
                at = bnd[2 * RANKS] + i
                r = rep[at]
                o_ref[pl.ds(r, 1), :] = o_ref[pl.ds(r, 1), :] + o_ref[pl.ds(mem[at], 1), :]
                return 0

            lax.fori_loop(0, bnd[2 * RANKS + 1], far, 0)

            def edge(i, _):
                for side, to in enumerate((low_ref, up_ref)):
                    got = [o_ref[pl.ds(er[side, i * BATCH + t], 1), :] for t in range(BATCH)]
                    for t, row in enumerate(got):
                        to[pl.ds(i * BATCH + t, 1), :] = row
                return 0

            lax.fori_loop(0, edges_n // BATCH, edge, 0)

    smem = pl.BlockSpec(memory_space=pltpu.SMEM)
    where = lambda b: (b // per, 0, b % per, 0, 0)
    where_u = lambda b: (b // per, first // c_n, b % per, 0, 0)
    rim = pl.BlockSpec((edges_n, feats), lambda b: (0, 0))
    rim_shape = jax.ShapeDtypeStruct((edges_n, feats), jnp.float32)
    return pl.pallas_call(
        kernel,
        grid=(nodes_n // step,),
        in_specs=[smem] * 4
        + [
            pl.BlockSpec((1, c_n, step, m_n, e_n), where),
            pl.BlockSpec((1, c_n, step, m_n, e_n), where_u),
            pl.BlockSpec((nodes_n, e_n), lambda b: (0, 0)),
        ],
        out_specs=[pl.BlockSpec((rows_n + 8, feats), lambda b: (0, 0)), rim, rim],
        out_shape=[jax.ShapeDtypeStruct((rows_n + 8, feats), jnp.float32), rim_shape, rim_shape],
        compiler_params=params(),
        cost_estimate=pl.CostEstimate(
            flops=rows_n * LANES * 400, bytes_accessed=rows_n * LANES * 12, transcendentals=0
        ),
        name="local_sums",
    )(members, reps, bounds, edge_reps, modes, u, mass)


def spread(table, rims, pairs, edge_reps, inverse, held, shape, first, c_n):
    _, m_n, nodes_n, e_n = shape
    rows_n = nodes_n * e_n
    step = 8
    edges_n = edge_reps.shape[1]
    members, reps, _ = pairs
    pairs_n = members.shape[0]
    feats = c_n * m_n

    def kernel(mem, rep, er, t_ref, low_ref, up_ref, inv_ref, *rest):
        o_ref, stage = rest[-2:]
        b = pl.program_id(0)

        @pl.when(b == 0)
        def _():
            def edge(i, _):
                for side, came in enumerate((low_ref, up_ref)):
                    spots = [er[side, i * BATCH + t] for t in range(BATCH)]
                    sums = [
                        t_ref[pl.ds(r, 1), :] + came[pl.ds(i * BATCH + t, 1), :] for t, r in enumerate(spots)
                    ]
                    for r, total in zip(spots, sums):
                        t_ref[pl.ds(r, 1), :] = total
                return 0

            lax.fori_loop(0, edges_n // BATCH, edge, 0)

            def back(i, _):
                got = [t_ref[pl.ds(rep[i * BATCH + t], 1), :] for t in range(BATCH)]
                for t, row in enumerate(got):
                    t_ref[pl.ds(mem[i * BATCH + t], 1), :] = row
                return 0

            lax.fori_loop(0, pairs_n // BATCH, back, 0)

        for t in range(step):
            n = b * step + t
            rows = t_ref[pl.ds(pl.multiple_of(n * e_n, e_n), e_n), :].T
            scaled = rows * inv_ref[pl.ds(n, 1), :]
            for c in range(c_n):
                stage[c, t] = scaled[c * m_n : (c + 1) * m_n]
        for c in range(c_n):
            o_ref[c] = jnp.swapaxes(stage[c], 0, 1)

    smem = pl.BlockSpec(memory_space=pltpu.SMEM)
    rim = pl.BlockSpec((edges_n, feats), lambda b: (0, 0))
    in_specs = [smem] * 3 + [
        pl.BlockSpec((rows_n + 8, feats), lambda b: (0, 0)),
        rim,
        rim,
        pl.BlockSpec((nodes_n, e_n), lambda b: (0, 0)),
    ]
    args = [members, reps, edge_reps, table, *rims, inverse]
    aliases = {}
    if held is not None:
        in_specs.append(pl.BlockSpec(memory_space=pl.ANY))
        args.append(held)
        aliases = {len(args) - 1: 0}
    return pl.pallas_call(
        kernel,
        grid=(nodes_n // step,),
        in_specs=in_specs,
        out_specs=pl.BlockSpec((c_n, m_n, step, e_n), lambda b: (first // c_n, 0, b, 0)),
        out_shape=jax.ShapeDtypeStruct(shape, jnp.float32),
        scratch_shapes=[pltpu.VMEM((c_n, step, m_n, e_n), jnp.float32)],
        input_output_aliases=aliases,
        compiler_params=params(),
        cost_estimate=pl.CostEstimate(
            flops=rows_n * LANES * 400, bytes_accessed=rows_n * LANES * 12, transcendentals=0
        ),
        name="spread",
    )(*args)


def fill_up(values, multiple, filler):
    short = -values.shape[-1] % multiple
    pad = [(0, 0)] * (values.ndim - 1) + [(0, short)]
    return jnp.pad(values, pad, constant_values=filler)


def pair_lists(ids, edges):
    rows_n = ids.shape[0]
    place = jnp.arange(rows_n, dtype=jnp.int32)
    ids_sorted, member = lax.sort((ids, place), num_keys=1)
    head = jnp.concatenate([jnp.ones((1,), bool), ids_sorted[1:] != ids_sorted[:-1]])
    code = lax.cummax(jnp.where(head, place * rows_n + member, 0))
    rep = code % rows_n
    rank = place - code // rows_n
    group = jnp.where(rank == 0, RANKS + 2, jnp.minimum(rank, RANKS + 1)).astype(jnp.int32)
    spare = jnp.full((RANKS * BATCH,), rows_n, jnp.int32)
    spare_group = jnp.arange(RANKS * BATCH, dtype=jnp.int32) // BATCH + 1
    _, members, reps = lax.sort(
        (
            jnp.concatenate([group, spare_group]),
            jnp.concatenate([member, spare]),
            jnp.concatenate([rep, spare]),
        ),
        num_keys=1,
        is_stable=True,
    )
    pairs_n = rows_n - UNIQUE + RANKS * BATCH
    numbers = jnp.stack([jnp.sum(group == r, dtype=jnp.int32) for r in range(1, RANKS + 2)])
    starts = jnp.cumsum(numbers) - numbers + BATCH * jnp.arange(RANKS + 1, dtype=jnp.int32)
    bounds = jnp.stack([starts, numbers], axis=1).reshape(-1).astype(jnp.int32)
    members = fill_up(members[:pairs_n], BATCH, rows_n)
    reps = fill_up(reps[:pairs_n], BATCH, rows_n)
    flat = edges.reshape(-1)
    start = jnp.sum(ids_sorted[None, :] < flat[:, None], axis=1, dtype=jnp.int32)
    edge_reps = fill_up(member[start].reshape(edges.shape), BATCH, rows_n)
    return (members, reps, bounds), edge_reps


def swap_edges(low, up):
    count = lax.axis_size("mesh")
    upward = [(i, (i + 1) % count) for i in range(count)]
    downward = [(j, i) for i, j in upward]
    return lax.ppermute(up, "mesh", upward), lax.ppermute(low, "mesh", downward)


def inverse_mass(mass, ids, edges):
    summed = jnp.zeros((UNIQUE,), jnp.float32).at[ids].add(mass.reshape(-1))
    came = jnp.concatenate(swap_edges(summed[edges[0]], summed[edges[1]]))
    summed = summed.at[edges.reshape(-1)].add(came)
    return (1.0 / summed[ids]).reshape(mass.shape)


def exchange(x):
    return lax.all_to_all(x, "four", split_axis=0, concat_axis=0, tiled=True)


def body(adj_modes, base_flow, geometry, mass, connect, edge_nodes):
    comps, m_n, nodes_n, e_n = adj_modes.shape
    parts = lax.axis_size("four")
    l_n = nodes_n // parts
    mine = lax.axis_index("four") * l_n
    synth, along, analysis = plane_tables(PLANES)
    both_3 = left_form(np.concatenate([synth, along]))
    synth_3, analysis_3 = left_form(synth), left_form(analysis)
    together = lax.optimization_barrier
    spot = lambda n: (n // l_n, n % l_n)
    along_r = [[spot(NP * i + j) for i in range(NP)] for j in range(NP)]
    along_s = [[spot(NP * i + j) for j in range(NP)] for i in range(NP)]
    inside = [[(a, l + j) for j in range(NP)] for a in range(parts) for l in range(0, l_n, NP)]
    whole_rows = l_n % NP == 0

    u_first = adj_modes[0].reshape(m_n, parts, l_n, e_n).transpose(1, 0, 2, 3)
    u_first, adj_modes = together((u_first, adj_modes))
    first_here = exchange(u_first)

    u = node_major(adj_modes, parts)
    ur_a, ur_b = derivative(u, along_r, 0, 2), derivative(u, along_r, 2, 1)
    sent = [u[:, 1:], ur_a] + ([] if whole_rows else [derivative(u, along_s)])
    sent = jnp.concatenate(sent, axis=1)
    sent, u, ur_b, first_here, connect, edge_nodes, mass, base_flow = together(
        (sent, u, ur_b, first_here, connect, edge_nodes, mass, base_flow)
    )

    here = exchange(sent)
    edges = edge_nodes[0]
    ids = connect.reshape(-1)
    pairs, edge_reps = pair_lists(ids, edges)
    inverse = inverse_mass(mass, ids, edges)
    base = base_flow.transpose(0, 2, 1, 3)
    if l_n % 8 == 0:
        u0_here = node_major(first_here, 1).reshape(parts, 1, l_n, m_n, e_n)
    else:
        u0_here = first_here.transpose(0, 2, 1, 3)[:, None]
    us0_here = derivative(u0_here, inside, 0, 1) if whole_rows else None
    held = (here, ur_b, pairs, edge_reps, inverse, base, u0_here, us0_here)
    here, ur_b, pairs, edge_reps, inverse, base, u0_here, us0_here = together(held)

    ur_b_here = exchange(ur_b)
    us_here = derivative(here, inside, 0, 2) if whole_rows else here[:, 5:7]
    if not whole_rows:
        us0_here = here[:, 4:5]
    geo = lax.dynamic_slice_in_dim(geometry, mine, l_n, 1)
    mass_here = lax.dynamic_slice_in_dim(mass, mine, l_n, 0)
    vr, part = base_products(both_3, synth_3, u0_here, here, us0_here, us_here, base, geo)
    f_a = forcing_modes(synth_3, analysis_3, here, vr, part, mass_here, 2, 0, 2)
    f_a, ur_b_here = together((f_a, ur_b_here))

    modes_a = exchange(f_a)
    f_b = forcing_modes(synth_3, analysis_3, ur_b_here, vr, part, mass_here, 0, 2, 1)
    f_b, modes_a = together((f_b, modes_a))

    modes_b = exchange(f_b)
    table, *rims = local_sums(modes_a, u, mass, pairs, edge_reps, 0)
    out = spread(table, swap_edges(*rims), pairs, edge_reps, inverse, None, adj_modes.shape, 0, 2)
    modes_b, out = together((modes_b, out))

    table, *rims = local_sums(modes_b, u, mass, pairs, edge_reps, 2)
    return spread(table, swap_edges(*rims), pairs, edge_reps, inverse, out, adj_modes.shape, 2, 1)


def solution(mesh):
    return jax.shard_map(
        body,
        mesh=mesh,
        in_specs=(
            P(None, "four", None, "mesh"),
            P(None, None, "four", "mesh"),
            P(None, None, "mesh"),
            P(None, "mesh"),
            P(None, "mesh"),
            P("mesh", None, None),
        ),
        out_specs=P(None, "four", None, "mesh"),
        check_vma=False,
    )
```

time: 928 us -> 905 us (0.975)
  waiting for transfers between devices: 377 us -> 343 us
  Pallas kernels: 250 us -> 225 us
  other arithmetic: 114 us -> 139 us
  local copies, waits for them, and re-layouts: 127 us -> 138 us
    all_to_all x5, waiting for transfers between devices: 368 us -> 333 us  [exchange(): return lax.all_to_all(x, 'four', split_axis=0, concat_axis=0, tiled=True)]
    pallas_call x6 -> x7, Pallas kernels: 170 us -> 149 us  [the longest x2 50 us: forcing_modes(): pl.pallas_call(kernel, grid=(c_n, l_n), in_specs=[whole, whole, pl.BlockS...]
    sort x1, other arithmetic: 8.67 us -> 19.5 us  [pair_lists(): lax.sort((jnp.concatenate([group, spare_group]), jnp.concatenate([member,...]
    concatenate x2 -> x3, other arithmetic: 1.4 us -> 11.7 us  [the longest x1 11.7 us: body(): sent = jnp.concatenate(sent, axis=1)]
    slice x3 -> x5, local copies, waits for them, and re-layouts: 0.19 us -> 10.1 us  [the longest x1 7.72 us: body(): sent = [u[:, 1:], ur_a] + ([] if whole_rows else [derivative(u, along_s)])]
    pallas_call x3 -> x4, Pallas kernels: 41 us -> 42.4 us  [derivative(): pl.pallas_call(kernel, grid=(c_n, m_n // rows), in_specs=[pl.BlockSpec(bl...]
  transfers between devices with their start and end apart: 11 -> 11, of which waited for: 9 -> 9; matrix products, arithmetic and copies ran while one was open for 26% -> 30% of each run, Pallas kernels for 20% -> 21%
where the time goes in v4:
time: 905 us; the launch traced here: 898 us
  waiting for transfers between devices  343 us (38%)
  Pallas kernels  225 us (25%)
  other arithmetic  139 us (15%)
  local copies, waits for them, and re-layouts  138 us (15%)
  starting transfers between devices  52.8 us (6%)
    all_to_all x5, waiting for transfers between devices, exchange(): return lax.all_to_all(x, 'four', split_axis=0, concat_axis=0, tiled=True)  333 us
    gather x1, local copies, waits for them, and re-layouts, inverse_mass(): return (1.0 / summed[ids]).reshape(mass.shape)  90.5 us
    scatter-add x1, other arithmetic, inverse_mass(): summed = jnp.zeros((UNIQUE,), jnp.float32).at[ids].add(mass.reshape(-1))  85.8 us
    pallas_call x2, Pallas kernels, forcing_modes(): pl.pallas_call(kernel, grid=(c_n, l_n), in_specs=[whole, whole, pl.BlockS...  50 us
    pallas_call x2, Pallas kernels, local_sums(): pl.pallas_call(kernel, grid=(nodes_n // step,), in_specs=[smem] * 4 + [pl...  44.1 us
    all_to_all x5, starting transfers between devices, exchange(): return lax.all_to_all(x, 'four', split_axis=0, concat_axis=0, tiled=True)  42.7 us
    pallas_call x4, Pallas kernels, derivative(): pl.pallas_call(kernel, grid=(c_n, m_n // rows), in_specs=[pl.BlockSpec(bl...  42.4 us
    pallas_call x2, Pallas kernels, spread(): pl.pallas_call(kernel, grid=(nodes_n // step,), in_specs=in_specs, out_sp...  33.4 us
  transfers between devices with their start and end apart: 11, of which 9 were waited for; matrix products, arithmetic and copies ran while one was open for 30% of the time, Pallas kernels for 21%

profile of v4, /device:TPU:9, one launch (start us, length us, event | category | flops | bytes accessed | tf_op | source)
XLA Modules:
  0.0 897.9 jit_solution(12942542990557902181)
XLA Ops:
  4.8 4.8 all-to-all-start
  9.7 13.9 %node_major.2.x_ref.u_ref = f32[4,3,16,64,256]{4,3,2,1,0:T(8,128)} custom-call(f32[3,64,64,256]{3,2,1,0:T(8,128)} %x_ref), custom_call_target="tpu_custom_call" | custom-call | flops 3145728 | bytes 25165824 | tf_op jit(solution)/shard_map/node_major/pallas_call | solution.py:90
  23.6 7.7 slice.53
  31.3 7.6 line_derivative.5
  38.9 13.6 %line_derivative.4 = f32[4,2,16,64,256]{4,3,2,1,0:T(8,128)} custom-call(f32[4,3,16,64,256]{4,3,2,1,0:T(8,128)} %node_major.2.x_ref.u_ref), custom_call_target="tpu_custom_call" | custom-call | flops 33554432 | bytes 16777216 | tf_op jit(solution)/shard_map/line_derivative/pallas_call | solution.py:119
  52.5 11.7 %pad_maximum_fusion = f32[4,4,16,64,256]{4,3,2,1,0:T(8,128)} fusion(f32[4,2,16,64,256]{4,3,2,1,0:T(8,128)} %line_derivative.4, f32[4,2,16,64,256]{4,3,2,1,0:T(8,128)} %slice.53), kind=kLoop, calls=%fused_computation.8 | loop fusion | flops 4194304 | bytes 33554432 | tf_op jit(solution)/shard_map/concatenate | solution.py:470
  64.1 34.8 %all-to-all-done.x_ref = f32[4,64,16,256]{3,2,1,0:T(8,128)} async-done(((f32[4,64,16,256]{3,2,1,0:T(8,128)}), f32[4,64,16,256]{3,2,1,0:T(8,128)}, u32[]{:S(2)}, u32[]{:S(2)}) %all-to-all-start) | async-done | bytes 4194336 | tf_op jit(solution)/shard_map/all_to_all | solution.py:445
  98.9 10.5 %all-to-all-start.1 = ((f32[4,4,16,64,256]{4,3,2,1,0:T(8,128)}), f32[4,4,16,64,256]{4,3,2,1,0:T(8,128)}, u32[]{:S(2)}, u32[]{:S(2)}) async-start(f32[4,4,16,64,256]{4,3,2,1,0:T(8,128)} %pad_maximum_fusion), calls=%async_computation.1 | async-start | bytes 33554432 | tf_op jit(solution)/shard_map/all_to_all | solution.py:445
  109.8 85.8 %scatter_custom_fusion = f32[12825]{0:T(1024)S(1)} fusion(s32[16384]{0:T(1024)S(1)} %bitcast.74, f32[16384]{0:T(1024)S(1)} %bitcast.78, f32[]{:T(128)} %constant.94.clone.1), kind=kCustom, calls=%fused_computation.43 | custom fusion | flops 16384 | bytes 51304 | tf_op jit(solution)/shard_map/scatter-add | solution.py:438
  202.5 7.1 sort.46
  214.2 19.5 %sort.47 = (s32[16408]{0:T(1024)}, s32[16408]{0:T(1024)S(1)}, s32[16408]{0:T(1024)S(1)}, s32[16408]{0:T(1024)}) sort(s32[16408]{0:T(1024)S(1)} %pad_add_fusion, s32[16408]{0:T(1024)S(1)} %concatenate.28, s32[16408]{0:T(1024)S(1)} %concatenate.29, s32[16408]{0:T(1024)S(1)} %iota.43), dimensions={0}, to_apply=%region_3.4 | sort | flops 246120 | bytes 525056 | tf_op jit(solution)/shard_map/sort | solution.py:409
  233.7 10.4 %node_major.3 = f32[1,4,16,64,256]{4,3,2,1,0:T(8,128)} custom-call(f32[4,64,16,256]{3,2,1,0:T(8,128)} %all-to-all-done.x_ref), custom_call_target="tpu_custom_call" | custom-call | flops 1048576 | bytes 8388608 | tf_op jit(solution)/shard_map/node_major/pallas_call | solution.py:90
  246.7 4.1 convert_reduce_fusion
  251.4 7.6 line_derivative.6.usa_ref
  263.5 23.3 %copy.31 = bf16[12,256,16,256]{3,1,2,0:T(8,128)(2,1)} copy(bf16[12,256,16,256]{3,2,1,0:T(8,128)(2,1)} %param.10) | data formatting | bytes 50331648 | tf_op jit(solution)/shard_map/optimization_barrier | solution.py:471
  290.2 90.5 %gather_fusion.3 = f32[16384]{0:T(1024)S(1)} fusion(f32[12825]{0:T(1024)S(1)} %scatter_fusion, s32[16384]{0:T(1024)S(1)} %broadcast_clamp_fusion), kind=kCustom, calls=%fused_computation.3 | custom fusion | bytes 196608 | tf_op jit(solution)/shard_map/gather | solution.py:441
  381.4 86.3 %all-to-all-done.1.x_ref.ub_ref.ur_ref = f32[4,4,16,64,256]{4,3,2,1,0:T(8,128)} async-done(((f32[4,4,16,64,256]{4,3,2,1,0:T(8,128)}), f32[4,4,16,64,256]{4,3,2,1,0:T(8,128)}, u32[]{:S(2)}, u32[]{:S(2)}) %all-to-all-start.1) | async-done | bytes 16777248 | tf_op jit(solution)/shard_map/all_to_all | solution.py:445
  467.7 8.9 all-to-all-start.2
  477.8 13.7 %line_derivative.7.usb_ref = f32[4,2,16,64,256]{4,3,2,1,0:T(8,128)} custom-call(f32[4,4,16,64,256]{4,3,2,1,0:T(8,128)} %all-to-all-done.1.x_ref.ub_ref.ur_ref), custom_call_target="tpu_custom_call" | custom-call | flops 33554432 | bytes 16777216 | tf_op jit(solution)/shard_map/line_derivative/pallas_call | solution.py:119
  491.6 30.6 %base_products.1 = (f32[16,256,256]{2,1,0:T(8,128)}, f32[3,16,256,256]{3,2,1,0:T(8,128)}) custom-call(bf16[512,768]{1,0:T(8,128)(2,1)} %constant.99.clone.both_ref, bf16[256,768]{1,0:T(8,128)(2,1)} %constant.100.clone.synth_ref, f32[4,1,16,64,256]{4,3,2,1,0:T(8,128)} %bitcast.68, f32[4,4,16,64,256]{4,3,2,1,0:T(8,128)} %all-to-all-done.1.x_ref.ub_ref.ur_ref, ...), custom_call_target="tpu_custom_call" | custom-call | flops 14495514624 | bytes 67108864 | tf_op jit(solution)/shard_map/base_products/pallas_call | solution.py:176
  522.1 32.8 %forcing_modes.2 = f32[4,2,16,64,256]{4,3,2,1,0:T(8,128)} custom-call(bf16[256,768]{1,0:T(8,128)(2,1)} %constant.100.clone.synth_ref, bf16[256,768]{1,0:T(8,128)(2,1)} %constant.101.clone.analysis_ref, f32[4,4,16,64,256]{4,3,2,1,0:T(8,128)} %all-to-all-done.1.x_ref.ub_ref.ur_ref, f32[16,256,256]{2,1,0:T(8,128)} %get-tuple-element.67.vr_ref, ...), custom_call_target="tpu_custom_call" | custom-call | flops 6442450944 | bytes 33554432 | tf_op jit(solution)/shard_map/forcing_modes/pallas_call | solution.py:218
  555.0 10.4 %all-to-all-done.2.ur_ref = f32[4,1,16,64,256]{4,3,2,1,0:T(8,128)} async-done(((f32[4,1,16,64,256]{4,3,2,1,0:T(8,128)}), f32[4,1,16,64,256]{4,3,2,1,0:T(8,128)}, u32[]{:S(2)}, u32[]{:S(2)}) %all-to-all-start.2) | async-done | bytes 4194336 | tf_op jit(solution)/shard_map/all_to_all | solution.py:445
  565.3 9.7 %all-to-all-start.3 = ((f32[4,2,16,64,256]{4,3,2,1,0:T(8,128)}), f32[4,2,16,64,256]{4,3,2,1,0:T(8,128)}, u32[]{:S(2)}, u32[]{:S(2)}) async-start(f32[4,2,16,64,256]{4,3,2,1,0:T(8,128)} %forcing_modes.2), calls=%async_computation.3 | async-start | bytes 16777216 | tf_op jit(solution)/shard_map/all_to_all | solution.py:445
  575.0 17.1 %forcing_modes.3 = f32[4,1,16,64,256]{4,3,2,1,0:T(8,128)} custom-call(bf16[256,768]{1,0:T(8,128)(2,1)} %constant.100.clone.synth_ref, bf16[256,768]{1,0:T(8,128)(2,1)} %constant.101.clone.analysis_ref, f32[4,1,16,64,256]{4,3,2,1,0:T(8,128)} %all-to-all-done.2.ur_ref, f32[16,256,256]{2,1,0:T(8,128)} %get-tuple-element.67.vr_ref, ...), custom_call_target="tpu_custom_call" | custom-call | flops 3221225472 | bytes 16777216 | tf_op jit(solution)/shard_map/forcing_modes/pallas_call | solution.py:218
  592.1 161.5 %all-to-all-done.3.f_ref = f32[4,2,16,64,256]{4,3,2,1,0:T(8,128)} async-done(((f32[4,2,16,64,256]{4,3,2,1,0:T(8,128)}), f32[4,2,16,64,256]{4,3,2,1,0:T(8,128)}, u32[]{:S(2)}, u32[]{:S(2)}) %all-to-all-start.3) | async-done | bytes 8388640 | tf_op jit(solution)/shard_map/all_to_all | solution.py:445
  753.6 8.8 all-to-all-start.4
  762.4 22.9 %local_sums.2 = (f32[16392,128]{1,0:T(8,128)}, f32[232,128]{1,0:T(8,128)}, f32[232,128]{1,0:T(8,128)}) custom-call(s32[3584]{0:T(1024)} %get-tuple-element.59.mem, s32[3584]{0:T(1024)} %get-tuple-element.60.rep, s32[8]{0:T(128)} %reshape.294.bnd, s32[2,232]{1,0:T(2,128)} %pad.15.er, f32[4,2,16,64,256]{4,3,2,1,0:T(8,128)} %all-to-all-done.3.f_ref, ...), custom_call_target="tpu_custom_call" | custom-call | flops 838860800 | bytes 25165824 | tf_op jit(solution)/shard_map/local_sums/pallas_call | solution.py:299
  794.4 17.2 %spread.2.rest_0_ = f32[3,64,64,256]{3,2,1,0:T(8,128)} custom-call(s32[3584]{0:T(1024)} %get-tuple-element.59.mem, s32[3584]{0:T(1024)} %get-tuple-element.60.rep, s32[2,232]{1,0:T(2,128)} %pad.15.er, f32[16392,128]{1,0:T(8,128)} %get-tuple-element.75.t_ref, f32[232,128]{1,0:T(8,128)} %copy-done.6, f32[232,128]{1,0:T(8,128)} %copy-done.7, f32[64,256]{1,0:T(8,128)} %div.50.inv_ref), custom_call_target="tpu_custom_call" | custom-call | flops 838860800 | bytes 25165824 | tf_op jit(solution)/shard_map/spread/pallas_call | solution.py:376
  811.6 39.6 %all-to-all-done.4.f_ref = f32[4,1,16,64,256]{4,3,2,1,0:T(8,128)} async-done(((f32[4,1,16,64,256]{4,3,2,1,0:T(8,128)}), f32[4,1,16,64,256]{4,3,2,1,0:T(8,128)}, u32[]{:S(2)}, u32[]{:S(2)}) %all-to-all-start.4) | async-done | bytes 4194336 | tf_op jit(solution)/shard_map/all_to_all | solution.py:445
  851.2 21.2 %local_sums.3 = (f32[16392,64]{1,0:T(8,128)}, f32[232,64]{1,0:T(8,128)}, f32[232,64]{1,0:T(8,128)}) custom-call(s32[3584]{0:T(1024)} %get-tuple-element.59.mem, s32[3584]{0:T(1024)} %get-tuple-element.60.rep, s32[8]{0:T(128)} %reshape.294.bnd, s32[2,232]{1,0:T(2,128)} %pad.15.er, f32[4,1,16,64,256]{4,3,2,1,0:T(8,128)} %all-to-all-done.4.f_ref, ...), custom_call_target="tpu_custom_call" | custom-call | flops 838860800 | bytes 25165824 | tf_op jit(solution)/shard_map/local_sums/pallas_call | solution.py:299
  872.4 3.7 collective-permute-start.4
  881.7 16.2 %spread.3 = f32[3,64,64,256]{3,2,1,0:T(8,128)} custom-call(s32[3584]{0:T(1024)} %get-tuple-element.59.mem, s32[3584]{0:T(1024)} %get-tuple-element.60.rep, s32[2,232]{1,0:T(2,128)} %pad.15.er, f32[16392,64]{1,0:T(8,128)} %get-tuple-element.80.t_ref, f32[232,64]{1,0:T(8,128)} %copy-done.4, f32[232,64]{1,0:T(8,128)} %copy-done.5, ...), custom_call_target="tpu_custom_call", output_to_operand_aliasing={{}: (7, {})} | custom-call | flops 838860800 | bytes 25165824 | tf_op jit(solution)/shard_map/spread/pallas_call | solution.py:376
  (83 shorter events, 44.1 us)
Async XLA Ops:
  0.0 476.6 %copy-start = (f32[4,64,256]{2,1,0:T(8,128)S(1)}, f32[4,64,256]{2,1,0:T(8,128)}, u32[]{:S(2)}) copy-start(f32[4,64,256]{2,1,0:T(8,128)} %param.11) | copy-start | bytes 786436
  0.0 2.3 slice-start
  4.8 94.1 %all-to-all-start = ((f32[4,64,16,256]{3,2,1,0:T(8,128)}), f32[4,64,16,256]{3,2,1,0:T(8,128)}, u32[]{:S(2)}, u32[]{:S(2)}) async-start(f32[4,64,16,256]{3,2,1,0:T(8,128)} %bitcast.70), calls=%async_computation | async-start | bytes 8388608 | tf_op jit(solution)/shard_map/all_to_all | solution.py:445
  64.1 45.3 %copy-start.8 = (s32[1,2,225]{2,1,0:T(2,128)S(1)}, s32[1,2,225]{2,1,0:T(2,128)}, u32[]{:S(2)}) copy-start(s32[1,2,225]{2,1,0:T(2,128)} %param.14) | copy-start | bytes 5404
  64.1 45.5 %copy-start.2 = (f32[64,256]{1,0:T(8,128)S(1)}, f32[64,256]{1,0:T(8,128)}, u32[]{:S(2)}) copy-start(f32[64,256]{1,0:T(8,128)} %mass_ref.1) | copy-start | bytes 196612
  64.1 45.5 %copy-start.3 = (s32[64,256]{1,0:T(8,128)S(1)}, s32[64,256]{1,0:T(8,128)}, u32[]{:S(2)}) copy-start(s32[64,256]{1,0:T(8,128)} %param.13) | copy-start | bytes 196612
  98.9 368.8 %all-to-all-start.1 = ((f32[4,4,16,64,256]{4,3,2,1,0:T(8,128)}), f32[4,4,16,64,256]{4,3,2,1,0:T(8,128)}, u32[]{:S(2)}, u32[]{:S(2)}) async-start(f32[4,4,16,64,256]{4,3,2,1,0:T(8,128)} %pad_maximum_fusion), calls=%async_computation.1 | async-start | bytes 33554432 | tf_op jit(solution)/shard_map/all_to_all | solution.py:445
  109.4 141.4 %copy-start.9 = (pred[3584]{0:T(1024)(128)(4,1)S(1)}, pred[3584]{0:T(1024)(128)(4,1)}, u32[]{:S(2)}) copy-start(pred[3584]{0:T(1024)(128)(4,1)} %constant.77.clone.1) | copy-start | bytes 10756
  197.4 89.5 %collective-permute-start = (f32[225]{0:T(256)S(1)}, f32[225]{0:T(256)S(1)}, u32[]{:S(2)}, u32[]{:S(2)}) collective-permute-start(f32[225]{0:T(256)S(1)} %gather_fusion.1), channel_id=1, source_target_pairs={{0,4},{4,8},{8,12},{12,16},{16,20},{20,24},{24,28},{28,0},{1,5},{5... | collective-permute-start | bytes 2708 | tf_op jit(solution)/shard_map/ppermute | solution.py:434
  202.2 84.7 %collective-permute-start.1 = (f32[225]{0:T(256)S(1)}, f32[225]{0:T(256)S(1)}, u32[]{:S(2)}, u32[]{:S(2)}) collective-permute-start(f32[225]{0:T(256)S(1)} %gather_fusion.2), channel_id=1, source_target_pairs={{4,0},{8,4},{12,8},{16,12},{20,16},{24,20},{28,24},{0,28},{5,1},{9... | collective-permute-start | bytes 2708 | tf_op jit(solution)/shard_map/ppermute | solution.py:434
  467.7 97.6 %all-to-all-start.2 = ((f32[4,1,16,64,256]{4,3,2,1,0:T(8,128)}), f32[4,1,16,64,256]{4,3,2,1,0:T(8,128)}, u32[]{:S(2)}, u32[]{:S(2)}) async-start(f32[4,1,16,64,256]{4,3,2,1,0:T(8,128)} %line_derivative.5), calls=%async_computation.2 | async-start | bytes 8388608 | tf_op jit(solution)/shard_map/all_to_all | solution.py:445
  565.3 188.3 %all-to-all-start.3 = ((f32[4,2,16,64,256]{4,3,2,1,0:T(8,128)}), f32[4,2,16,64,256]{4,3,2,1,0:T(8,128)}, u32[]{:S(2)}, u32[]{:S(2)}) async-start(f32[4,2,16,64,256]{4,3,2,1,0:T(8,128)} %forcing_modes.2), calls=%async_computation.3 | async-start | bytes 16777216 | tf_op jit(solution)/shard_map/all_to_all | solution.py:445
  753.6 97.6 %all-to-all-start.4 = ((f32[4,1,16,64,256]{4,3,2,1,0:T(8,128)}), f32[4,1,16,64,256]{4,3,2,1,0:T(8,128)}, u32[]{:S(2)}, u32[]{:S(2)}) async-start(f32[4,1,16,64,256]{4,3,2,1,0:T(8,128)} %forcing_modes.3), calls=%async_computation.4 | async-start | bytes 8388608 | tf_op jit(solution)/shard_map/all_to_all | solution.py:445
  785.3 5.2 collective-permute-start.2
  788.4 5.3 collective-permute-start.3
  790.6 3.2 copy-start.6
  793.7 0.7 copy-start.7
  872.4 5.9 collective-permute-start.4
  876.1 4.9 collective-permute-start.5
  878.3 2.8 copy-start.4
  881.0 0.7 copy-start.5
  881.7 16.2 %copy-start.1 = (f32[4,64,256]{2,1,0:T(8,128)S(1)}, f32[4,64,256]{2,1,0:T(8,128)}, u32[]{:S(2)}) copy-start(f32[4,64,256]{2,1,0:T(8,128)} %param.11) | copy-start | bytes 786436

commit v5 on v4

--- a/solution.py
+++ b/solution.py
@@ -14,8 +14,8 @@
 UNIQUE = 12825
 STEP_SIZE = 0.1
 LANES = 128
-BATCH = 8
-RANKS = 3
+BATCH = 16
+CLASSES = 4
 VMEM_LIMIT = 56 * 1024 * 1024
 
 
@@ -238,6 +238,210 @@
     )(synth, analysis, ur, vr, part, mass)
 
 
+def forcing_and_rims(synth, analysis, ur, u, vr, part, mass, connect, edge_ids, c, u_at):
+    s_n, _, l_n, m_n, e_n = ur.shape
+    p_n = vr.shape[1]
+    k_n = edge_ids.shape[0]
+
+    def kernel(synth_ref, analysis_ref, ur_ref, u_ref, vr_ref, part_ref, mass_ref, conn_ref, id_ref, o_ref, rim_ref):
+        l = pl.program_id(0)
+        dr = product(synth_ref[...], right_form(ur_ref[:, 0, 0].reshape(s_n * m_n, e_n)))
+        forcing = part_ref[0, 0] - vr_ref[0] * dr
+        weight = mass_ref[pl.ds(l, 1), :]
+        modes = product(analysis_ref[...], right_form(forcing)) * (STEP_SIZE * weight)
+        o_ref[:, 0, 0] = modes.reshape(s_n, m_n, e_n)
+        high, low = split(modes + weight * u_ref[:, 0, 0].reshape(s_n * m_n, e_n))
+        here = jnp.where(id_ref[...] == conn_ref[pl.ds(l, 1), :], 1.0, 0.0).astype(jnp.bfloat16)
+        sums = lax.dot_general(
+            jnp.concatenate([here, here], axis=1),
+            jnp.concatenate([high, low], axis=1),
+            (((1,), (1,)), ((), ())),
+            preferred_element_type=jnp.float32,
+        )
+
+        @pl.when(l == 0)
+        def _():
+            rim_ref[...] = sums
+
+        @pl.when(l > 0)
+        def _():
+            rim_ref[...] += sums
+
+    whole = pl.BlockSpec((p_n, 3 * p_n), lambda l: (0, 0))
+    block = (s_n, 1, 1, m_n, e_n)
+    nodes = pl.BlockSpec((l_n, e_n), lambda l: (0, 0))
+    return pl.pallas_call(
+        kernel,
+        grid=(l_n,),
+        in_specs=[
+            whole,
+            whole,
+            pl.BlockSpec(block, lambda l: (0, 0, l, 0, 0)),
+            pl.BlockSpec(block, lambda l: (0, u_at, l, 0, 0)),
+            pl.BlockSpec((1, p_n, e_n), lambda l: (l, 0, 0)),
+            pl.BlockSpec((1, 1, p_n, e_n), lambda l: (c, l, 0, 0)),
+            nodes,
+            nodes,
+            pl.BlockSpec((k_n, 1), lambda l: (0, 0)),
+        ],
+        out_specs=[
+            pl.BlockSpec(block, lambda l: (0, 0, l, 0, 0)),
+            pl.BlockSpec((k_n, s_n * m_n), lambda l: (0, 0)),
+        ],
+        out_shape=[
+            jax.ShapeDtypeStruct((s_n, 1, l_n, m_n, e_n), jnp.float32),
+            jax.ShapeDtypeStruct((k_n, s_n * m_n), jnp.float32),
+        ],
+        compiler_params=params(),
+        cost_estimate=pl.CostEstimate(
+            flops=4 * 2 * 3 * l_n * p_n * p_n * e_n, bytes_accessed=l_n * p_n * e_n * 20, transcendentals=0
+        ),
+        name="forcing_and_rims",
+    )(synth, analysis, ur, u, vr, part, mass, connect, edge_ids)
+
+
+def take_rims(modes, rims, takers):
+    s_n, _, l_n, m_n, e_n = modes.shape
+    k_n = takers.shape[0]
+
+    def kernel(f_ref, rim_ref, to_ref, o_ref):
+        l = pl.program_id(0)
+        column = l * e_n + lax.broadcasted_iota(jnp.int32, (1, e_n), 1)
+        there = jnp.where(to_ref[...] == column, 1.0, 0.0).astype(jnp.bfloat16)
+        high, low = split(rim_ref[...])
+        add = product(jnp.concatenate([high, low], axis=1), jnp.concatenate([there, there], axis=0))
+        o_ref[:, 0, 0] = f_ref[:, 0, 0] + add.reshape(s_n, m_n, e_n)
+
+    block = pl.BlockSpec((s_n, 1, 1, m_n, e_n), lambda l: (0, 0, l, 0, 0))
+    return pl.pallas_call(
+        kernel,
+        grid=(l_n,),
+        in_specs=[
+            block,
+            pl.BlockSpec((s_n * m_n, k_n), lambda l: (0, 0)),
+            pl.BlockSpec((k_n, 1), lambda l: (0, 0)),
+        ],
+        out_specs=block,
+        out_shape=jax.ShapeDtypeStruct(modes.shape, jnp.float32),
+        input_output_aliases={0: 0},
+        compiler_params=params(),
+        cost_estimate=pl.CostEstimate(
+            flops=4 * l_n * s_n * m_n * k_n * e_n, bytes_accessed=8 * modes.size, transcendentals=0
+        ),
+        name="take_rims",
+    )(modes, rims, takers)
+
+
+def rows_of(ref, places):
+    return [ref[pl.ds(r, 1), :] for r in places]
+
+
+def put_rows(ref, places, rows):
+    for r, row in zip(places, rows):
+        ref[pl.ds(r, 1), :] = row
+
+
+def sum_class(ref, mem, rep, start, number, both):
+    def batch(i, _):
+        at = start + i * BATCH
+        heads = [rep[at + t] for t in range(BATCH)]
+        others = [mem[at + t] for t in range(BATCH)]
+        sums = [a + b for a, b in zip(rows_of(ref, heads), rows_of(ref, others))]
+        put_rows(ref, heads, sums)
+        if both:
+            put_rows(ref, others, sums)
+        return 0
+
+    lax.fori_loop(0, pl.cdiv(number, BATCH), batch, 0)
+
+
+def sum_rest(ref, mem, rep, start, number):
+    def one(i, _):
+        r = rep[start + i]
+        ref[pl.ds(r, 1), :] = ref[pl.ds(r, 1), :] + ref[pl.ds(mem[start + i], 1), :]
+        return 0
+
+    lax.fori_loop(0, number, one, 0)
+
+
+def hand_back(ref, mem, rep, start, end):
+    def batch(i, _):
+        at = start + i * BATCH
+        put_rows(ref, [mem[at + t] for t in range(BATCH)], rows_of(ref, [rep[at + t] for t in range(BATCH)]))
+        return 0
+
+    lax.fori_loop(0, pl.cdiv(end - start, BATCH), batch, 0)
+
+
+def finish(modes, u, mass, pairs, inverse, held, shape, c):
+    s_n, _, l_n, m_n, e_n = modes.shape
+    _, _, nodes_n, _ = shape
+    rows_n = nodes_n * e_n
+    members, reps, bounds = pairs
+    step = min(8, l_n)
+    per = l_n // step
+    fills = nodes_n // step
+    outs = nodes_n // 8
+
+    def kernel(mem, rep, bnd, f_ref, u_ref, mass_ref, inv_ref, _, o_ref, table, stage):
+        b = pl.program_id(0)
+
+        @pl.when(b < fills)
+        def _():
+            for t in range(step):
+                node = b * step + t
+                rows = f_ref[0, 0, t] + mass_ref[pl.ds(node, 1), :] * u_ref[0, 0, t]
+                table[pl.ds(pl.multiple_of(node * e_n, e_n), e_n), :] = rows.T
+
+        @pl.when(b == fills - 1)
+        def _():
+            table[pl.ds(rows_n, 8), :] = jnp.zeros((8, m_n), jnp.float32)
+            for k in range(CLASSES):
+                sum_class(table, mem, rep, bnd[2 * k], bnd[2 * k + 1], k == 0)
+            sum_rest(table, mem, rep, bnd[2 * CLASSES], bnd[2 * CLASSES + 1])
+            hand_back(table, mem, rep, bnd[2], bnd[2 * CLASSES] + bnd[2 * CLASSES + 1])
+
+        @pl.when(b >= fills)
+        def _():
+            for t in range(8):
+                n = (b - fills) * 8 + t
+                rows = table[pl.ds(pl.multiple_of(n * e_n, e_n), e_n), :].T
+                stage[t] = rows * inv_ref[pl.ds(n, 1), :]
+            o_ref[0] = jnp.swapaxes(stage[...], 0, 1)
+
+    smem = pl.BlockSpec(memory_space=pltpu.SMEM)
+
+    def where(channel):
+        def index(b):
+            b = jnp.minimum(b, fills - 1)
+            return (b // per, channel, b % per, 0, 0)
+
+        return index
+
+    nodes = pl.BlockSpec((nodes_n, e_n), lambda b: (0, 0))
+    return pl.pallas_call(
+        kernel,
+        grid=(fills + outs,),
+        in_specs=[smem] * 3
+        + [
+            pl.BlockSpec((1, 1, step, m_n, e_n), where(0)),
+            pl.BlockSpec((1, 1, step, m_n, e_n), where(c)),
+            nodes,
+            nodes,
+            pl.BlockSpec(memory_space=pl.ANY),
+        ],
+        out_specs=pl.BlockSpec((1, m_n, 8, e_n), lambda b: (c, 0, jnp.maximum(b - fills, 0), 0)),
+        out_shape=jax.ShapeDtypeStruct(shape, jnp.float32),
+        scratch_shapes=[pltpu.VMEM((rows_n + 8, m_n), jnp.float32), pltpu.VMEM((8, m_n, e_n), jnp.float32)],
+        input_output_aliases={7: 0},
+        compiler_params=params(),
+        cost_estimate=pl.CostEstimate(
+            flops=rows_n * LANES * 400, bytes_accessed=rows_n * m_n * 12, transcendentals=0
+        ),
+        name="finish",
+    )(members, reps, bounds, modes, u, mass, inverse, held)
+
+
 def local_sums(modes, u, mass, pairs, edge_reps, first):
     s_n, c_n, l_n, m_n, e_n = modes.shape
     nodes_n = s_n * l_n
@@ -261,32 +465,14 @@
         def _():
             o_ref[pl.ds(rows_n, 8), :] = jnp.zeros((8, feats), jnp.float32)
 
-            for rank in range(RANKS):
-
-                def close(i, _):
-                    at = bnd[2 * rank] + i * BATCH
-                    heads = [rep[at + t] for t in range(BATCH)]
-                    others = [mem[at + t] for t in range(BATCH)]
-                    sums = [o_ref[pl.ds(r, 1), :] + o_ref[pl.ds(k, 1), :] for r, k in zip(heads, others)]
-                    for r, total in zip(heads, sums):
-                        o_ref[pl.ds(r, 1), :] = total
-                    return 0
-
-                lax.fori_loop(0, pl.cdiv(bnd[2 * rank + 1], BATCH), close, 0)
-
-            def far(i, _):
-                at = bnd[2 * RANKS] + i
-                r = rep[at]
-                o_ref[pl.ds(r, 1), :] = o_ref[pl.ds(r, 1), :] + o_ref[pl.ds(mem[at], 1), :]
-                return 0
-
-            lax.fori_loop(0, bnd[2 * RANKS + 1], far, 0)
+            for k in range(CLASSES):
+                sum_class(o_ref, mem, rep, bnd[2 * k], bnd[2 * k + 1], False)
+            sum_rest(o_ref, mem, rep, bnd[2 * CLASSES], bnd[2 * CLASSES + 1])
 
             def edge(i, _):
                 for side, to in enumerate((low_ref, up_ref)):
-                    got = [o_ref[pl.ds(er[side, i * BATCH + t], 1), :] for t in range(BATCH)]
-                    for t, row in enumerate(got):
-                        to[pl.ds(i * BATCH + t, 1), :] = row
+                    got = rows_of(o_ref, [er[side, i * BATCH + t] for t in range(BATCH)])
+                    put_rows(to, [i * BATCH + t for t in range(BATCH)], got)
                 return 0
 
             lax.fori_loop(0, edges_n // BATCH, edge, 0)
@@ -320,11 +506,10 @@
     rows_n = nodes_n * e_n
     step = 8
     edges_n = edge_reps.shape[1]
-    members, reps, _ = pairs
-    pairs_n = members.shape[0]
+    members, reps, bounds = pairs
     feats = c_n * m_n
 
-    def kernel(mem, rep, er, t_ref, low_ref, up_ref, inv_ref, *rest):
+    def kernel(mem, rep, bnd, er, t_ref, low_ref, up_ref, inv_ref, *rest):
         o_ref, stage = rest[-2:]
         b = pl.program_id(0)
 
@@ -333,22 +518,12 @@
             def edge(i, _):
                 for side, came in enumerate((low_ref, up_ref)):
                     spots = [er[side, i * BATCH + t] for t in range(BATCH)]
-                    sums = [
-                        t_ref[pl.ds(r, 1), :] + came[pl.ds(i * BATCH + t, 1), :] for t, r in enumerate(spots)
-                    ]
-                    for r, total in zip(spots, sums):
-                        t_ref[pl.ds(r, 1), :] = total
+                    more = rows_of(came, [i * BATCH + t for t in range(BATCH)])
+                    put_rows(t_ref, spots, [a + b for a, b in zip(rows_of(t_ref, spots), more)])
                 return 0
 
             lax.fori_loop(0, edges_n // BATCH, edge, 0)
-
-            def back(i, _):
-                got = [t_ref[pl.ds(rep[i * BATCH + t], 1), :] for t in range(BATCH)]
-                for t, row in enumerate(got):
-                    t_ref[pl.ds(mem[i * BATCH + t], 1), :] = row
-                return 0
-
-            lax.fori_loop(0, pairs_n // BATCH, back, 0)
+            hand_back(t_ref, mem, rep, 0, bnd[2 * CLASSES] + bnd[2 * CLASSES + 1])
 
         for t in range(step):
             n = b * step + t
@@ -361,13 +536,13 @@
 
     smem = pl.BlockSpec(memory_space=pltpu.SMEM)
     rim = pl.BlockSpec((edges_n, feats), lambda b: (0, 0))
-    in_specs = [smem] * 3 + [
+    in_specs = [smem] * 4 + [
         pl.BlockSpec((rows_n + 8, feats), lambda b: (0, 0)),
         rim,
         rim,
         pl.BlockSpec((nodes_n, e_n), lambda b: (0, 0)),
     ]
-    args = [members, reps, edge_reps, table, *rims, inverse]
+    args = [members, reps, bounds, edge_reps, table, *rims, inverse]
     aliases = {}
     if held is not None:
         in_specs.append(pl.BlockSpec(memory_space=pl.ANY))
@@ -400,12 +575,14 @@
     place = jnp.arange(rows_n, dtype=jnp.int32)
     ids_sorted, member = lax.sort((ids, place), num_keys=1)
     head = jnp.concatenate([jnp.ones((1,), bool), ids_sorted[1:] != ids_sorted[:-1]])
+    last = jnp.concatenate([head[1:], jnp.ones((1,), bool)])
     code = lax.cummax(jnp.where(head, place * rows_n + member, 0))
     rep = code % rows_n
     rank = place - code // rows_n
-    group = jnp.where(rank == 0, RANKS + 2, jnp.minimum(rank, RANKS + 1)).astype(jnp.int32)
-    spare = jnp.full((RANKS * BATCH,), rows_n, jnp.int32)
-    spare_group = jnp.arange(RANKS * BATCH, dtype=jnp.int32) // BATCH + 1
+    group = jnp.where((rank == 1) & last, 0, jnp.minimum(rank, CLASSES))
+    group = jnp.where(rank == 0, CLASSES + 1, group).astype(jnp.int32)
+    spare = jnp.full((CLASSES * BATCH,), rows_n, jnp.int32)
+    spare_group = jnp.arange(CLASSES * BATCH, dtype=jnp.int32) // BATCH
     _, members, reps = lax.sort(
         (
             jnp.concatenate([group, spare_group]),
@@ -415,16 +592,33 @@
         num_keys=1,
         is_stable=True,
     )
-    pairs_n = rows_n - UNIQUE + RANKS * BATCH
-    numbers = jnp.stack([jnp.sum(group == r, dtype=jnp.int32) for r in range(1, RANKS + 2)])
-    starts = jnp.cumsum(numbers) - numbers + BATCH * jnp.arange(RANKS + 1, dtype=jnp.int32)
+    pairs_n = rows_n - UNIQUE + CLASSES * BATCH
+    numbers = jnp.stack([jnp.sum(group == k, dtype=jnp.int32) for k in range(CLASSES + 1)])
+    starts = jnp.cumsum(numbers) - numbers + BATCH * jnp.arange(CLASSES + 1, dtype=jnp.int32)
     bounds = jnp.stack([starts, numbers], axis=1).reshape(-1).astype(jnp.int32)
-    members = fill_up(members[:pairs_n], BATCH, rows_n)
-    reps = fill_up(reps[:pairs_n], BATCH, rows_n)
+    more = BATCH + -pairs_n % BATCH
+    members = jnp.pad(members[:pairs_n], (0, more), constant_values=rows_n)
+    reps = jnp.pad(reps[:pairs_n], (0, more), constant_values=rows_n)
     flat = edges.reshape(-1)
     start = jnp.sum(ids_sorted[None, :] < flat[:, None], axis=1, dtype=jnp.int32)
     edge_reps = fill_up(member[start].reshape(edges.shape), BATCH, rows_n)
     return (members, reps, bounds), edge_reps
+
+
+def edge_takers(edges, connect_here, edge_reps):
+    k_n = edge_reps.shape[1]
+    here_n = connect_here.size
+    ids = fill_up(edges, BATCH, -1)
+    column = jnp.arange(here_n, dtype=jnp.int32)
+    same = ids[:, :, None] == connect_here.reshape(-1)
+    first = jnp.min(jnp.where(same, column, here_n), axis=2)
+    has = (first < here_n).astype(jnp.float32)
+    theirs = jnp.stack(swap_edges(has[0], has[1]))
+    lost = jnp.max(theirs * (1.0 - has))
+    spread_out = lax.pmax(lost, ("mesh", "four")) > 0.5
+    at_rep = jnp.where(edge_reps // here_n == lax.axis_index("four"), edge_reps % here_n, -1)
+    takers = jnp.where(spread_out, at_rep, jnp.where(first < here_n, first, -1))
+    return ids.reshape(2 * k_n, 1), takers.reshape(2 * k_n, 1).astype(jnp.int32), spread_out
 
 
 def swap_edges(low, up):
@@ -483,21 +677,29 @@
     else:
         u0_here = first_here.transpose(0, 2, 1, 3)[:, None]
     us0_here = derivative(u0_here, inside, 0, 1) if whole_rows else None
-    held = (here, ur_b, pairs, edge_reps, inverse, base, u0_here, us0_here)
-    here, ur_b, pairs, edge_reps, inverse, base, u0_here, us0_here = together(held)
+    mass_here = lax.dynamic_slice_in_dim(mass, mine, l_n, 0)
+    connect_here = lax.dynamic_slice_in_dim(connect, mine, l_n, 0)
+    edge_ids, takers, spread_out = edge_takers(edges, connect_here, edge_reps)
+    held = (here, ur_b, pairs, edge_reps, inverse, base, u0_here, us0_here, edge_ids, takers, spread_out)
+    here, ur_b, pairs, edge_reps, inverse, base, u0_here, us0_here, edge_ids, takers, spread_out = together(held)
 
     ur_b_here = exchange(ur_b)
     us_here = derivative(here, inside, 0, 2) if whole_rows else here[:, 5:7]
     if not whole_rows:
         us0_here = here[:, 4:5]
     geo = lax.dynamic_slice_in_dim(geometry, mine, l_n, 1)
-    mass_here = lax.dynamic_slice_in_dim(mass, mine, l_n, 0)
     vr, part = base_products(both_3, synth_3, u0_here, here, us0_here, us_here, base, geo)
     f_a = forcing_modes(synth_3, analysis_3, here, vr, part, mass_here, 2, 0, 2)
     f_a, ur_b_here = together((f_a, ur_b_here))
 
     modes_a = exchange(f_a)
-    f_b = forcing_modes(synth_3, analysis_3, ur_b_here, vr, part, mass_here, 0, 2, 1)
+    f_b, rims = forcing_and_rims(
+        synth_3, analysis_3, ur_b_here, here, vr, part, mass_here, connect_here, edge_ids, 2, 1
+    )
+    half = rims.shape[0] // 2
+    rims = jnp.concatenate(swap_edges(rims[:half], rims[half:]))
+    rims = lax.cond(spread_out, lambda r: lax.psum(r, "four"), lambda r: r, rims)
+    f_b = take_rims(f_b, rims.T, takers)
     f_b, modes_a = together((f_b, modes_a))
 
     modes_b = exchange(f_b)
@@ -505,8 +707,7 @@
     out = spread(table, swap_edges(*rims), pairs, edge_reps, inverse, None, adj_modes.shape, 0, 2)
     modes_b, out = together((modes_b, out))
 
-    table, *rims = local_sums(modes_b, u, mass, pairs, edge_reps, 2)
-    return spread(table, swap_edges(*rims), pairs, edge_reps, inverse, out, adj_modes.shape, 2, 1)
+    return finish(modes_b, u, mass, pairs, inverse, out, adj_modes.shape, 2)
 
 
 def solution(mesh):

time: 905 us -> 930 us (1.028)
  waiting for transfers between devices: 343 us -> 220 us
  blocking collectives: 0 us -> 104 us
  between operations: 0.29 us -> 14.7 us
  Pallas kernels: 225 us -> 238 us
  local copies, waits for them, and re-layouts: 138 us -> 149 us
    all_to_all x5, waiting for transfers between devices: 333 us -> 208 us  [exchange(): return lax.all_to_all(x, 'four', split_axis=0, concat_axis=0, tiled=True)]
    pmax x0 -> x1, blocking collectives: none -> 104 us  [edge_takers(): spread_out = lax.pmax(lost, ('mesh', 'four')) > 0.5]
    pallas_call x0 -> x3, Pallas kernels: none -> 61.6 us  [the longest x1 27.7 us: finish(): pl.pallas_call(kernel, grid=(fills + outs,), in_specs=[smem] * 3 + [pl.Bl...]
    pallas_call x2 -> x1, Pallas kernels: 44.1 us -> 25.9 us  [local_sums(): pl.pallas_call(kernel, grid=(nodes_n // step,), in_specs=[smem] * 4 + [pl...]
    pallas_call x2 -> x1, Pallas kernels: 50 us -> 32.8 us  [forcing_modes(): pl.pallas_call(kernel, grid=(c_n, l_n), in_specs=[whole, whole, pl.BlockS...]
    pallas_call x2 -> x1, Pallas kernels: 33.4 us -> 20 us  [spread(): pl.pallas_call(kernel, grid=(nodes_n // step,), in_specs=in_specs, out_sp...]
  transfers between devices with their start and end apart: 11 -> 13, of which waited for: 9 -> 8; matrix products, arithmetic and copies ran while one was open for 30% -> 31% of each run, Pallas kernels for 21% -> 23%
where the time goes in v5:
time: 930 us; the launch traced here: 914 us
  Pallas kernels  238 us (26%)
  waiting for transfers between devices  220 us (24%)
  local copies, waits for them, and re-layouts  149 us (16%)
  other arithmetic  137 us (15%)
  blocking collectives  104 us (11%)
  starting transfers between devices  51.3 us (6%)
  between operations  14.7 us (2%)
    all_to_all x5, waiting for transfers between devices, exchange(): return lax.all_to_all(x, 'four', split_axis=0, concat_axis=0, tiled=True)  208 us
    pmax x1, blocking collectives, edge_takers(): spread_out = lax.pmax(lost, ('mesh', 'four')) > 0.5  104 us
    gather x1, local copies, waits for them, and re-layouts, inverse_mass(): return (1.0 / summed[ids]).reshape(mass.shape)  90.5 us
    scatter-add x1, other arithmetic, inverse_mass(): summed = jnp.zeros((UNIQUE,), jnp.float32).at[ids].add(mass.reshape(-1))  85.8 us
    pallas_call x4, Pallas kernels, derivative(): pl.pallas_call(kernel, grid=(c_n, m_n // rows), in_specs=[pl.BlockSpec(bl...  42.4 us
    all_to_all x5, starting transfers between devices, exchange(): return lax.all_to_all(x, 'four', split_axis=0, concat_axis=0, tiled=True)  40.2 us
    pallas_call x1, Pallas kernels, forcing_modes(): pl.pallas_call(kernel, grid=(c_n, l_n), in_specs=[whole, whole, pl.BlockS...  32.8 us
    pallas_call x1, Pallas kernels, base_products(): pl.pallas_call(kernel, grid=(l_n,), in_specs=[pl.BlockSpec((2 * p_n, 3 *...  30.6 us
  transfers between devices with their start and end apart: 13, of which 8 were waited for; matrix products, arithmetic and copies ran while one was open for 31% of the time, Pallas kernels for 23%

profile of v5, /device:TPU:9, one launch (start us, length us, event | category | flops | bytes accessed | tf_op | source)
XLA Modules:
  0.0 914.4 jit_solution(8754227055842802310)
XLA Ops:
  11.4 4.8 all-to-all-start
  16.2 13.9 %node_major.2.x_ref.u_ref = f32[4,3,16,64,256]{4,3,2,1,0:T(8,128)} custom-call(f32[3,64,64,256]{3,2,1,0:T(8,128)} %x_ref), custom_call_target="tpu_custom_call" | custom-call | flops 3145728 | bytes 25165824 | tf_op jit(solution)/shard_map/node_major/pallas_call | solution.py:90
  30.1 7.7 slice.69
  37.8 7.6 line_derivative.5
  45.4 13.6 %line_derivative.4 = f32[4,2,16,64,256]{4,3,2,1,0:T(8,128)} custom-call(f32[4,3,16,64,256]{4,3,2,1,0:T(8,128)} %node_major.2.x_ref.u_ref), custom_call_target="tpu_custom_call" | custom-call | flops 33554432 | bytes 16777216 | tf_op jit(solution)/shard_map/line_derivative/pallas_call | solution.py:119
  59.0 11.7 %pad_maximum_fusion = f32[4,4,16,64,256]{4,3,2,1,0:T(8,128)} fusion(f32[4,2,16,64,256]{4,3,2,1,0:T(8,128)} %line_derivative.4, f32[4,2,16,64,256]{4,3,2,1,0:T(8,128)} %slice.69), kind=kLoop, calls=%fused_computation.8 | loop fusion | flops 4194304 | bytes 33554432 | tf_op jit(solution)/shard_map/concatenate | solution.py:664
  70.7 34.8 %all-to-all-done.x_ref = f32[4,64,16,256]{3,2,1,0:T(8,128)} async-done(((f32[4,64,16,256]{3,2,1,0:T(8,128)}), f32[4,64,16,256]{3,2,1,0:T(8,128)}, u32[]{:S(2)}, u32[]{:S(2)}) %all-to-all-start) | async-done | bytes 4194336 | tf_op jit(solution)/shard_map/all_to_all | solution.py:639
  105.5 10.5 %all-to-all-start.1 = ((f32[4,4,16,64,256]{4,3,2,1,0:T(8,128)}), f32[4,4,16,64,256]{4,3,2,1,0:T(8,128)}, u32[]{:S(2)}, u32[]{:S(2)}) async-start(f32[4,4,16,64,256]{4,3,2,1,0:T(8,128)} %pad_maximum_fusion), calls=%async_computation.1 | async-start | bytes 33554432 | tf_op jit(solution)/shard_map/all_to_all | solution.py:639
  116.3 85.8 %scatter_custom_fusion = f32[12825]{0:T(1024)S(1)} fusion(s32[16384]{0:T(1024)S(1)} %bitcast.91, f32[16384]{0:T(1024)S(1)} %bitcast.95, f32[]{:T(128)} %constant.121.clone.1), kind=kCustom, calls=%fused_computation.40 | custom fusion | flops 16384 | bytes 51304 | tf_op jit(solution)/shard_map/scatter-add | solution.py:632
  212.7 7.1 sort.46
  225.2 19.5 %sort.47 = (s32[16448]{0:T(1024)}, s32[16448]{0:T(1024)S(1)}, s32[16448]{0:T(1024)S(1)}, s32[16448]{0:T(1024)}) sort(s32[16448]{0:T(1024)S(1)} %pad_add_fusion, s32[16448]{0:T(1024)S(1)} %concatenate.41, s32[16448]{0:T(1024)S(1)} %concatenate.42, s32[16448]{0:T(1024)S(1)} %iota.90), dimensions={0}, to_apply=%region_3.4 | sort | flops 246720 | bytes 526336 | tf_op jit(solution)/shard_map/sort | solution.py:586
  247.8 10.6 %node_major.3 = f32[1,4,16,64,256]{4,3,2,1,0:T(8,128)} custom-call(f32[4,64,16,256]{3,2,1,0:T(8,128)} %all-to-all-done.x_ref), custom_call_target="tpu_custom_call" | custom-call | flops 1048576 | bytes 8388608 | tf_op jit(solution)/shard_map/node_major/pallas_call | solution.py:90
  258.5 4.0 convert_reduce_fusion
  263.2 7.5 line_derivative.6.usa_ref
  274.6 23.3 %copy.41 = bf16[12,256,16,256]{3,1,2,0:T(8,128)(2,1)} copy(bf16[12,256,16,256]{3,2,1,0:T(8,128)(2,1)} %param.12) | data formatting | bytes 50331648 | tf_op jit(solution)/shard_map/optimization_barrier | solution.py:665
  301.3 90.5 %gather_fusion.3 = f32[16384]{0:T(1024)S(1)} fusion(f32[12825]{0:T(1024)S(1)} %scatter_fusion, s32[16384]{0:T(1024)S(1)} %broadcast_clamp_fusion), kind=kCustom, calls=%fused_computation.3 | custom fusion | bytes 196608 | tf_op jit(solution)/shard_map/gather | solution.py:635
  393.1 104.1 %pmax.7 = f32[]{:T(128)} all-reduce(f32[]{:T(128)} %fusion.6), channel_id=1, replica_groups=mesh['mesh'=8,'four'=4] {'mesh','four'}, use_global_device_ids=true, to_apply=%region_15.16 | all-reduce | flops 1 | bytes 8 | tf_op jit(solution)/shard_map/pmax | solution.py:618
  498.5 6.6 all-to-all-start.2
  506.3 13.7 %line_derivative.7.usb_ref = f32[4,2,16,64,256]{4,3,2,1,0:T(8,128)} custom-call(f32[4,4,16,64,256]{4,3,2,1,0:T(8,128)} %all-to-all-done.1.x_ref.ub_ref.ur_ref.u_ref), custom_call_target="tpu_custom_call" | custom-call | flops 33554432 | bytes 16777216 | tf_op jit(solution)/shard_map/line_derivative/pallas_call | solution.py:119
  520.1 30.6 %base_products.1 = (f32[16,256,256]{2,1,0:T(8,128)}, f32[3,16,256,256]{3,2,1,0:T(8,128)}) custom-call(bf16[512,768]{1,0:T(8,128)(2,1)} %constant.131.clone.both_ref, bf16[256,768]{1,0:T(8,128)(2,1)} %constant.132.clone.synth_ref, f32[4,1,16,64,256]{4,3,2,1,0:T(8,128)} %bitcast.84, f32[4,4,16,64,256]{4,3,2,1,0:T(8,128)} %all-to-all-done.1.x_ref.ub_ref.ur_ref.u_ref, ...), custom_call_target="tpu_custom_call" | custom-call | flops 14495514624 | bytes 67108864 | tf_op jit(solution)/shard_map/base_products/pallas_call | solution.py:176
  550.6 32.8 %forcing_modes.1 = f32[4,2,16,64,256]{4,3,2,1,0:T(8,128)} custom-call(bf16[256,768]{1,0:T(8,128)(2,1)} %constant.132.clone.synth_ref, bf16[256,768]{1,0:T(8,128)(2,1)} %constant.133.clone.analysis_ref, f32[4,4,16,64,256]{4,3,2,1,0:T(8,128)} %all-to-all-done.1.x_ref.ub_ref.ur_ref.u_ref, f32[16,256,256]{2,1,0:T(8,128)} %get-tuple-element.73.vr_ref, ...), custom_call_target="tpu_custom_call" | custom-call | flops 6442450944 | bytes 33554432 | tf_op jit(solution)/shard_map/forcing_modes/pallas_call | solution.py:218
  583.5 10.5 %all-to-all-done.2.ur_ref = f32[4,1,16,64,256]{4,3,2,1,0:T(8,128)} async-done(((f32[4,1,16,64,256]{4,3,2,1,0:T(8,128)}), f32[4,1,16,64,256]{4,3,2,1,0:T(8,128)}, u32[]{:S(2)}, u32[]{:S(2)}) %all-to-all-start.2) | async-done | bytes 4194336 | tf_op jit(solution)/shard_map/all_to_all | solution.py:639
  594.0 9.5 %all-to-all-start.3 = ((f32[4,2,16,64,256]{4,3,2,1,0:T(8,128)}), f32[4,2,16,64,256]{4,3,2,1,0:T(8,128)}, u32[]{:S(2)}, u32[]{:S(2)}) async-start(f32[4,2,16,64,256]{4,3,2,1,0:T(8,128)} %forcing_modes.1), calls=%async_computation.3 | async-start | bytes 16777216 | tf_op jit(solution)/shard_map/all_to_all | solution.py:639
  604.9 20.7 %forcing_and_rims.1 = (f32[4,1,16,64,256]{4,3,2,1,0:T(8,128)}, f32[480,256]{1,0:T(8,128)}) custom-call(bf16[256,768]{1,0:T(8,128)(2,1)} %constant.132.clone.synth_ref, bf16[256,768]{1,0:T(8,128)(2,1)} %constant.133.clone.analysis_ref, f32[4,1,16,64,256]{4,3,2,1,0:T(8,128)} %all-to-all-done.2.ur_ref, ...), custom_call_target="tpu_custom_call" | custom-call | flops 6442450944 | bytes 20971520 | tf_op jit(solution)/shard_map/forcing_and_rims/pallas_call | solution.py:273
  633.1 4.2 collective-permute-done.5
  640.2 13.2 %take_rims.1 = f32[4,1,16,64,256]{4,3,2,1,0:T(8,128)} custom-call(f32[4,1,16,64,256]{4,3,2,1,0:T(8,128)} %get-tuple-element.78.f_ref, f32[256,480]{1,0:T(8,128)} %bitcast.87, s32[480,1]{1,0:T(8,128)} %copy.34.to_ref), custom_call_target="tpu_custom_call", output_to_operand_aliasing={{}: (0, {})} | custom-call | flops 2013265920 | bytes 8388608 | tf_op jit(solution)/shard_map/take_rims/pallas_call | solution.py:316
  653.4 128.7 %all-to-all-done.3.f_ref = f32[4,2,16,64,256]{4,3,2,1,0:T(8,128)} async-done(((f32[4,2,16,64,256]{4,3,2,1,0:T(8,128)}), f32[4,2,16,64,256]{4,3,2,1,0:T(8,128)}, u32[]{:S(2)}, u32[]{:S(2)}) %all-to-all-start.3) | async-done | bytes 8388640 | tf_op jit(solution)/shard_map/all_to_all | solution.py:639
  782.1 8.8 all-to-all-start.4
  790.9 25.9 %local_sums.1 = (f32[16392,128]{1,0:T(8,128)}, f32[240,128]{1,0:T(8,128)}, f32[240,128]{1,0:T(8,128)}) custom-call(s32[3648]{0:T(1024)} %get-tuple-element.66.mem, s32[3648]{0:T(1024)} %get-tuple-element.67.rep, s32[10]{0:T(128)} %reshape.456.bnd, s32[2,240]{1,0:T(2,128)} %get-tuple-element.84.er, f32[4,2,16,64,256]{4,3,2,1,0:T(8,128)} %all-to-all-done.3.f_ref, ...), custom_call_target="tpu_custom_call" | custom-call | flops 838860800 | bytes 25165824 | tf_op jit(solution)/shard_map/local_sums/pallas_call | solution.py:485
  825.5 20.0 %spread.1._ = f32[3,64,64,256]{3,2,1,0:T(8,128)} custom-call(s32[3648]{0:T(1024)} %get-tuple-element.66.mem, s32[3648]{0:T(1024)} %get-tuple-element.67.rep, s32[10]{0:T(128)} %reshape.456.bnd, s32[2,240]{1,0:T(2,128)} %get-tuple-element.84.er, f32[16392,128]{1,0:T(8,128)} %get-tuple-element.87.t_ref, f32[240,128]{1,0:T(8,128)} %copy-done.4, ...), custom_call_target="tpu_custom_call" | custom-call | flops 838860800 | bytes 25165824 | tf_op jit(solution)/shard_map/spread/pallas_call | solution.py:551
  845.5 34.1 %all-to-all-done.4.f_ref = f32[4,1,16,64,256]{4,3,2,1,0:T(8,128)} async-done(((f32[4,1,16,64,256]{4,3,2,1,0:T(8,128)}), f32[4,1,16,64,256]{4,3,2,1,0:T(8,128)}, u32[]{:S(2)}, u32[]{:S(2)}) %all-to-all-start.4) | async-done | bytes 4194336 | tf_op jit(solution)/shard_map/all_to_all | solution.py:639
  879.7 27.7 %finish.1 = f32[3,64,64,256]{3,2,1,0:T(8,128)} custom-call(s32[3648]{0:T(1024)} %get-tuple-element.66.mem, s32[3648]{0:T(1024)} %get-tuple-element.67.rep, s32[10]{0:T(128)} %reshape.456.bnd, f32[4,1,16,64,256]{4,3,2,1,0:T(8,128)} %all-to-all-done.4.f_ref, f32[4,3,16,64,256]{4,3,2,1,0:T(8,128)} %node_major.2.x_ref.u_ref, ...), custom_call_target="tpu_custom_call", output_to_operand_aliasing={{}: (7, {})} | custom-call | flops 838860800 | bytes 12582912 | tf_op jit(solution)/shard_map/finish/pallas_call | solution.py:422
  (101 shorter events, 55.7 us)
Async XLA Ops:
  6.5 498.6 %copy-start = (f32[4,64,256]{2,1,0:T(8,128)S(1)}, f32[4,64,256]{2,1,0:T(8,128)}, u32[]{:S(2)}) copy-start(f32[4,64,256]{2,1,0:T(8,128)} %param.13) | copy-start | bytes 786436
  6.5 2.3 slice-start
  11.4 94.1 %all-to-all-start = ((f32[4,64,16,256]{3,2,1,0:T(8,128)}), f32[4,64,16,256]{3,2,1,0:T(8,128)}, u32[]{:S(2)}, u32[]{:S(2)}) async-start(f32[4,64,16,256]{3,2,1,0:T(8,128)} %bitcast.86), calls=%async_computation | async-start | bytes 8388608 | tf_op jit(solution)/shard_map/all_to_all | solution.py:639
  70.7 45.3 %copy-start.6 = (s32[1,2,225]{2,1,0:T(2,128)S(1)}, s32[1,2,225]{2,1,0:T(2,128)}, u32[]{:S(2)}) copy-start(s32[1,2,225]{2,1,0:T(2,128)} %param.16) | copy-start | bytes 5404
  70.7 45.5 %copy-start.3 = (s32[64,256]{1,0:T(8,128)S(1)}, s32[64,256]{1,0:T(8,128)}, u32[]{:S(2)}) copy-start(s32[64,256]{1,0:T(8,128)} %param.15) | copy-start | bytes 196612
  70.7 45.5 %copy-start.2 = (f32[64,256]{1,0:T(8,128)S(1)}, f32[64,256]{1,0:T(8,128)}, u32[]{:S(2)}) copy-start(f32[64,256]{1,0:T(8,128)} %mass_ref.1) | copy-start | bytes 196612
  105.5 393.0 %all-to-all-start.1 = ((f32[4,4,16,64,256]{4,3,2,1,0:T(8,128)}), f32[4,4,16,64,256]{4,3,2,1,0:T(8,128)}, u32[]{:S(2)}, u32[]{:S(2)}) async-start(f32[4,4,16,64,256]{4,3,2,1,0:T(8,128)} %pad_maximum_fusion), calls=%async_computation.1 | async-start | bytes 33554432 | tf_op jit(solution)/shard_map/all_to_all | solution.py:639
  115.9 146.6 %copy-start.7 = (pred[3648]{0:T(1024)(128)(4,1)S(1)}, pred[3648]{0:T(1024)(128)(4,1)}, u32[]{:S(2)}) copy-start(pred[3648]{0:T(1024)(128)(4,1)} %constant.104.clone.1) | copy-start | bytes 10948
  203.9 94.0 %collective-permute-start = (f32[225]{0:T(256)S(1)}, f32[225]{0:T(256)S(1)}, u32[]{:S(2)}, u32[]{:S(2)}) collective-permute-start(f32[225]{0:T(256)S(1)} %gather_fusion.1), channel_id=1, source_target_pairs={{0,4},{4,8},{8,12},{12,16},{16,20},{20,24},{24,28},{28,0},{1,5},{5... | collective-permute-start | bytes 2708 | tf_op jit(solution)/shard_map/ppermute | solution.py:628
  208.7 89.2 %collective-permute-start.1 = (f32[225]{0:T(256)S(1)}, f32[225]{0:T(256)S(1)}, u32[]{:S(2)}, u32[]{:S(2)}) collective-permute-start(f32[225]{0:T(256)S(1)} %gather_fusion.2), channel_id=1, source_target_pairs={{4,0},{8,4},{12,8},{16,12},{20,16},{24,20},{28,24},{0,28},{5,1},{9... | collective-permute-start | bytes 2708 | tf_op jit(solution)/shard_map/ppermute | solution.py:628
  210.3 181.5 %collective-permute-start.2 = (f32[240]{0:T(256)S(1)}, f32[240]{0:T(256)S(1)}, u32[]{:S(2)}, u32[]{:S(2)}) collective-permute-start(f32[240]{0:T(256)S(1)} %bitcast.107), channel_id=1, source_target_pairs={{0,4},{4,8},{8,12},{12,16},{16,20},{20,24},{24,28},{28,0},{1,5},{5... | collective-permute-start | bytes 2888 | tf_op jit(solution)/shard_map/ppermute | solution.py:628
  212.1 179.8 %collective-permute-start.3 = (f32[240]{0:T(256)S(1)}, f32[240]{0:T(256)S(1)}, u32[]{:S(2)}, u32[]{:S(2)}) collective-permute-start(f32[240]{0:T(256)S(1)} %bitcast.105), channel_id=1, source_target_pairs={{4,0},{8,4},{12,8},{16,12},{20,16},{24,20},{28,24},{0,28},{5,1},{9... | collective-permute-start | bytes 2888 | tf_op jit(solution)/shard_map/ppermute | solution.py:628
  498.5 95.5 %all-to-all-start.2 = ((f32[4,1,16,64,256]{4,3,2,1,0:T(8,128)}), f32[4,1,16,64,256]{4,3,2,1,0:T(8,128)}, u32[]{:S(2)}, u32[]{:S(2)}) async-start(f32[4,1,16,64,256]{4,3,2,1,0:T(8,128)} %line_derivative.5), calls=%async_computation.2 | async-start | bytes 8388608 | tf_op jit(solution)/shard_map/all_to_all | solution.py:639
  594.0 188.1 %all-to-all-start.3 = ((f32[4,2,16,64,256]{4,3,2,1,0:T(8,128)}), f32[4,2,16,64,256]{4,3,2,1,0:T(8,128)}, u32[]{:S(2)}, u32[]{:S(2)}) async-start(f32[4,2,16,64,256]{4,3,2,1,0:T(8,128)} %forcing_modes.1), calls=%async_computation.3 | async-start | bytes 16777216 | tf_op jit(solution)/shard_map/all_to_all | solution.py:639
  626.8 6.3 collective-permute-start.4
  629.5 7.8 collective-permute-start.5
  782.1 97.6 %all-to-all-start.4 = ((f32[4,1,16,64,256]{4,3,2,1,0:T(8,128)}), f32[4,1,16,64,256]{4,3,2,1,0:T(8,128)}, u32[]{:S(2)}, u32[]{:S(2)}) async-start(f32[4,1,16,64,256]{4,3,2,1,0:T(8,128)} %take_rims.1), calls=%async_computation.4 | async-start | bytes 8388608 | tf_op jit(solution)/shard_map/all_to_all | solution.py:639
  816.8 4.9 collective-permute-start.6
  819.5 5.4 collective-permute-start.7
  821.7 3.2 copy-start.4
  824.9 0.7 copy-start.5
  879.7 27.7 %copy-start.1 = (f32[4,64,256]{2,1,0:T(8,128)S(1)}, f32[4,64,256]{2,1,0:T(8,128)}, u32[]{:S(2)}) copy-start(f32[4,64,256]{2,1,0:T(8,128)} %param.13) | copy-start | bytes 786436

commit v6 on v5

--- a/solution.py
+++ b/solution.py
@@ -76,6 +76,34 @@
     return pltpu.CompilerParams(vmem_limit_bytes=VMEM_LIMIT, **kw)
 
 
+def slabs(x, parts):
+    _, m_n, n_n, e_n = x.shape
+    l_n = n_n // parts
+    if l_n % 8:
+        return x[0].reshape(m_n, parts, l_n, e_n).transpose(1, 0, 2, 3)
+
+    def kernel(x_ref, o_ref, sems):
+        copies = [
+            pltpu.make_async_copy(x_ref.at[0, :, pl.ds(q * l_n, l_n), :], o_ref.at[q], sems.at[q])
+            for q in range(parts)
+        ]
+        for copy in copies:
+            copy.start()
+        for copy in copies:
+            copy.wait()
+
+    return pl.pallas_call(
+        kernel,
+        in_specs=[pl.BlockSpec(memory_space=pl.ANY)],
+        out_specs=pl.BlockSpec(memory_space=pl.ANY),
+        out_shape=jax.ShapeDtypeStruct((parts, m_n, l_n, e_n), jnp.float32),
+        scratch_shapes=[pltpu.SemaphoreType.DMA((parts,))],
+        compiler_params=params(),
+        cost_estimate=pl.CostEstimate(flops=0, bytes_accessed=8 * m_n * n_n * e_n, transcendentals=0),
+        name="slabs",
+    )(x)
+
+
 def node_major(x, parts):
     c_n, m_n, n_n, e_n = x.shape
     l_n = n_n // parts
@@ -300,36 +328,57 @@
     )(synth, analysis, ur, u, vr, part, mass, connect, edge_ids)
 
 
-def take_rims(modes, rims, takers):
+def own_sums(modes, u, mass, connect, rims, edge_ids, u_at):
     s_n, _, l_n, m_n, e_n = modes.shape
-    k_n = takers.shape[0]
-
-    def kernel(f_ref, rim_ref, to_ref, o_ref):
+    k_n = edge_ids.shape[0]
+    coefs = s_n * m_n
+
+    def kernel(f_ref, u_ref, mass_ref, conn_ref, turned_ref, rim_ref, id_ref, o_ref, held):
         l = pl.program_id(0)
-        column = l * e_n + lax.broadcasted_iota(jnp.int32, (1, e_n), 1)
-        there = jnp.where(to_ref[...] == column, 1.0, 0.0).astype(jnp.bfloat16)
+
+        @pl.when(l == 0)
+        def _():
+            for k in range(l_n):
+                weighted = f_ref[:, 0, k] + mass_ref[k : k + 1, :] * u_ref[:, 0, k]
+                high, low = split(weighted.reshape(coefs, e_n))
+                held[k] = jnp.concatenate([high, low], axis=1)
+
+        mine = conn_ref[pl.ds(l, 1), :]
+
+        def same(ids):
+            there = jnp.where(ids == mine, 1.0, 0.0).astype(jnp.bfloat16)
+            return jnp.concatenate([there, there], axis=0)
+
         high, low = split(rim_ref[...])
-        add = product(jnp.concatenate([high, low], axis=1), jnp.concatenate([there, there], axis=0))
-        o_ref[:, 0, 0] = f_ref[:, 0, 0] + add.reshape(s_n, m_n, e_n)
-
-    block = pl.BlockSpec((s_n, 1, 1, m_n, e_n), lambda l: (0, 0, l, 0, 0))
+        total = product(jnp.concatenate([high, low], axis=1), same(id_ref[...]))
+        for k in range(l_n):
+            total = total + product(held[k], same(turned_ref[k]))
+        o_ref[:, 0, 0] = total.reshape(s_n, m_n, e_n)
+
+    def whole(*shape):
+        return pl.BlockSpec(shape, lambda l: (0,) * len(shape))
+
     return pl.pallas_call(
         kernel,
         grid=(l_n,),
         in_specs=[
-            block,
-            pl.BlockSpec((s_n * m_n, k_n), lambda l: (0, 0)),
-            pl.BlockSpec((k_n, 1), lambda l: (0, 0)),
-        ],
-        out_specs=block,
+            whole(s_n, 1, l_n, m_n, e_n),
+            pl.BlockSpec((s_n, 1, l_n, m_n, e_n), lambda l: (0, u_at, 0, 0, 0)),
+            whole(l_n, e_n),
+            whole(l_n, e_n),
+            whole(l_n, e_n, 1),
+            whole(coefs, k_n),
+            whole(k_n, 1),
+        ],
+        out_specs=pl.BlockSpec((s_n, 1, 1, m_n, e_n), lambda l: (0, 0, l, 0, 0)),
         out_shape=jax.ShapeDtypeStruct(modes.shape, jnp.float32),
-        input_output_aliases={0: 0},
+        scratch_shapes=[pltpu.VMEM((l_n, coefs, 2 * e_n), jnp.bfloat16)],
         compiler_params=params(),
         cost_estimate=pl.CostEstimate(
-            flops=4 * l_n * s_n * m_n * k_n * e_n, bytes_accessed=8 * modes.size, transcendentals=0
-        ),
-        name="take_rims",
-    )(modes, rims, takers)
+            flops=4 * l_n * l_n * coefs * e_n * e_n, bytes_accessed=12 * modes.size, transcendentals=0
+        ),
+        name="own_sums",
+    )(modes, u, mass, connect, connect[:, :, None], rims, edge_ids)
 
 
 def rows_of(ref, places):
@@ -373,73 +422,59 @@
     lax.fori_loop(0, pl.cdiv(end - start, BATCH), batch, 0)
 
 
-def finish(modes, u, mass, pairs, inverse, held, shape, c):
-    s_n, _, l_n, m_n, e_n = modes.shape
+def finish(sums, pairs, inverse, held, shape, c):
+    s_n, _, l_n, m_n, e_n = sums.shape
     _, _, nodes_n, _ = shape
     rows_n = nodes_n * e_n
     members, reps, bounds = pairs
-    step = min(8, l_n)
-    per = l_n // step
-    fills = nodes_n // step
-    outs = nodes_n // 8
-
-    def kernel(mem, rep, bnd, f_ref, u_ref, mass_ref, inv_ref, _, o_ref, table, stage):
+    step = max(8, l_n)
+    outs = nodes_n // step
+
+    def kernel(mem, rep, bnd, f_ref, inv_ref, _, o_ref, table, stage):
         b = pl.program_id(0)
 
-        @pl.when(b < fills)
+        @pl.when(b < s_n)
         def _():
-            for t in range(step):
-                node = b * step + t
-                rows = f_ref[0, 0, t] + mass_ref[pl.ds(node, 1), :] * u_ref[0, 0, t]
-                table[pl.ds(pl.multiple_of(node * e_n, e_n), e_n), :] = rows.T
-
-        @pl.when(b == fills - 1)
+            for t in range(l_n):
+                node = b * l_n + t
+                table[pl.ds(pl.multiple_of(node * e_n, e_n), e_n), :] = f_ref[0, 0, t].T
+
+        @pl.when(b == s_n - 1)
         def _():
             table[pl.ds(rows_n, 8), :] = jnp.zeros((8, m_n), jnp.float32)
             for k in range(CLASSES):
                 sum_class(table, mem, rep, bnd[2 * k], bnd[2 * k + 1], k == 0)
             sum_rest(table, mem, rep, bnd[2 * CLASSES], bnd[2 * CLASSES + 1])
-            hand_back(table, mem, rep, bnd[2], bnd[2 * CLASSES] + bnd[2 * CLASSES + 1])
-
-        @pl.when(b >= fills)
+            hand_back(table, mem, rep, bnd[2], bnd[2 * CLASSES + 2] + bnd[2 * CLASSES + 3])
+
+        @pl.when(b >= s_n)
         def _():
-            for t in range(8):
-                n = (b - fills) * 8 + t
+            for t in range(step):
+                n = (b - s_n) * step + t
                 rows = table[pl.ds(pl.multiple_of(n * e_n, e_n), e_n), :].T
                 stage[t] = rows * inv_ref[pl.ds(n, 1), :]
             o_ref[0] = jnp.swapaxes(stage[...], 0, 1)
 
     smem = pl.BlockSpec(memory_space=pltpu.SMEM)
-
-    def where(channel):
-        def index(b):
-            b = jnp.minimum(b, fills - 1)
-            return (b // per, channel, b % per, 0, 0)
-
-        return index
-
-    nodes = pl.BlockSpec((nodes_n, e_n), lambda b: (0, 0))
-    return pl.pallas_call(
-        kernel,
-        grid=(fills + outs,),
+    return pl.pallas_call(
+        kernel,
+        grid=(s_n + outs,),
         in_specs=[smem] * 3
         + [
-            pl.BlockSpec((1, 1, step, m_n, e_n), where(0)),
-            pl.BlockSpec((1, 1, step, m_n, e_n), where(c)),
-            nodes,
-            nodes,
+            pl.BlockSpec((1, 1, l_n, m_n, e_n), lambda b: (jnp.minimum(b, s_n - 1), 0, 0, 0, 0)),
+            pl.BlockSpec((nodes_n, e_n), lambda b: (0, 0)),
             pl.BlockSpec(memory_space=pl.ANY),
         ],
-        out_specs=pl.BlockSpec((1, m_n, 8, e_n), lambda b: (c, 0, jnp.maximum(b - fills, 0), 0)),
+        out_specs=pl.BlockSpec((1, m_n, step, e_n), lambda b: (c, 0, jnp.maximum(b - s_n, 0), 0)),
         out_shape=jax.ShapeDtypeStruct(shape, jnp.float32),
-        scratch_shapes=[pltpu.VMEM((rows_n + 8, m_n), jnp.float32), pltpu.VMEM((8, m_n, e_n), jnp.float32)],
-        input_output_aliases={7: 0},
+        scratch_shapes=[pltpu.VMEM((rows_n + 8, m_n), jnp.float32), pltpu.VMEM((step, m_n, e_n), jnp.float32)],
+        input_output_aliases={5: 0},
         compiler_params=params(),
         cost_estimate=pl.CostEstimate(
             flops=rows_n * LANES * 400, bytes_accessed=rows_n * m_n * 12, transcendentals=0
         ),
         name="finish",
-    )(members, reps, bounds, modes, u, mass, inverse, held)
+    )(members, reps, bounds, sums, inverse, held)
 
 
 def local_sums(modes, u, mass, pairs, edge_reps, first):
@@ -570,62 +605,95 @@
     return jnp.pad(values, pad, constant_values=filler)
 
 
-def pair_lists(ids, edges):
-    rows_n = ids.shape[0]
-    place = jnp.arange(rows_n, dtype=jnp.int32)
-    ids_sorted, member = lax.sort((ids, place), num_keys=1)
-    head = jnp.concatenate([jnp.ones((1,), bool), ids_sorted[1:] != ids_sorted[:-1]])
-    last = jnp.concatenate([head[1:], jnp.ones((1,), bool)])
-    code = lax.cummax(jnp.where(head, place * rows_n + member, 0))
-    rep = code % rows_n
-    rank = place - code // rows_n
-    group = jnp.where((rank == 1) & last, 0, jnp.minimum(rank, CLASSES))
-    group = jnp.where(rank == 0, CLASSES + 1, group).astype(jnp.int32)
+def grouped(group, classes, member, rep, pairs_n):
+    rows_n = group.shape[0]
     spare = jnp.full((CLASSES * BATCH,), rows_n, jnp.int32)
     spare_group = jnp.arange(CLASSES * BATCH, dtype=jnp.int32) // BATCH
     _, members, reps = lax.sort(
         (
-            jnp.concatenate([group, spare_group]),
+            jnp.concatenate([group.astype(jnp.int32), spare_group]),
             jnp.concatenate([member, spare]),
             jnp.concatenate([rep, spare]),
         ),
         num_keys=1,
         is_stable=True,
     )
-    pairs_n = rows_n - UNIQUE + CLASSES * BATCH
-    numbers = jnp.stack([jnp.sum(group == k, dtype=jnp.int32) for k in range(CLASSES + 1)])
-    starts = jnp.cumsum(numbers) - numbers + BATCH * jnp.arange(CLASSES + 1, dtype=jnp.int32)
+    spares = BATCH * jnp.minimum(jnp.arange(classes, dtype=jnp.int32), CLASSES)
+    numbers = jnp.stack([jnp.sum(group == k, dtype=jnp.int32) for k in range(classes)])
+    starts = jnp.cumsum(numbers) - numbers + spares
     bounds = jnp.stack([starts, numbers], axis=1).reshape(-1).astype(jnp.int32)
-    more = BATCH + -pairs_n % BATCH
-    members = jnp.pad(members[:pairs_n], (0, more), constant_values=rows_n)
-    reps = jnp.pad(reps[:pairs_n], (0, more), constant_values=rows_n)
+    length = pairs_n + CLASSES * BATCH
+    more = BATCH + -length % BATCH
+    members = jnp.pad(members[:length], (0, more), constant_values=rows_n)
+    reps = jnp.pad(reps[:length], (0, more), constant_values=rows_n)
+    return members, reps, bounds
+
+
+def pair_lists(ids, edges, parts):
+    rows_n = ids.shape[0]
+    place = jnp.arange(rows_n, dtype=jnp.int32)
+    ids_sorted, member = lax.sort((ids, place), num_keys=1, is_stable=True)
+    yes = jnp.ones((1,), bool)
+    head = jnp.concatenate([yes, ids_sorted[1:] != ids_sorted[:-1]])
+    last = jnp.concatenate([head[1:], yes])
+    code = lax.cummax(jnp.where(head, place * rows_n + member, 0))
+    rep = code % rows_n
+    rank = place - code // rows_n
+    pairs_n = rows_n - UNIQUE
+    group = jnp.where((rank == 1) & last, 0, jnp.minimum(rank, CLASSES))
+    group = jnp.where(rank == 0, CLASSES + 1, group)
+    pairs = grouped(group, CLASSES + 1, member, rep, pairs_n)
+
+    device = member // (rows_n // parts)
+    device_first = head | jnp.concatenate([yes, device[1:] != device[:-1]])
+    device_no = lax.cumsum(device_first.astype(jnp.int32))
+    device_rank = device_no - lax.cummax(jnp.where(head, device_no, 0))
+    most = lax.cummax(jnp.where(last, (rows_n - place) * parts + device_rank, 0), reverse=True) % parts
+    group = jnp.where(device_first, jnp.minimum(device_rank, CLASSES), CLASSES + 1)
+    group = jnp.where((rank == 1) & last & (device_rank == 1), 0, group)
+    group = jnp.where((rank == 0) | (most == 0), CLASSES + 2, group)
+    across = grouped(group, CLASSES + 2, member, rep, pairs_n)
+
     flat = edges.reshape(-1)
     start = jnp.sum(ids_sorted[None, :] < flat[:, None], axis=1, dtype=jnp.int32)
     edge_reps = fill_up(member[start].reshape(edges.shape), BATCH, rows_n)
-    return (members, reps, bounds), edge_reps
+    return pairs, across, edge_reps
+
+
+def shifted(x, axis, step):
+    count = lax.axis_size(axis)
+    return lax.ppermute(x, axis, [(i, (i + step) % count) for i in range(count)])
+
+
+def largest(x):
+    for axis in ("mesh", "four"):
+        step = 1
+        while step < lax.axis_size(axis):
+            x = jnp.maximum(x, shifted(x, axis, step))
+            step *= 2
+    return x
+
+
+def total_over_four(x):
+    total = x
+    for step in range(1, lax.axis_size("four")):
+        total = total + shifted(x, "four", step)
+    return total
+
+
+def swap_edges(low, up):
+    return shifted(up, "mesh", 1), shifted(low, "mesh", -1)
 
 
 def edge_takers(edges, connect_here, edge_reps):
-    k_n = edge_reps.shape[1]
     here_n = connect_here.size
     ids = fill_up(edges, BATCH, -1)
-    column = jnp.arange(here_n, dtype=jnp.int32)
-    same = ids[:, :, None] == connect_here.reshape(-1)
-    first = jnp.min(jnp.where(same, column, here_n), axis=2)
-    has = (first < here_n).astype(jnp.float32)
+    has = jnp.any(ids[:, :, None] == connect_here.reshape(-1), axis=2).astype(jnp.float32)
     theirs = jnp.stack(swap_edges(has[0], has[1]))
-    lost = jnp.max(theirs * (1.0 - has))
-    spread_out = lax.pmax(lost, ("mesh", "four")) > 0.5
-    at_rep = jnp.where(edge_reps // here_n == lax.axis_index("four"), edge_reps % here_n, -1)
-    takers = jnp.where(spread_out, at_rep, jnp.where(first < here_n, first, -1))
-    return ids.reshape(2 * k_n, 1), takers.reshape(2 * k_n, 1).astype(jnp.int32), spread_out
-
-
-def swap_edges(low, up):
-    count = lax.axis_size("mesh")
-    upward = [(i, (i + 1) % count) for i in range(count)]
-    downward = [(j, i) for i, j in upward]
-    return lax.ppermute(up, "mesh", upward), lax.ppermute(low, "mesh", downward)
+    spread_out = largest(jnp.max(theirs * (1.0 - has)).reshape(1))[0] > 0.5
+    at_rep = jnp.where(edge_reps // here_n == lax.axis_index("four"), ids, -1)
+    taken = jnp.where(spread_out, at_rep, ids)
+    return ids.reshape(-1, 1), taken.reshape(-1, 1), spread_out
 
 
 def inverse_mass(mass, ids, edges):
@@ -654,7 +722,7 @@
     inside = [[(a, l + j) for j in range(NP)] for a in range(parts) for l in range(0, l_n, NP)]
     whole_rows = l_n % NP == 0
 
-    u_first = adj_modes[0].reshape(m_n, parts, l_n, e_n).transpose(1, 0, 2, 3)
+    u_first = slabs(adj_modes, parts)
     u_first, adj_modes = together((u_first, adj_modes))
     first_here = exchange(u_first)
 
@@ -669,7 +737,7 @@
     here = exchange(sent)
     edges = edge_nodes[0]
     ids = connect.reshape(-1)
-    pairs, edge_reps = pair_lists(ids, edges)
+    pairs, across, edge_reps = pair_lists(ids, edges, parts)
     inverse = inverse_mass(mass, ids, edges)
     base = base_flow.transpose(0, 2, 1, 3)
     if l_n % 8 == 0:
@@ -679,9 +747,9 @@
     us0_here = derivative(u0_here, inside, 0, 1) if whole_rows else None
     mass_here = lax.dynamic_slice_in_dim(mass, mine, l_n, 0)
     connect_here = lax.dynamic_slice_in_dim(connect, mine, l_n, 0)
-    edge_ids, takers, spread_out = edge_takers(edges, connect_here, edge_reps)
-    held = (here, ur_b, pairs, edge_reps, inverse, base, u0_here, us0_here, edge_ids, takers, spread_out)
-    here, ur_b, pairs, edge_reps, inverse, base, u0_here, us0_here, edge_ids, takers, spread_out = together(held)
+    edge_ids, taken_ids, spread_out = edge_takers(edges, connect_here, edge_reps)
+    held = (here, ur_b, pairs, across, edge_reps, inverse, base, u0_here, us0_here, edge_ids, taken_ids, spread_out)
+    here, ur_b, pairs, across, edge_reps, inverse, base, u0_here, us0_here, edge_ids, taken_ids, spread_out = together(held)
 
     ur_b_here = exchange(ur_b)
     us_here = derivative(here, inside, 0, 2) if whole_rows else here[:, 5:7]
@@ -698,8 +766,8 @@
     )
     half = rims.shape[0] // 2
     rims = jnp.concatenate(swap_edges(rims[:half], rims[half:]))
-    rims = lax.cond(spread_out, lambda r: lax.psum(r, "four"), lambda r: r, rims)
-    f_b = take_rims(f_b, rims.T, takers)
+    rims = lax.cond(spread_out, total_over_four, lambda r: r, rims)
+    f_b = own_sums(f_b, here, mass_here, connect_here, rims.T, taken_ids, 1)
     f_b, modes_a = together((f_b, modes_a))
 
     modes_b = exchange(f_b)
@@ -707,7 +775,7 @@
     out = spread(table, swap_edges(*rims), pairs, edge_reps, inverse, None, adj_modes.shape, 0, 2)
     modes_b, out = together((modes_b, out))
 
-    return finish(modes_b, u, mass, pairs, inverse, out, adj_modes.shape, 2)
+    return finish(modes_b, across, inverse, out, adj_modes.shape, 2)
 
 
 def solution(mesh):

time: 930 us -> 1010 us (1.086)
  Pallas kernels: 238 us -> 373 us
  blocking collectives: 104 us -> 0 us
  starting transfers between devices: 51.3 us -> 95.3 us
  other arithmetic: 137 us -> 161 us
  waiting for transfers between devices: 220 us -> 205 us
    pallas_call x2 -> x3, Pallas kernels: 40.9 us -> 176 us  [the longest x1 128 us: slabs(): pl.pallas_call(kernel, in_specs=[pl.BlockSpec(memory_space=pl.ANY)], out_...]
    pmax x1 -> x0, blocking collectives: 104 us -> none  [edge_takers(): spread_out = lax.pmax(lost, ('mesh', 'four')) > 0.5]
    ppermute x8 -> x13, starting transfers between devices: 11.1 us -> 53.6 us  [shifted(): lax.ppermute(x, axis, [(i, (i + step) % count) for i in range(count)])]
    sort x2 -> x3, other arithmetic: 26.6 us -> 45.9 us  [the longest x2 38.8 us: grouped(): lax.sort((jnp.concatenate([group.astype(jnp.int32), spare_group]), jnp.co...]
    all_to_all x5, waiting for transfers between devices: 208 us -> 190 us  [exchange(): return lax.all_to_all(x, 'four', split_axis=0, concat_axis=0, tiled=True)]
  transfers between devices with their start and end apart: 13 -> 18, of which waited for: 8 -> 12; matrix products, arithmetic and copies ran while one was open for 31% -> 32% of each run, Pallas kernels for 23% -> 23%
where the time goes in v6:
time: 1010 us; the launch traced here: 994 us
  Pallas kernels  373 us (37%)
  waiting for transfers between devices  205 us (20%)
  other arithmetic  161 us (16%)
  local copies, waits for them, and re-layouts  155 us (15%)
  starting transfers between devices  95.3 us (9%)
    all_to_all x5, waiting for transfers between devices, exchange(): return lax.all_to_all(x, 'four', split_axis=0, concat_axis=0, tiled=True)  190 us
    pallas_call x1, Pallas kernels, slabs(): pl.pallas_call(kernel, in_specs=[pl.BlockSpec(memory_space=pl.ANY)], out_...  128 us
    gather x1, local copies, waits for them, and re-layouts, inverse_mass(): return (1.0 / summed[ids]).reshape(mass.shape)  90.5 us
    scatter-add x1, other arithmetic, inverse_mass(): summed = jnp.zeros((UNIQUE,), jnp.float32).at[ids].add(mass.reshape(-1))  85.8 us
    ppermute x13, starting transfers between devices, shifted(): lax.ppermute(x, axis, [(i, (i + step) % count) for i in range(count)])  53.6 us
    pallas_call x4, Pallas kernels, derivative(): pl.pallas_call(kernel, grid=(c_n, m_n // rows), in_specs=[pl.BlockSpec(bl...  42.9 us
    all_to_all x5, starting transfers between devices, exchange(): return lax.all_to_all(x, 'four', split_axis=0, concat_axis=0, tiled=True)  41.7 us
    sort x2, other arithmetic, grouped(): lax.sort((jnp.concatenate([group.astype(jnp.int32), spare_group]), jnp.co...  38.8 us
  transfers between devices with their start and end apart: 18, of which 12 were waited for; matrix products, arithmetic and copies ran while one was open for 32% of the time, Pallas kernels for 23%

profile of v6, /device:TPU:9, one launch (start us, length us, event | category | flops | bytes accessed | tf_op | source)
XLA Modules:
  0.0 994.3 jit_solution(15660610615482425735)
XLA Ops:
  0.0 128.2 %slabs.1 = f32[4,64,16,256]{3,2,1,0:T(8,128)} custom-call(f32[3,64,64,256]{3,2,1,0:T(8,128)} %x_ref.2), custom_call_target="tpu_custom_call" | custom-call | bytes 8388608 | tf_op jit(solution)/shard_map/slabs/pallas_call | solution.py:95
  128.2 4.9 all-to-all-start
  133.1 13.8 %node_major.2.x_ref.u_ref = f32[4,3,16,64,256]{4,3,2,1,0:T(8,128)} custom-call(f32[3,64,64,256]{3,2,1,0:T(8,128)} %x_ref.2), custom_call_target="tpu_custom_call" | custom-call | flops 3145728 | bytes 25165824 | tf_op jit(solution)/shard_map/node_major/pallas_call | solution.py:118
  146.9 7.7 slice.110
  154.7 7.6 line_derivative.5
  162.2 13.7 %line_derivative.4 = f32[4,2,16,64,256]{4,3,2,1,0:T(8,128)} custom-call(f32[4,3,16,64,256]{4,3,2,1,0:T(8,128)} %node_major.2.x_ref.u_ref), custom_call_target="tpu_custom_call" | custom-call | flops 33554432 | bytes 16777216 | tf_op jit(solution)/shard_map/line_derivative/pallas_call | solution.py:147
  175.9 11.7 %pad_maximum_fusion = f32[4,4,16,64,256]{4,3,2,1,0:T(8,128)} fusion(f32[4,2,16,64,256]{4,3,2,1,0:T(8,128)} %line_derivative.4, f32[4,2,16,64,256]{4,3,2,1,0:T(8,128)} %slice.110), kind=kLoop, calls=%fused_computation.9 | loop fusion | flops 4194304 | bytes 33554432 | tf_op jit(solution)/shard_map/concatenate | solution.py:732
  187.6 34.8 %all-to-all-done.x_ref = f32[4,64,16,256]{3,2,1,0:T(8,128)} async-done(((f32[4,64,16,256]{3,2,1,0:T(8,128)}), f32[4,64,16,256]{3,2,1,0:T(8,128)}, u32[]{:S(2)}, u32[]{:S(2)}) %all-to-all-start) | async-done | bytes 4194336 | tf_op jit(solution)/shard_map/all_to_all | solution.py:707
  222.4 10.4 %all-to-all-start.1 = ((f32[4,4,16,64,256]{4,3,2,1,0:T(8,128)}), f32[4,4,16,64,256]{4,3,2,1,0:T(8,128)}, u32[]{:S(2)}, u32[]{:S(2)}) async-start(f32[4,4,16,64,256]{4,3,2,1,0:T(8,128)} %pad_maximum_fusion), calls=%async_computation.1 | async-start | bytes 33554432 | tf_op jit(solution)/shard_map/all_to_all | solution.py:707
  237.9 7.1 sort.77
  261.8 85.8 %scatter_custom_fusion = f32[12825]{0:T(1024)S(1)} fusion(s32[16384]{0:T(1024)S(1)} %bitcast.138, f32[16384]{0:T(1024)S(1)} %bitcast.142, f32[]{:T(128)} %constant.155.clone.1), kind=kCustom, calls=%fused_computation.83 | custom fusion | flops 16384 | bytes 51304 | tf_op jit(solution)/shard_map/scatter-add | solution.py:700
  353.0 19.3 %sort.78 = (s32[16448]{0:T(1024)}, s32[16448]{0:T(1024)S(1)}, s32[16448]{0:T(1024)S(1)}, s32[16448]{0:T(1024)}) sort(s32[16448]{0:T(1024)S(1)} %get-tuple-element.141, s32[16448]{0:T(1024)S(1)} %concatenate.62, s32[16448]{0:T(1024)S(1)} %concatenate.63, s32[16448]{0:T(1024)S(1)} %iota.175), dimensions={0}, to_apply=%region_3.4 | sort | flops 246720 | bytes 526336 | tf_op jit(solution)/shard_map/sort | solution.py:612
  372.3 19.5 %sort.79 = (s32[16448]{0:T(1024)}, s32[16448]{0:T(1024)S(1)}, s32[16448]{0:T(1024)S(1)}, s32[16448]{0:T(1024)}) sort(s32[16448]{0:T(1024)S(1)} %get-tuple-element.140, s32[16448]{0:T(1024)S(1)} %concatenate.62, s32[16448]{0:T(1024)S(1)} %concatenate.63, s32[16448]{0:T(1024)S(1)} %iota.183), dimensions={0}, to_apply=%region_16.17 | sort | flops 246720 | bytes 526336 | tf_op jit(solution)/shard_map/sort | solution.py:612
  398.9 10.5 %node_major.3 = f32[1,4,16,64,256]{4,3,2,1,0:T(8,128)} custom-call(f32[4,64,16,256]{3,2,1,0:T(8,128)} %all-to-all-done.x_ref), custom_call_target="tpu_custom_call" | custom-call | flops 1048576 | bytes 8388608 | tf_op jit(solution)/shard_map/node_major/pallas_call | solution.py:118
  409.4 7.9 line_derivative.6.usa_ref
  426.5 23.3 %copy.66 = bf16[12,256,16,256]{3,1,2,0:T(8,128)(2,1)} copy(bf16[12,256,16,256]{3,2,1,0:T(8,128)(2,1)} %param.12) | data formatting | bytes 50331648 | tf_op jit(solution)/shard_map/optimization_barrier | solution.py:733
  453.2 90.5 %gather_fusion.3 = f32[16384]{0:T(1024)S(1)} fusion(f32[12825]{0:T(1024)S(1)} %scatter_fusion, s32[16384]{0:T(1024)S(1)} %broadcast_clamp_fusion), kind=kCustom, calls=%fused_computation.3 | custom fusion | bytes 196608 | tf_op jit(solution)/shard_map/gather | solution.py:703
  556.5 34.7 %collective-permute-start.10 = (f32[1]{0:T(128)}, f32[1]{0:T(128)}, u32[]{:S(2)}, u32[]{:S(2)}) collective-permute-start(f32[1]{0:T(128)} %max.17), channel_id=1, source_target_pairs={{0,1},{1,2},{2,3},{3,0},{4,5},{5,6},{6,7},{7,4},{8,9},{9,10},{10,1... | collective-permute-start | bytes 20 | tf_op jit(solution)/shard_map/ppermute | solution.py:665
  596.4 5.9 all-to-all-start.2
  603.6 13.7 %line_derivative.7.usb_ref = f32[4,2,16,64,256]{4,3,2,1,0:T(8,128)} custom-call(f32[4,4,16,64,256]{4,3,2,1,0:T(8,128)} %all-to-all-done.1.x_ref.ub_ref.ur_ref.u_ref), custom_call_target="tpu_custom_call" | custom-call | flops 33554432 | bytes 16777216 | tf_op jit(solution)/shard_map/line_derivative/pallas_call | solution.py:147
  617.3 30.6 %base_products.1 = (f32[16,256,256]{2,1,0:T(8,128)}, f32[3,16,256,256]{3,2,1,0:T(8,128)}) custom-call(bf16[512,768]{1,0:T(8,128)(2,1)} %constant.162.clone.both_ref, bf16[256,768]{1,0:T(8,128)(2,1)} %constant.163.clone.synth_ref, f32[4,1,16,64,256]{4,3,2,1,0:T(8,128)} %bitcast.133, f32[4,4,16,64,256]{4,3,2,1,0:T(8,128)} %all-to-all-done.1.x_ref.ub_ref.ur_ref.u_ref, ...), custom_call_target="tpu_custom_call" | custom-call | flops 14495514624 | bytes 67108864 | tf_op jit(solution)/shard_map/base_products/pallas_call | solution.py:204
  647.9 32.8 %forcing_modes.1 = f32[4,2,16,64,256]{4,3,2,1,0:T(8,128)} custom-call(bf16[256,768]{1,0:T(8,128)(2,1)} %constant.163.clone.synth_ref, bf16[256,768]{1,0:T(8,128)(2,1)} %constant.164.clone.analysis_ref, f32[4,4,16,64,256]{4,3,2,1,0:T(8,128)} %all-to-all-done.1.x_ref.ub_ref.ur_ref.u_ref, f32[16,256,256]{2,1,0:T(8,128)} %get-tuple-element.83.vr_ref, ...), custom_call_target="tpu_custom_call" | custom-call | flops 6442450944 | bytes 33554432 | tf_op jit(solution)/shard_map/forcing_modes/pallas_call | solution.py:246
  680.7 8.5 all-to-all-done.2.ur_ref
  689.2 11.6 %all-to-all-start.3 = ((f32[4,2,16,64,256]{4,3,2,1,0:T(8,128)}), f32[4,2,16,64,256]{4,3,2,1,0:T(8,128)}, u32[]{:S(2)}, u32[]{:S(2)}) async-start(f32[4,2,16,64,256]{4,3,2,1,0:T(8,128)} %forcing_modes.1), calls=%async_computation.3 | async-start | bytes 16777216 | tf_op jit(solution)/shard_map/all_to_all | solution.py:707
  702.2 20.7 %forcing_and_rims.1 = (f32[4,1,16,64,256]{4,3,2,1,0:T(8,128)}, f32[480,256]{1,0:T(8,128)}) custom-call(bf16[256,768]{1,0:T(8,128)(2,1)} %constant.163.clone.synth_ref, bf16[256,768]{1,0:T(8,128)(2,1)} %constant.164.clone.analysis_ref, f32[4,1,16,64,256]{4,3,2,1,0:T(8,128)} %all-to-all-done.2.ur_ref, ...), custom_call_target="tpu_custom_call" | custom-call | flops 6442450944 | bytes 20971520 | tf_op jit(solution)/shard_map/forcing_and_rims/pallas_call | solution.py:301
  735.8 30.3 %own_sums.1 = f32[4,1,16,64,256]{4,3,2,1,0:T(8,128)} custom-call(f32[4,1,16,64,256]{4,3,2,1,0:T(8,128)} %get-tuple-element.88.f_ref, f32[4,4,16,64,256]{4,3,2,1,0:T(8,128)} %all-to-all-done.1.x_ref.ub_ref.ur_ref.u_ref, f32[16,256]{1,0:T(8,128)} %constant_dynamic-slice_fusion.mass_ref, s32[16,256]{1,0:T(8,128)} %constant_dynamic-slice_fusion.2.conn_ref, ...), custom_call_target="tpu_custom_call" | custom-call | flops 17179869184 | bytes 12582912 | tf_op jit(solution)/shard_map/own_sums/pallas_call | solution.py:361
  766.2 113.2 %all-to-all-done.3.f_ref = f32[4,2,16,64,256]{4,3,2,1,0:T(8,128)} async-done(((f32[4,2,16,64,256]{4,3,2,1,0:T(8,128)}), f32[4,2,16,64,256]{4,3,2,1,0:T(8,128)}, u32[]{:S(2)}, u32[]{:S(2)}) %all-to-all-start.3) | async-done | bytes 8388640 | tf_op jit(solution)/shard_map/all_to_all | solution.py:707
  879.4 8.8 all-to-all-start.4
  888.2 25.7 %local_sums.1 = (f32[16392,128]{1,0:T(8,128)}, f32[240,128]{1,0:T(8,128)}, f32[240,128]{1,0:T(8,128)}) custom-call(s32[3648]{0:T(1024)} %get-tuple-element.94.mem, s32[3648]{0:T(1024)} %get-tuple-element.95.rep, s32[10]{0:T(128)} %reshape.1032.bnd, s32[2,240]{1,0:T(2,128)} %get-tuple-element.97.er, f32[4,2,16,64,256]{4,3,2,1,0:T(8,128)} %all-to-all-done.3.f_ref, ...), custom_call_target="tpu_custom_call" | custom-call | flops 838860800 | bytes 25165824 | tf_op jit(solution)/shard_map/local_sums/pallas_call | solution.py:520
  922.9 20.0 %spread.1._ = f32[3,64,64,256]{3,2,1,0:T(8,128)} custom-call(s32[3648]{0:T(1024)} %get-tuple-element.94.mem, s32[3648]{0:T(1024)} %get-tuple-element.95.rep, s32[10]{0:T(128)} %reshape.1032.bnd, s32[2,240]{1,0:T(2,128)} %get-tuple-element.97.er, f32[16392,128]{1,0:T(8,128)} %get-tuple-element.100.t_ref, f32[240,128]{1,0:T(8,128)} %copy-done.4, ...), custom_call_target="tpu_custom_call" | custom-call | flops 838860800 | bytes 25165824 | tf_op jit(solution)/shard_map/spread/pallas_call | solution.py:586
  942.9 34.0 %all-to-all-done.4.f_ref = f32[4,1,16,64,256]{4,3,2,1,0:T(8,128)} async-done(((f32[4,1,16,64,256]{4,3,2,1,0:T(8,128)}), f32[4,1,16,64,256]{4,3,2,1,0:T(8,128)}, u32[]{:S(2)}, u32[]{:S(2)}) %all-to-all-start.4) | async-done | bytes 4194336 | tf_op jit(solution)/shard_map/all_to_all | solution.py:707
  976.9 17.2 %finish.1 = f32[3,64,64,256]{3,2,1,0:T(8,128)} custom-call(s32[3648]{0:T(1024)} %get-tuple-element.76.mem, s32[3648]{0:T(1024)} %get-tuple-element.77.rep, s32[12]{0:T(128)} %reshape.1037.bnd, f32[4,1,16,64,256]{4,3,2,1,0:T(8,128)} %all-to-all-done.4.f_ref, f32[64,256]{1,0:T(8,128)} %div.68.inv_ref, ...), custom_call_target="tpu_custom_call", output_to_operand_aliasing={{}: (5, {})} | custom-call | flops 838860800 | bytes 12582912 | tf_op jit(solution)/shard_map/finish/pallas_call | solution.py:459
  (150 shorter events, 85.0 us)
Async XLA Ops:
  0.0 602.4 %copy-start = (f32[4,64,256]{2,1,0:T(8,128)S(1)}, f32[4,64,256]{2,1,0:T(8,128)}, u32[]{:S(2)}) copy-start(f32[4,64,256]{2,1,0:T(8,128)} %param.13) | copy-start | bytes 786436
  128.2 94.2 %all-to-all-start = ((f32[4,64,16,256]{3,2,1,0:T(8,128)}), f32[4,64,16,256]{3,2,1,0:T(8,128)}, u32[]{:S(2)}, u32[]{:S(2)}) async-start(f32[4,64,16,256]{3,2,1,0:T(8,128)} %slabs.1), calls=%async_computation | async-start | bytes 8388608 | tf_op jit(solution)/shard_map/all_to_all | solution.py:707
  187.6 45.4 %copy-start.6 = (s32[1,2,225]{2,1,0:T(2,128)S(1)}, s32[1,2,225]{2,1,0:T(2,128)}, u32[]{:S(2)}) copy-start(s32[1,2,225]{2,1,0:T(2,128)} %param.16) | copy-start | bytes 5404
  187.6 45.5 %copy-start.2 = (s32[64,256]{1,0:T(8,128)S(1)}, s32[64,256]{1,0:T(8,128)}, u32[]{:S(2)}) copy-start(s32[64,256]{1,0:T(8,128)} %param.15) | copy-start | bytes 196612
  187.6 74.1 %copy-start.3 = (f32[64,256]{1,0:T(8,128)S(1)}, f32[64,256]{1,0:T(8,128)}, u32[]{:S(2)}) copy-start(f32[64,256]{1,0:T(8,128)} %mass_ref) | copy-start | bytes 196612
  222.4 374.0 %all-to-all-start.1 = ((f32[4,4,16,64,256]{4,3,2,1,0:T(8,128)}), f32[4,4,16,64,256]{4,3,2,1,0:T(8,128)}, u32[]{:S(2)}, u32[]{:S(2)}) async-start(f32[4,4,16,64,256]{4,3,2,1,0:T(8,128)} %pad_maximum_fusion), calls=%async_computation.1 | async-start | bytes 33554432 | tf_op jit(solution)/shard_map/all_to_all | solution.py:707
  234.4 310.0 %collective-permute-start.5 = (f32[240]{0:T(256)S(1)}, f32[240]{0:T(256)S(1)}, u32[]{:S(2)}, u32[]{:S(2)}) collective-permute-start(f32[240]{0:T(256)S(1)} %bitcast.158), channel_id=1, source_target_pairs={{0,4},{4,8},{8,12},{12,16},{16,20},{20,24},{24,28},{28,0},{1,5},{5... | collective-permute-start | bytes 2888 | tf_op jit(solution)/shard_map/ppermute | solution.py:665
  237.4 307.0 %collective-permute-start.6 = (f32[240]{0:T(256)S(1)}, f32[240]{0:T(256)S(1)}, u32[]{:S(2)}, u32[]{:S(2)}) collective-permute-start(f32[240]{0:T(256)S(1)} %bitcast.157), channel_id=1, source_target_pairs={{0,28},{4,0},{8,4},{12,8},{16,12},{20,16},{24,20},{28,24},{1,29},{... | collective-permute-start | bytes 2888 | tf_op jit(solution)/shard_map/ppermute | solution.py:665
  349.4 100.4 %collective-permute-start.3 = (f32[225]{0:T(256)S(1)}, f32[225]{0:T(256)S(1)}, u32[]{:S(2)}, u32[]{:S(2)}) collective-permute-start(f32[225]{0:T(256)S(1)} %gather_fusion.1), channel_id=1, source_target_pairs={{0,4},{4,8},{8,12},{12,16},{16,20},{20,24},{24,28},{28,0},{1,5},{5... | collective-permute-start | bytes 2708 | tf_op jit(solution)/shard_map/ppermute | solution.py:665
  352.9 96.9 %collective-permute-start.4 = (f32[225]{0:T(256)S(1)}, f32[225]{0:T(256)S(1)}, u32[]{:S(2)}, u32[]{:S(2)}) collective-permute-start(f32[225]{0:T(256)S(1)} %gather_fusion.2), channel_id=1, source_target_pairs={{0,28},{4,0},{8,4},{12,8},{16,12},{20,16},{24,20},{28,24},{1,29},{... | collective-permute-start | bytes 2708 | tf_op jit(solution)/shard_map/ppermute | solution.py:665
  398.9 22.3 %copy-start.7 = (pred[3648]{0:T(1024)(128)(4,1)S(1)}, pred[3648]{0:T(1024)(128)(4,1)}, u32[]{:S(2)}) copy-start(pred[3648]{0:T(1024)(128)(4,1)} %constant.135.clone.1) | copy-start | bytes 10948
  545.0 3.2 collective-permute-start.7
  549.5 3.3 collective-permute-start.8
  553.4 2.4 collective-permute-start.9
  556.5 34.7 %collective-permute-start.10 = (f32[1]{0:T(128)}, f32[1]{0:T(128)}, u32[]{:S(2)}, u32[]{:S(2)}) collective-permute-start(f32[1]{0:T(128)} %max.17), channel_id=1, source_target_pairs={{0,1},{1,2},{2,3},{3,0},{4,5},{5,6},{6,7},{7,4},{8,9},{9,10},{10,1... | collective-permute-start | bytes 20 | tf_op jit(solution)/shard_map/ppermute | solution.py:665
  591.8 3.3 collective-permute-start.11
  596.4 92.8 %all-to-all-start.2 = ((f32[4,1,16,64,256]{4,3,2,1,0:T(8,128)}), f32[4,1,16,64,256]{4,3,2,1,0:T(8,128)}, u32[]{:S(2)}, u32[]{:S(2)}) async-start(f32[4,1,16,64,256]{4,3,2,1,0:T(8,128)} %line_derivative.5), calls=%async_computation.2 | async-start | bytes 8388608 | tf_op jit(solution)/shard_map/all_to_all | solution.py:707
  689.2 190.2 %all-to-all-start.3 = ((f32[4,2,16,64,256]{4,3,2,1,0:T(8,128)}), f32[4,2,16,64,256]{4,3,2,1,0:T(8,128)}, u32[]{:S(2)}, u32[]{:S(2)}) async-start(f32[4,2,16,64,256]{4,3,2,1,0:T(8,128)} %forcing_modes.1), calls=%async_computation.3 | async-start | bytes 16777216 | tf_op jit(solution)/shard_map/all_to_all | solution.py:707
  724.0 6.9 collective-permute-start.12
  727.0 7.8 collective-permute-start.13
  879.4 97.5 %all-to-all-start.4 = ((f32[4,1,16,64,256]{4,3,2,1,0:T(8,128)}), f32[4,1,16,64,256]{4,3,2,1,0:T(8,128)}, u32[]{:S(2)}, u32[]{:S(2)}) async-start(f32[4,1,16,64,256]{4,3,2,1,0:T(8,128)} %own_sums.1), calls=%async_computation.4 | async-start | bytes 8388608 | tf_op jit(solution)/shard_map/all_to_all | solution.py:707
  913.9 5.1 collective-permute-start.14
  916.8 5.4 collective-permute-start.15
  919.0 3.2 copy-start.4
  922.2 0.7 copy-start.5
  922.9 71.2 %copy-start.1 = (f32[4,64,256]{2,1,0:T(8,128)S(1)}, f32[4,64,256]{2,1,0:T(8,128)}, u32[]{:S(2)}) copy-start(f32[4,64,256]{2,1,0:T(8,128)} %param.13) | copy-start | bytes 786436

commit v7 on v6

--- a/solution.py
+++ b/solution.py
@@ -16,6 +16,7 @@
 LANES = 128
 BATCH = 16
 CLASSES = 4
+PACK = 15
 VMEM_LIMIT = 56 * 1024 * 1024
 
 
@@ -82,22 +83,17 @@
     if l_n % 8:
         return x[0].reshape(m_n, parts, l_n, e_n).transpose(1, 0, 2, 3)
 
-    def kernel(x_ref, o_ref, sems):
-        copies = [
-            pltpu.make_async_copy(x_ref.at[0, :, pl.ds(q * l_n, l_n), :], o_ref.at[q], sems.at[q])
-            for q in range(parts)
-        ]
-        for copy in copies:
-            copy.start()
-        for copy in copies:
-            copy.wait()
-
-    return pl.pallas_call(
-        kernel,
-        in_specs=[pl.BlockSpec(memory_space=pl.ANY)],
-        out_specs=pl.BlockSpec(memory_space=pl.ANY),
+    rows = m_n // 4 if m_n % 4 == 0 else m_n
+
+    def kernel(x_ref, o_ref):
+        o_ref[...] = x_ref[...]
+
+    return pl.pallas_call(
+        kernel,
+        grid=(parts, m_n // rows),
+        in_specs=[pl.BlockSpec((1, rows, l_n, e_n), lambda q, m: (0, m, q, 0))],
+        out_specs=pl.BlockSpec((1, rows, l_n, e_n), lambda q, m: (q, m, 0, 0)),
         out_shape=jax.ShapeDtypeStruct((parts, m_n, l_n, e_n), jnp.float32),
-        scratch_shapes=[pltpu.SemaphoreType.DMA((parts,))],
         compiler_params=params(),
         cost_estimate=pl.CostEstimate(flops=0, bytes_accessed=8 * m_n * n_n * e_n, transcendentals=0),
         name="slabs",
@@ -382,19 +378,27 @@
 
 
 def rows_of(ref, places):
+    if len(ref.shape) == 3:
+        return [ref[r >> 3, pl.ds(r & 7, 1), :] for r in places]
     return [ref[pl.ds(r, 1), :] for r in places]
 
 
 def put_rows(ref, places, rows):
     for r, row in zip(places, rows):
-        ref[pl.ds(r, 1), :] = row
-
-
-def sum_class(ref, mem, rep, start, number, both):
+        if len(ref.shape) == 3:
+            ref[r >> 3, pl.ds(r & 7, 1), :] = row
+        else:
+            ref[pl.ds(r, 1), :] = row
+
+
+def some_pairs(codes, at, number):
+    found = [codes[at + t] for t in range(number)]
+    return [code >> PACK for code in found], [code & (1 << PACK) - 1 for code in found]
+
+
+def sum_class(ref, codes, start, number, both):
     def batch(i, _):
-        at = start + i * BATCH
-        heads = [rep[at + t] for t in range(BATCH)]
-        others = [mem[at + t] for t in range(BATCH)]
+        others, heads = some_pairs(codes, start + i * BATCH, BATCH)
         sums = [a + b for a, b in zip(rows_of(ref, heads), rows_of(ref, others))]
         put_rows(ref, heads, sums)
         if both:
@@ -404,19 +408,19 @@
     lax.fori_loop(0, pl.cdiv(number, BATCH), batch, 0)
 
 
-def sum_rest(ref, mem, rep, start, number):
+def sum_rest(ref, codes, start, number):
     def one(i, _):
-        r = rep[start + i]
-        ref[pl.ds(r, 1), :] = ref[pl.ds(r, 1), :] + ref[pl.ds(mem[start + i], 1), :]
+        others, heads = some_pairs(codes, start + i, 1)
+        put_rows(ref, heads, [rows_of(ref, heads)[0] + rows_of(ref, others)[0]])
         return 0
 
     lax.fori_loop(0, number, one, 0)
 
 
-def hand_back(ref, mem, rep, start, end):
+def hand_back(ref, codes, start, end):
     def batch(i, _):
-        at = start + i * BATCH
-        put_rows(ref, [mem[at + t] for t in range(BATCH)], rows_of(ref, [rep[at + t] for t in range(BATCH)]))
+        others, heads = some_pairs(codes, start + i * BATCH, BATCH)
+        put_rows(ref, others, rows_of(ref, heads))
         return 0
 
     lax.fori_loop(0, pl.cdiv(end - start, BATCH), batch, 0)
@@ -426,32 +430,33 @@
     s_n, _, l_n, m_n, e_n = sums.shape
     _, _, nodes_n, _ = shape
     rows_n = nodes_n * e_n
-    members, reps, bounds = pairs
+    codes, bounds = pairs
     step = max(8, l_n)
+    tiles = e_n // 8
     outs = nodes_n // step
 
-    def kernel(mem, rep, bnd, f_ref, inv_ref, _, o_ref, table, stage):
+    def kernel(codes, bnd, f_ref, inv_ref, _, o_ref, table, stage):
         b = pl.program_id(0)
 
         @pl.when(b < s_n)
         def _():
             for t in range(l_n):
                 node = b * l_n + t
-                table[pl.ds(pl.multiple_of(node * e_n, e_n), e_n), :] = f_ref[0, 0, t].T
+                table[pl.ds(node * tiles, tiles)] = f_ref[0, 0, t].T.reshape(tiles, 8, m_n)
 
         @pl.when(b == s_n - 1)
         def _():
-            table[pl.ds(rows_n, 8), :] = jnp.zeros((8, m_n), jnp.float32)
+            table[nodes_n * tiles] = jnp.zeros((8, m_n), jnp.float32)
             for k in range(CLASSES):
-                sum_class(table, mem, rep, bnd[2 * k], bnd[2 * k + 1], k == 0)
-            sum_rest(table, mem, rep, bnd[2 * CLASSES], bnd[2 * CLASSES + 1])
-            hand_back(table, mem, rep, bnd[2], bnd[2 * CLASSES + 2] + bnd[2 * CLASSES + 3])
+                sum_class(table, codes, bnd[2 * k], bnd[2 * k + 1], k == 0)
+            sum_rest(table, codes, bnd[2 * CLASSES], bnd[2 * CLASSES + 1])
+            hand_back(table, codes, bnd[2], bnd[2 * CLASSES + 2] + bnd[2 * CLASSES + 3])
 
         @pl.when(b >= s_n)
         def _():
             for t in range(step):
                 n = (b - s_n) * step + t
-                rows = table[pl.ds(pl.multiple_of(n * e_n, e_n), e_n), :].T
+                rows = table[pl.ds(n * tiles, tiles)].reshape(e_n, m_n).T
                 stage[t] = rows * inv_ref[pl.ds(n, 1), :]
             o_ref[0] = jnp.swapaxes(stage[...], 0, 1)
 
@@ -459,7 +464,7 @@
     return pl.pallas_call(
         kernel,
         grid=(s_n + outs,),
-        in_specs=[smem] * 3
+        in_specs=[smem] * 2
         + [
             pl.BlockSpec((1, 1, l_n, m_n, e_n), lambda b: (jnp.minimum(b, s_n - 1), 0, 0, 0, 0)),
             pl.BlockSpec((nodes_n, e_n), lambda b: (0, 0)),
@@ -467,14 +472,14 @@
         ],
         out_specs=pl.BlockSpec((1, m_n, step, e_n), lambda b: (c, 0, jnp.maximum(b - s_n, 0), 0)),
         out_shape=jax.ShapeDtypeStruct(shape, jnp.float32),
-        scratch_shapes=[pltpu.VMEM((rows_n + 8, m_n), jnp.float32), pltpu.VMEM((step, m_n, e_n), jnp.float32)],
-        input_output_aliases={5: 0},
+        scratch_shapes=[pltpu.VMEM((nodes_n * tiles + 1, 8, m_n), jnp.float32), pltpu.VMEM((step, m_n, e_n), jnp.float32)],
+        input_output_aliases={4: 0},
         compiler_params=params(),
         cost_estimate=pl.CostEstimate(
             flops=rows_n * LANES * 400, bytes_accessed=rows_n * m_n * 12, transcendentals=0
         ),
         name="finish",
-    )(members, reps, bounds, sums, inverse, held)
+    )(codes, bounds, sums, inverse, held)
 
 
 def local_sums(modes, u, mass, pairs, edge_reps, first):
@@ -483,11 +488,11 @@
     rows_n = nodes_n * e_n
     step = min(8, l_n)
     per = l_n // step
-    members, reps, bounds = pairs
+    codes, bounds = pairs
     edges_n = edge_reps.shape[1]
     feats = c_n * m_n
 
-    def kernel(mem, rep, bnd, er, f_ref, u_ref, mass_ref, o_ref, low_ref, up_ref):
+    def kernel(codes, bnd, er, f_ref, u_ref, mass_ref, o_ref, low_ref, up_ref):
         b = pl.program_id(0)
         for t in range(step):
             node = b * step + t
@@ -501,8 +506,8 @@
             o_ref[pl.ds(rows_n, 8), :] = jnp.zeros((8, feats), jnp.float32)
 
             for k in range(CLASSES):
-                sum_class(o_ref, mem, rep, bnd[2 * k], bnd[2 * k + 1], False)
-            sum_rest(o_ref, mem, rep, bnd[2 * CLASSES], bnd[2 * CLASSES + 1])
+                sum_class(o_ref, codes, bnd[2 * k], bnd[2 * k + 1], False)
+            sum_rest(o_ref, codes, bnd[2 * CLASSES], bnd[2 * CLASSES + 1])
 
             def edge(i, _):
                 for side, to in enumerate((low_ref, up_ref)):
@@ -520,7 +525,7 @@
     return pl.pallas_call(
         kernel,
         grid=(nodes_n // step,),
-        in_specs=[smem] * 4
+        in_specs=[smem] * 3
         + [
             pl.BlockSpec((1, c_n, step, m_n, e_n), where),
             pl.BlockSpec((1, c_n, step, m_n, e_n), where_u),
@@ -533,7 +538,7 @@
             flops=rows_n * LANES * 400, bytes_accessed=rows_n * LANES * 12, transcendentals=0
         ),
         name="local_sums",
-    )(members, reps, bounds, edge_reps, modes, u, mass)
+    )(codes, bounds, edge_reps, modes, u, mass)
 
 
 def spread(table, rims, pairs, edge_reps, inverse, held, shape, first, c_n):
@@ -541,10 +546,10 @@
     rows_n = nodes_n * e_n
     step = 8
     edges_n = edge_reps.shape[1]
-    members, reps, bounds = pairs
+    codes, bounds = pairs
     feats = c_n * m_n
 
-    def kernel(mem, rep, bnd, er, t_ref, low_ref, up_ref, inv_ref, *rest):
+    def kernel(codes, bnd, er, t_ref, low_ref, up_ref, inv_ref, *rest):
         o_ref, stage = rest[-2:]
         b = pl.program_id(0)
 
@@ -558,7 +563,7 @@
                 return 0
 
             lax.fori_loop(0, edges_n // BATCH, edge, 0)
-            hand_back(t_ref, mem, rep, 0, bnd[2 * CLASSES] + bnd[2 * CLASSES + 1])
+            hand_back(t_ref, codes, 0, bnd[2 * CLASSES] + bnd[2 * CLASSES + 1])
 
         for t in range(step):
             n = b * step + t
@@ -571,13 +576,13 @@
 
     smem = pl.BlockSpec(memory_space=pltpu.SMEM)
     rim = pl.BlockSpec((edges_n, feats), lambda b: (0, 0))
-    in_specs = [smem] * 4 + [
+    in_specs = [smem] * 3 + [
         pl.BlockSpec((rows_n + 8, feats), lambda b: (0, 0)),
         rim,
         rim,
         pl.BlockSpec((nodes_n, e_n), lambda b: (0, 0)),
     ]
-    args = [members, reps, bounds, edge_reps, table, *rims, inverse]
+    args = [codes, bounds, edge_reps, table, *rims, inverse]
     aliases = {}
     if held is not None:
         in_specs.append(pl.BlockSpec(memory_space=pl.ANY))
@@ -607,13 +612,13 @@
 
 def grouped(group, classes, member, rep, pairs_n):
     rows_n = group.shape[0]
-    spare = jnp.full((CLASSES * BATCH,), rows_n, jnp.int32)
+    assert rows_n < 1 << PACK
+    nobody = rows_n * (1 << PACK) + rows_n
     spare_group = jnp.arange(CLASSES * BATCH, dtype=jnp.int32) // BATCH
-    _, members, reps = lax.sort(
+    _, codes = lax.sort(
         (
             jnp.concatenate([group.astype(jnp.int32), spare_group]),
-            jnp.concatenate([member, spare]),
-            jnp.concatenate([rep, spare]),
+            jnp.concatenate([member * (1 << PACK) + rep, jnp.full((CLASSES * BATCH,), nobody, jnp.int32)]),
         ),
         num_keys=1,
         is_stable=True,
@@ -623,10 +628,7 @@
     starts = jnp.cumsum(numbers) - numbers + spares
     bounds = jnp.stack([starts, numbers], axis=1).reshape(-1).astype(jnp.int32)
     length = pairs_n + CLASSES * BATCH
-    more = BATCH + -length % BATCH
-    members = jnp.pad(members[:length], (0, more), constant_values=rows_n)
-    reps = jnp.pad(reps[:length], (0, more), constant_values=rows_n)
-    return members, reps, bounds
+    return jnp.pad(codes[:length], (0, BATCH + -length % BATCH), constant_values=nobody), bounds
 
 
 def pair_lists(ids, edges, parts):
@@ -665,12 +667,11 @@
     return lax.ppermute(x, axis, [(i, (i + step) % count) for i in range(count)])
 
 
-def largest(x):
-    for axis in ("mesh", "four"):
-        step = 1
-        while step < lax.axis_size(axis):
-            x = jnp.maximum(x, shifted(x, axis, step))
-            step *= 2
+def largest_of_partitions(x):
+    step = 1
+    while step < lax.axis_size("mesh"):
+        x = jnp.maximum(x, shifted(x, "mesh", step))
+        step *= 2
     return x
 
 
@@ -685,12 +686,12 @@
     return shifted(up, "mesh", 1), shifted(low, "mesh", -1)
 
 
-def edge_takers(edges, connect_here, edge_reps):
-    here_n = connect_here.size
+def edge_takers(edges, connect, edge_reps, parts):
+    here_n = connect.size // parts
     ids = fill_up(edges, BATCH, -1)
-    has = jnp.any(ids[:, :, None] == connect_here.reshape(-1), axis=2).astype(jnp.float32)
+    has = jnp.any(ids[:, None, :, None] == connect.reshape(1, parts, 1, here_n), axis=3).astype(jnp.float32)
     theirs = jnp.stack(swap_edges(has[0], has[1]))
-    spread_out = largest(jnp.max(theirs * (1.0 - has)).reshape(1))[0] > 0.5
+    spread_out = largest_of_partitions(jnp.max(theirs * (1.0 - has)).reshape(1))[0] > 0.5
     at_rep = jnp.where(edge_reps // here_n == lax.axis_index("four"), ids, -1)
     taken = jnp.where(spread_out, at_rep, ids)
     return ids.reshape(-1, 1), taken.reshape(-1, 1), spread_out
@@ -747,7 +748,7 @@
     us0_here = derivative(u0_here, inside, 0, 1) if whole_rows else None
     mass_here = lax.dynamic_slice_in_dim(mass, mine, l_n, 0)
     connect_here = lax.dynamic_slice_in_dim(connect, mine, l_n, 0)
-    edge_ids, taken_ids, spread_out = edge_takers(edges, connect_here, edge_reps)
+    edge_ids, taken_ids, spread_out = edge_takers(edges, connect, edge_reps, parts)
     held = (here, ur_b, pairs, across, edge_reps, inverse, base, u0_here, us0_here, edge_ids, taken_ids, spread_out)
     here, ur_b, pairs, across, edge_reps, inverse, base, u0_here, us0_here, edge_ids, taken_ids, spread_out = together(held)
 

time: 1010 us -> 897 us (0.89)
  Pallas kernels: 373 us -> 258 us
  waiting for transfers between devices: 205 us -> 244 us
  starting transfers between devices: 95.3 us -> 60.6 us
    pallas_call x3, Pallas kernels: 171 us -> 57 us  [the longest x1 24.1 us: finish(): pl.pallas_call(kernel, grid=(s_n + outs,), in_specs=[smem] * 2 + [pl.Bloc...]
    all_to_all x5, waiting for transfers between devices: 190 us -> 231 us  [exchange(): return lax.all_to_all(x, 'four', split_axis=0, concat_axis=0, tiled=True)]
    ppermute x13 -> x11, starting transfers between devices: 53.6 us -> 17.7 us  [shifted(): lax.ppermute(x, axis, [(i, (i + step) % count) for i in range(count)])]
  transfers between devices with their start and end apart: 18 -> 16, of which waited for: 12 -> 12; matrix products, arithmetic and copies ran while one was open for 32% -> 36% of each run, Pallas kernels for 23% -> 25%
where the time goes in v7:
time: 897 us; the launch traced here: 881 us
  Pallas kernels  258 us (29%)
  waiting for transfers between devices  244 us (27%)
  other arithmetic  160 us (18%)
  local copies, waits for them, and re-layouts  155 us (17%)
  starting transfers between devices  60.6 us (7%)
    all_to_all x5, waiting for transfers between devices, exchange(): return lax.all_to_all(x, 'four', split_axis=0, concat_axis=0, tiled=True)  231 us
    gather x1, local copies, waits for them, and re-layouts, inverse_mass(): return (1.0 / summed[ids]).reshape(mass.shape)  90.5 us
    scatter-add x1, other arithmetic, inverse_mass(): summed = jnp.zeros((UNIQUE,), jnp.float32).at[ids].add(mass.reshape(-1))  85.8 us
    all_to_all x5, starting transfers between devices, exchange(): return lax.all_to_all(x, 'four', split_axis=0, concat_axis=0, tiled=True)  43 us
    pallas_call x4, Pallas kernels, derivative(): pl.pallas_call(kernel, grid=(c_n, m_n // rows), in_specs=[pl.BlockSpec(bl...  42.5 us
    sort x2, other arithmetic, grouped(): lax.sort((jnp.concatenate([group.astype(jnp.int32), spare_group]), jnp.co...  34.5 us
    pallas_call x1, Pallas kernels, forcing_modes(): pl.pallas_call(kernel, grid=(c_n, l_n), in_specs=[whole, whole, pl.BlockS...  32.8 us
    pallas_call x1, Pallas kernels, base_products(): pl.pallas_call(kernel, grid=(l_n,), in_specs=[pl.BlockSpec((2 * p_n, 3 *...  30.6 us
  transfers between devices with their start and end apart: 16, of which 12 were waited for; matrix products, arithmetic and copies ran while one was open for 36% of the time, Pallas kernels for 25%

profile of v7, /device:TPU:9, one launch (start us, length us, event | category | flops | bytes accessed | tf_op | source)
XLA Modules:
  0.0 881.4 jit_solution(12114464066895080050)
XLA Ops:
  0.0 10.2 %slabs.1 = f32[4,64,16,256]{3,2,1,0:T(8,128)} custom-call(f32[3,64,64,256]{3,2,1,0:T(8,128)} %x_ref.2), custom_call_target="tpu_custom_call" | custom-call | bytes 8388608 | tf_op jit(solution)/shard_map/slabs/pallas_call | solution.py:91
  10.2 4.9 all-to-all-start
  15.1 13.8 %node_major.2.x_ref.u_ref = f32[4,3,16,64,256]{4,3,2,1,0:T(8,128)} custom-call(f32[3,64,64,256]{3,2,1,0:T(8,128)} %x_ref.2), custom_call_target="tpu_custom_call" | custom-call | flops 3145728 | bytes 25165824 | tf_op jit(solution)/shard_map/node_major/pallas_call | solution.py:114
  28.9 7.7 slice.100
  36.7 7.6 line_derivative.5
  44.2 13.7 %line_derivative.4 = f32[4,2,16,64,256]{4,3,2,1,0:T(8,128)} custom-call(f32[4,3,16,64,256]{4,3,2,1,0:T(8,128)} %node_major.2.x_ref.u_ref), custom_call_target="tpu_custom_call" | custom-call | flops 33554432 | bytes 16777216 | tf_op jit(solution)/shard_map/line_derivative/pallas_call | solution.py:143
  57.9 11.7 %pad_maximum_fusion = f32[4,4,16,64,256]{4,3,2,1,0:T(8,128)} fusion(f32[4,2,16,64,256]{4,3,2,1,0:T(8,128)} %line_derivative.4, f32[4,2,16,64,256]{4,3,2,1,0:T(8,128)} %slice.100), kind=kLoop, calls=%fused_computation.10 | loop fusion | flops 4194304 | bytes 33554432 | tf_op jit(solution)/shard_map/concatenate | solution.py:733
  69.6 34.8 %all-to-all-done.x_ref = f32[4,64,16,256]{3,2,1,0:T(8,128)} async-done(((f32[4,64,16,256]{3,2,1,0:T(8,128)}), f32[4,64,16,256]{3,2,1,0:T(8,128)}, u32[]{:S(2)}, u32[]{:S(2)}) %all-to-all-start) | async-done | bytes 4194336 | tf_op jit(solution)/shard_map/all_to_all | solution.py:708
  104.4 10.4 %all-to-all-start.1 = ((f32[4,4,16,64,256]{4,3,2,1,0:T(8,128)}), f32[4,4,16,64,256]{4,3,2,1,0:T(8,128)}, u32[]{:S(2)}, u32[]{:S(2)}) async-start(f32[4,4,16,64,256]{4,3,2,1,0:T(8,128)} %pad_maximum_fusion), calls=%async_computation.1 | async-start | bytes 33554432 | tf_op jit(solution)/shard_map/all_to_all | solution.py:708
  122.6 7.1 sort.61
  146.8 85.8 %scatter_custom_fusion = f32[12825]{0:T(1024)S(1)} fusion(s32[16384]{0:T(1024)S(1)} %bitcast.137, f32[16384]{0:T(1024)S(1)} %bitcast.141, f32[]{:T(128)} %constant.157.clone.1), kind=kCustom, calls=%fused_computation.84 | custom fusion | flops 16384 | bytes 51304 | tf_op jit(solution)/shard_map/scatter-add | solution.py:701
  238.0 17.2 %sort.62 = (s32[16448]{0:T(1024)}, s32[16448]{0:T(1024)S(1)}, s32[16448]{0:T(1024)}) sort(s32[16448]{0:T(1024)S(1)} %get-tuple-element.128, s32[16448]{0:T(1024)S(1)} %concatenate.58, s32[16448]{0:T(1024)S(1)} %iota.175), dimensions={0}, to_apply=%region_3.4 | sort | flops 246720 | bytes 394752 | tf_op jit(solution)/shard_map/sort | solution.py:618
  255.2 17.3 %sort.63 = (s32[16448]{0:T(1024)}, s32[16448]{0:T(1024)S(1)}, s32[16448]{0:T(1024)}) sort(s32[16448]{0:T(1024)S(1)} %get-tuple-element.127, s32[16448]{0:T(1024)S(1)} %concatenate.58, s32[16448]{0:T(1024)S(1)} %iota.183), dimensions={0}, to_apply=%region_16.17 | sort | flops 246720 | bytes 394752 | tf_op jit(solution)/shard_map/sort | solution.py:618
  279.6 10.5 %node_major.3 = f32[1,4,16,64,256]{4,3,2,1,0:T(8,128)} custom-call(f32[4,64,16,256]{3,2,1,0:T(8,128)} %all-to-all-done.x_ref), custom_call_target="tpu_custom_call" | custom-call | flops 1048576 | bytes 8388608 | tf_op jit(solution)/shard_map/node_major/pallas_call | solution.py:114
  290.0 7.5 line_derivative.6.usa_ref
  306.7 23.3 %copy.65 = bf16[12,256,16,256]{3,1,2,0:T(8,128)(2,1)} copy(bf16[12,256,16,256]{3,2,1,0:T(8,128)(2,1)} %param.12) | data formatting | bytes 50331648 | tf_op jit(solution)/shard_map/optimization_barrier | solution.py:734
  333.4 90.5 %gather_fusion.3 = f32[16384]{0:T(1024)S(1)} fusion(f32[12825]{0:T(1024)S(1)} %scatter_fusion, s32[16384]{0:T(1024)S(1)} %broadcast_clamp_fusion), kind=kCustom, calls=%fused_computation.3 | custom fusion | bytes 196608 | tf_op jit(solution)/shard_map/gather | solution.py:704
  437.4 35.8 %all-to-all-done.1.x_ref.ub_ref.ur_ref.u_ref = f32[4,4,16,64,256]{4,3,2,1,0:T(8,128)} async-done(((f32[4,4,16,64,256]{4,3,2,1,0:T(8,128)}), f32[4,4,16,64,256]{4,3,2,1,0:T(8,128)}, u32[]{:S(2)}, u32[]{:S(2)}) %all-to-all-start.1) | async-done | bytes 16777248 | tf_op jit(solution)/shard_map/all_to_all | solution.py:708
  473.2 9.2 %all-to-all-start.2 = ((f32[4,1,16,64,256]{4,3,2,1,0:T(8,128)}), f32[4,1,16,64,256]{4,3,2,1,0:T(8,128)}, u32[]{:S(2)}, u32[]{:S(2)}) async-start(f32[4,1,16,64,256]{4,3,2,1,0:T(8,128)} %line_derivative.5), calls=%async_computation.2 | async-start | bytes 8388608 | tf_op jit(solution)/shard_map/all_to_all | solution.py:708
  483.6 13.7 %line_derivative.7.usb_ref = f32[4,2,16,64,256]{4,3,2,1,0:T(8,128)} custom-call(f32[4,4,16,64,256]{4,3,2,1,0:T(8,128)} %all-to-all-done.1.x_ref.ub_ref.ur_ref.u_ref), custom_call_target="tpu_custom_call" | custom-call | flops 33554432 | bytes 16777216 | tf_op jit(solution)/shard_map/line_derivative/pallas_call | solution.py:143
  497.3 30.6 %base_products.1 = (f32[16,256,256]{2,1,0:T(8,128)}, f32[3,16,256,256]{3,2,1,0:T(8,128)}) custom-call(bf16[512,768]{1,0:T(8,128)(2,1)} %constant.164.clone.both_ref, bf16[256,768]{1,0:T(8,128)(2,1)} %constant.165.clone.synth_ref, f32[4,1,16,64,256]{4,3,2,1,0:T(8,128)} %bitcast.132, f32[4,4,16,64,256]{4,3,2,1,0:T(8,128)} %all-to-all-done.1.x_ref.ub_ref.ur_ref.u_ref, ...), custom_call_target="tpu_custom_call" | custom-call | flops 14495514624 | bytes 67108864 | tf_op jit(solution)/shard_map/base_products/pallas_call | solution.py:200
  527.9 32.8 %forcing_modes.1 = f32[4,2,16,64,256]{4,3,2,1,0:T(8,128)} custom-call(bf16[256,768]{1,0:T(8,128)(2,1)} %constant.165.clone.synth_ref, bf16[256,768]{1,0:T(8,128)(2,1)} %constant.166.clone.analysis_ref, f32[4,4,16,64,256]{4,3,2,1,0:T(8,128)} %all-to-all-done.1.x_ref.ub_ref.ur_ref.u_ref, f32[16,256,256]{2,1,0:T(8,128)} %get-tuple-element.74.vr_ref, ...), custom_call_target="tpu_custom_call" | custom-call | flops 6442450944 | bytes 33554432 | tf_op jit(solution)/shard_map/forcing_modes/pallas_call | solution.py:242
  560.7 10.3 %all-to-all-done.2.ur_ref = f32[4,1,16,64,256]{4,3,2,1,0:T(8,128)} async-done(((f32[4,1,16,64,256]{4,3,2,1,0:T(8,128)}), f32[4,1,16,64,256]{4,3,2,1,0:T(8,128)}, u32[]{:S(2)}, u32[]{:S(2)}) %all-to-all-start.2) | async-done | bytes 4194336 | tf_op jit(solution)/shard_map/all_to_all | solution.py:708
  571.1 9.7 %all-to-all-start.3 = ((f32[4,2,16,64,256]{4,3,2,1,0:T(8,128)}), f32[4,2,16,64,256]{4,3,2,1,0:T(8,128)}, u32[]{:S(2)}, u32[]{:S(2)}) async-start(f32[4,2,16,64,256]{4,3,2,1,0:T(8,128)} %forcing_modes.1), calls=%async_computation.3 | async-start | bytes 16777216 | tf_op jit(solution)/shard_map/all_to_all | solution.py:708
  582.2 20.7 %forcing_and_rims.1 = (f32[4,1,16,64,256]{4,3,2,1,0:T(8,128)}, f32[480,256]{1,0:T(8,128)}) custom-call(bf16[256,768]{1,0:T(8,128)(2,1)} %constant.165.clone.synth_ref, bf16[256,768]{1,0:T(8,128)(2,1)} %constant.166.clone.analysis_ref, f32[4,1,16,64,256]{4,3,2,1,0:T(8,128)} %all-to-all-done.2.ur_ref, ...), custom_call_target="tpu_custom_call" | custom-call | flops 6442450944 | bytes 20971520 | tf_op jit(solution)/shard_map/forcing_and_rims/pallas_call | solution.py:297
  615.8 30.3 %own_sums.1 = f32[4,1,16,64,256]{4,3,2,1,0:T(8,128)} custom-call(f32[4,1,16,64,256]{4,3,2,1,0:T(8,128)} %get-tuple-element.79.f_ref, f32[4,4,16,64,256]{4,3,2,1,0:T(8,128)} %all-to-all-done.1.x_ref.ub_ref.ur_ref.u_ref, f32[16,256]{1,0:T(8,128)} %constant_dynamic-slice_fusion.1.mass_ref, s32[16,256]{1,0:T(8,128)} %constant_dynamic-slice_fusion.conn_ref, ...), custom_call_target="tpu_custom_call" | custom-call | flops 17179869184 | bytes 12582912 | tf_op jit(solution)/shard_map/own_sums/pallas_call | solution.py:357
  646.1 113.2 %all-to-all-done.3.f_ref = f32[4,2,16,64,256]{4,3,2,1,0:T(8,128)} async-done(((f32[4,2,16,64,256]{4,3,2,1,0:T(8,128)}), f32[4,2,16,64,256]{4,3,2,1,0:T(8,128)}, u32[]{:S(2)}, u32[]{:S(2)}) %all-to-all-start.3) | async-done | bytes 8388640 | tf_op jit(solution)/shard_map/all_to_all | solution.py:708
  759.4 8.8 all-to-all-start.4
  768.2 22.7 %local_sums.1 = (f32[16392,128]{1,0:T(8,128)}, f32[240,128]{1,0:T(8,128)}, f32[240,128]{1,0:T(8,128)}) custom-call(s32[3648]{0:T(1024)} %get-tuple-element.85.codes, s32[10]{0:T(128)} %reshape.1033.bnd, s32[2,240]{1,0:T(2,128)} %get-tuple-element.87.er, f32[4,2,16,64,256]{4,3,2,1,0:T(8,128)} %all-to-all-done.3.f_ref, ...), custom_call_target="tpu_custom_call" | custom-call | flops 838860800 | bytes 25165824 | tf_op jit(solution)/shard_map/local_sums/pallas_call | solution.py:525
  799.8 19.8 %spread.1._ = f32[3,64,64,256]{3,2,1,0:T(8,128)} custom-call(s32[3648]{0:T(1024)} %get-tuple-element.85.codes, s32[10]{0:T(128)} %reshape.1033.bnd, s32[2,240]{1,0:T(2,128)} %get-tuple-element.87.er, f32[16392,128]{1,0:T(8,128)} %get-tuple-element.90.t_ref, f32[240,128]{1,0:T(8,128)} %copy-done.4, f32[240,128]{1,0:T(8,128)} %copy-done.5, f32[64,256]{1,0:T(8,128)} %div.68.inv_ref), custom_call_target="tpu_custom_call" | custom-call | flops 838860800 | bytes 25165824 | tf_op jit(solution)/shard_map/spread/pallas_call | solution.py:591
  819.6 37.3 %all-to-all-done.4.f_ref = f32[4,1,16,64,256]{4,3,2,1,0:T(8,128)} async-done(((f32[4,1,16,64,256]{4,3,2,1,0:T(8,128)}), f32[4,1,16,64,256]{4,3,2,1,0:T(8,128)}, u32[]{:S(2)}, u32[]{:S(2)}) %all-to-all-start.4) | async-done | bytes 4194336 | tf_op jit(solution)/shard_map/all_to_all | solution.py:708
  856.9 24.1 %finish.1 = f32[3,64,64,256]{3,2,1,0:T(8,128)} custom-call(s32[3648]{0:T(1024)} %get-tuple-element.68.codes, s32[12]{0:T(128)} %reshape.1038.bnd, f32[4,1,16,64,256]{4,3,2,1,0:T(8,128)} %all-to-all-done.4.f_ref, f32[64,256]{1,0:T(8,128)} %div.68.inv_ref, f32[3,64,64,256]{3,2,1,0:T(8,128)} %spread.1._), custom_call_target="tpu_custom_call", output_to_operand_aliasing={{}: (4, {})} | custom-call | flops 838860800 | bytes 12582912 | tf_op jit(solution)/shard_map/finish/pallas_call | solution.py:464
  (145 shorter events, 84.8 us)
Async XLA Ops:
  0.0 482.4 %copy-start = (f32[4,64,256]{2,1,0:T(8,128)S(1)}, f32[4,64,256]{2,1,0:T(8,128)}, u32[]{:S(2)}) copy-start(f32[4,64,256]{2,1,0:T(8,128)} %param.13) | copy-start | bytes 786436
  10.2 94.2 %all-to-all-start = ((f32[4,64,16,256]{3,2,1,0:T(8,128)}), f32[4,64,16,256]{3,2,1,0:T(8,128)}, u32[]{:S(2)}, u32[]{:S(2)}) async-start(f32[4,64,16,256]{3,2,1,0:T(8,128)} %slabs.1), calls=%async_computation | async-start | bytes 8388608 | tf_op jit(solution)/shard_map/all_to_all | solution.py:708
  69.6 45.4 %copy-start.6 = (s32[1,2,225]{2,1,0:T(2,128)S(1)}, s32[1,2,225]{2,1,0:T(2,128)}, u32[]{:S(2)}) copy-start(s32[1,2,225]{2,1,0:T(2,128)} %param.16) | copy-start | bytes 5404
  69.6 45.5 %copy-start.2 = (s32[64,256]{1,0:T(8,128)S(1)}, s32[64,256]{1,0:T(8,128)}, u32[]{:S(2)}) copy-start(s32[64,256]{1,0:T(8,128)} %param.15) | copy-start | bytes 196612
  69.6 77.1 %copy-start.3 = (f32[64,256]{1,0:T(8,128)S(1)}, f32[64,256]{1,0:T(8,128)}, u32[]{:S(2)}) copy-start(f32[64,256]{1,0:T(8,128)} %mass_ref) | copy-start | bytes 196612
  104.4 368.7 %all-to-all-start.1 = ((f32[4,4,16,64,256]{4,3,2,1,0:T(8,128)}), f32[4,4,16,64,256]{4,3,2,1,0:T(8,128)}, u32[]{:S(2)}, u32[]{:S(2)}) async-start(f32[4,4,16,64,256]{4,3,2,1,0:T(8,128)} %pad_maximum_fusion), calls=%async_computation.1 | async-start | bytes 33554432 | tf_op jit(solution)/shard_map/all_to_all | solution.py:708
  119.4 305.3 %collective-permute-start.5 = (f32[4,240]{1,0:T(4,128)S(1)}, f32[4,240]{1,0:T(4,128)S(1)}, u32[]{:S(2)}, u32[]{:S(2)}) collective-permute-start(f32[4,240]{1,0:T(4,128)S(1)} %get-tuple-element.119), channel_id=1, source_target_pairs={{0,4},{4,8},{8,12},{12,16},{16,20},{20,24},{24,28},{28,0},{1,5},{5... | collective-permute-start | bytes 11528 | tf_op jit(solution)/shard_map/ppermute | solution.py:667
  122.3 302.3 %collective-permute-start.6 = (f32[4,240]{1,0:T(4,128)S(1)}, f32[4,240]{1,0:T(4,128)S(1)}, u32[]{:S(2)}, u32[]{:S(2)}) collective-permute-start(f32[4,240]{1,0:T(4,128)S(1)} %get-tuple-element.120), channel_id=1, source_target_pairs={{0,28},{4,0},{8,4},{12,8},{16,12},{20,16},{24,20},{28,24},{1,29},{... | collective-permute-start | bytes 11528 | tf_op jit(solution)/shard_map/ppermute | solution.py:667
  234.4 95.7 %collective-permute-start.3 = (f32[225]{0:T(256)S(1)}, f32[225]{0:T(256)S(1)}, u32[]{:S(2)}, u32[]{:S(2)}) collective-permute-start(f32[225]{0:T(256)S(1)} %gather_fusion.1), channel_id=1, source_target_pairs={{0,4},{4,8},{8,12},{12,16},{16,20},{20,24},{24,28},{28,0},{1,5},{5... | collective-permute-start | bytes 2708 | tf_op jit(solution)/shard_map/ppermute | solution.py:667
  237.9 92.2 %collective-permute-start.4 = (f32[225]{0:T(256)S(1)}, f32[225]{0:T(256)S(1)}, u32[]{:S(2)}, u32[]{:S(2)}) collective-permute-start(f32[225]{0:T(256)S(1)} %gather_fusion.2), channel_id=1, source_target_pairs={{0,28},{4,0},{8,4},{12,8},{16,12},{20,16},{24,20},{28,24},{1,29},{... | collective-permute-start | bytes 2708 | tf_op jit(solution)/shard_map/ppermute | solution.py:667
  279.6 21.9 %copy-start.7 = (pred[3648]{0:T(1024)(128)(4,1)S(1)}, pred[3648]{0:T(1024)(128)(4,1)}, u32[]{:S(2)}) copy-start(pred[3648]{0:T(1024)(128)(4,1)} %constant.135.clone.1) | copy-start | bytes 10948
  425.3 3.2 collective-permute-start.7
  429.8 3.3 collective-permute-start.8
  433.7 2.4 collective-permute-start.9
  473.2 97.9 %all-to-all-start.2 = ((f32[4,1,16,64,256]{4,3,2,1,0:T(8,128)}), f32[4,1,16,64,256]{4,3,2,1,0:T(8,128)}, u32[]{:S(2)}, u32[]{:S(2)}) async-start(f32[4,1,16,64,256]{4,3,2,1,0:T(8,128)} %line_derivative.5), calls=%async_computation.2 | async-start | bytes 8388608 | tf_op jit(solution)/shard_map/all_to_all | solution.py:708
  571.1 188.3 %all-to-all-start.3 = ((f32[4,2,16,64,256]{4,3,2,1,0:T(8,128)}), f32[4,2,16,64,256]{4,3,2,1,0:T(8,128)}, u32[]{:S(2)}, u32[]{:S(2)}) async-start(f32[4,2,16,64,256]{4,3,2,1,0:T(8,128)} %forcing_modes.1), calls=%async_computation.3 | async-start | bytes 16777216 | tf_op jit(solution)/shard_map/all_to_all | solution.py:708
  604.0 7.0 collective-permute-start.10
  606.9 7.8 collective-permute-start.11
  759.4 97.5 %all-to-all-start.4 = ((f32[4,1,16,64,256]{4,3,2,1,0:T(8,128)}), f32[4,1,16,64,256]{4,3,2,1,0:T(8,128)}, u32[]{:S(2)}, u32[]{:S(2)}) async-start(f32[4,1,16,64,256]{4,3,2,1,0:T(8,128)} %own_sums.1), calls=%async_computation.4 | async-start | bytes 8388608 | tf_op jit(solution)/shard_map/all_to_all | solution.py:708
  790.9 5.1 collective-permute-start.12
  793.7 5.4 collective-permute-start.13
  795.9 3.2 copy-start.4
  799.1 0.7 copy-start.5
  799.8 81.2 %copy-start.1 = (f32[4,64,256]{2,1,0:T(8,128)S(1)}, f32[4,64,256]{2,1,0:T(8,128)}, u32[]{:S(2)}) copy-start(f32[4,64,256]{2,1,0:T(8,128)} %param.13) | copy-start | bytes 786436

commit v8 on v7

--- a/solution.py
+++ b/solution.py
@@ -77,29 +77,6 @@
     return pltpu.CompilerParams(vmem_limit_bytes=VMEM_LIMIT, **kw)
 
 
-def slabs(x, parts):
-    _, m_n, n_n, e_n = x.shape
-    l_n = n_n // parts
-    if l_n % 8:
-        return x[0].reshape(m_n, parts, l_n, e_n).transpose(1, 0, 2, 3)
-
-    rows = m_n // 4 if m_n % 4 == 0 else m_n
-
-    def kernel(x_ref, o_ref):
-        o_ref[...] = x_ref[...]
-
-    return pl.pallas_call(
-        kernel,
-        grid=(parts, m_n // rows),
-        in_specs=[pl.BlockSpec((1, rows, l_n, e_n), lambda q, m: (0, m, q, 0))],
-        out_specs=pl.BlockSpec((1, rows, l_n, e_n), lambda q, m: (q, m, 0, 0)),
-        out_shape=jax.ShapeDtypeStruct((parts, m_n, l_n, e_n), jnp.float32),
-        compiler_params=params(),
-        cost_estimate=pl.CostEstimate(flops=0, bytes_accessed=8 * m_n * n_n * e_n, transcendentals=0),
-        name="slabs",
-    )(x)
-
-
 def node_major(x, parts):
     c_n, m_n, n_n, e_n = x.shape
     l_n = n_n // parts
@@ -378,17 +355,12 @@
 
 
 def rows_of(ref, places):
-    if len(ref.shape) == 3:
-        return [ref[r >> 3, pl.ds(r & 7, 1), :] for r in places]
     return [ref[pl.ds(r, 1), :] for r in places]
 
 
 def put_rows(ref, places, rows):
     for r, row in zip(places, rows):
-        if len(ref.shape) == 3:
-            ref[r >> 3, pl.ds(r & 7, 1), :] = row
-        else:
-            ref[pl.ds(r, 1), :] = row
+        ref[pl.ds(r, 1), :] = row
 
 
 def some_pairs(codes, at, number):
@@ -426,27 +398,33 @@
     lax.fori_loop(0, pl.cdiv(end - start, BATCH), batch, 0)
 
 
-def finish(sums, pairs, inverse, held, shape, c):
+def finish(sums, pairs, shared, inverse, held, shape, c):
     s_n, _, l_n, m_n, e_n = sums.shape
     _, _, nodes_n, _ = shape
     rows_n = nodes_n * e_n
     codes, bounds = pairs
+    batch = nodes_n // shared.shape[0]
     step = max(8, l_n)
-    tiles = e_n // 8
     outs = nodes_n // step
 
-    def kernel(codes, bnd, f_ref, inv_ref, _, o_ref, table, stage):
+    def kernel(codes, bnd, mark, f_ref, again_ref, inv_ref, _, o_ref, table, stage):
         b = pl.program_id(0)
+
+        def place(node):
+            return pl.ds(pl.multiple_of(node * e_n, e_n), e_n)
 
         @pl.when(b < s_n)
         def _():
-            for t in range(l_n):
-                node = b * l_n + t
-                table[pl.ds(node * tiles, tiles)] = f_ref[0, 0, t].T.reshape(tiles, 8, m_n)
+            for at in range(0, l_n, batch):
+
+                @pl.when(mark[(b * l_n + at) // batch] != 0)
+                def _():
+                    for t in range(at, at + batch):
+                        table[place(b * l_n + t), :] = f_ref[0, 0, t].T
 
         @pl.when(b == s_n - 1)
         def _():
-            table[nodes_n * tiles] = jnp.zeros((8, m_n), jnp.float32)
+            table[pl.ds(rows_n, 8), :] = jnp.zeros((8, m_n), jnp.float32)
             for k in range(CLASSES):
                 sum_class(table, codes, bnd[2 * k], bnd[2 * k + 1], k == 0)
             sum_rest(table, codes, bnd[2 * CLASSES], bnd[2 * CLASSES + 1])
@@ -454,32 +432,44 @@
 
         @pl.when(b >= s_n)
         def _():
-            for t in range(step):
-                n = (b - s_n) * step + t
-                rows = table[pl.ds(n * tiles, tiles)].reshape(e_n, m_n).T
-                stage[t] = rows * inv_ref[pl.ds(n, 1), :]
+            first = (b - s_n) * step
+            for at in range(0, step, batch):
+                marked = mark[(first + at) // batch] != 0
+
+                @pl.when(marked)
+                def _():
+                    for t in range(at, at + batch):
+                        n = first + t
+                        stage[t] = table[place(n), :].T * inv_ref[pl.ds(n, 1), :]
+
+                @pl.when(jnp.logical_not(marked))
+                def _():
+                    for t in range(at, at + batch):
+                        stage[t] = again_ref[t // l_n, 0, t % l_n] * inv_ref[pl.ds(first + t, 1), :]
+
             o_ref[0] = jnp.swapaxes(stage[...], 0, 1)
 
     smem = pl.BlockSpec(memory_space=pltpu.SMEM)
     return pl.pallas_call(
         kernel,
         grid=(s_n + outs,),
-        in_specs=[smem] * 2
+        in_specs=[smem] * 3
         + [
             pl.BlockSpec((1, 1, l_n, m_n, e_n), lambda b: (jnp.minimum(b, s_n - 1), 0, 0, 0, 0)),
+            pl.BlockSpec((step // l_n, 1, l_n, m_n, e_n), lambda b: (jnp.maximum(b - s_n, 0), 0, 0, 0, 0)),
             pl.BlockSpec((nodes_n, e_n), lambda b: (0, 0)),
             pl.BlockSpec(memory_space=pl.ANY),
         ],
         out_specs=pl.BlockSpec((1, m_n, step, e_n), lambda b: (c, 0, jnp.maximum(b - s_n, 0), 0)),
         out_shape=jax.ShapeDtypeStruct(shape, jnp.float32),
-        scratch_shapes=[pltpu.VMEM((nodes_n * tiles + 1, 8, m_n), jnp.float32), pltpu.VMEM((step, m_n, e_n), jnp.float32)],
-        input_output_aliases={4: 0},
+        scratch_shapes=[pltpu.VMEM((rows_n + 8, m_n), jnp.float32), pltpu.VMEM((step, m_n, e_n), jnp.float32)],
+        input_output_aliases={6: 0},
         compiler_params=params(),
         cost_estimate=pl.CostEstimate(
             flops=rows_n * LANES * 400, bytes_accessed=rows_n * m_n * 12, transcendentals=0
         ),
         name="finish",
-    )(codes, bounds, sums, inverse, held)
+    )(codes, bounds, shared, sums, sums, inverse, held)
 
 
 def local_sums(modes, u, mass, pairs, edge_reps, first):
@@ -631,7 +621,7 @@
     return jnp.pad(codes[:length], (0, BATCH + -length % BATCH), constant_values=nobody), bounds
 
 
-def pair_lists(ids, edges, parts):
+def pair_lists(ids, edges, parts, nodes_n):
     rows_n = ids.shape[0]
     place = jnp.arange(rows_n, dtype=jnp.int32)
     ids_sorted, member = lax.sort((ids, place), num_keys=1, is_stable=True)
@@ -655,11 +645,14 @@
     group = jnp.where((rank == 1) & last & (device_rank == 1), 0, group)
     group = jnp.where((rank == 0) | (most == 0), CLASSES + 2, group)
     across = grouped(group, CLASSES + 2, member, rep, pairs_n)
+    points = rows_n // nodes_n * min(8, nodes_n // parts)
+    point_group = jnp.arange(rows_n // points, dtype=jnp.int32)
+    shared = jnp.any((member // points == point_group[:, None]) & (most > 0), axis=1).astype(jnp.int32)
 
     flat = edges.reshape(-1)
     start = jnp.sum(ids_sorted[None, :] < flat[:, None], axis=1, dtype=jnp.int32)
     edge_reps = fill_up(member[start].reshape(edges.shape), BATCH, rows_n)
-    return pairs, across, edge_reps
+    return pairs, across, shared, edge_reps
 
 
 def shifted(x, axis, step):
@@ -723,7 +716,7 @@
     inside = [[(a, l + j) for j in range(NP)] for a in range(parts) for l in range(0, l_n, NP)]
     whole_rows = l_n % NP == 0
 
-    u_first = slabs(adj_modes, parts)
+    u_first = adj_modes[0].reshape(m_n, parts, l_n, e_n).transpose(1, 0, 2, 3)
     u_first, adj_modes = together((u_first, adj_modes))
     first_here = exchange(u_first)
 
@@ -738,7 +731,7 @@
     here = exchange(sent)
     edges = edge_nodes[0]
     ids = connect.reshape(-1)
-    pairs, across, edge_reps = pair_lists(ids, edges, parts)
+    pairs, across, shared, edge_reps = pair_lists(ids, edges, parts, nodes_n)
     inverse = inverse_mass(mass, ids, edges)
     base = base_flow.transpose(0, 2, 1, 3)
     if l_n % 8 == 0:
@@ -749,8 +742,8 @@
     mass_here = lax.dynamic_slice_in_dim(mass, mine, l_n, 0)
     connect_here = lax.dynamic_slice_in_dim(connect, mine, l_n, 0)
     edge_ids, taken_ids, spread_out = edge_takers(edges, connect, edge_reps, parts)
-    held = (here, ur_b, pairs, across, edge_reps, inverse, base, u0_here, us0_here, edge_ids, taken_ids, spread_out)
-    here, ur_b, pairs, across, edge_reps, inverse, base, u0_here, us0_here, edge_ids, taken_ids, spread_out = together(held)
+    held = (here, ur_b, pairs, across, shared, edge_reps, inverse, base, u0_here, us0_here, edge_ids, taken_ids, spread_out)
+    here, ur_b, pairs, across, shared, edge_reps, inverse, base, u0_here, us0_here, edge_ids, taken_ids, spread_out = together(held)
 
     ur_b_here = exchange(ur_b)
     us_here = derivative(here, inside, 0, 2) if whole_rows else here[:, 5:7]
@@ -776,7 +769,7 @@
     out = spread(table, swap_edges(*rims), pairs, edge_reps, inverse, None, adj_modes.shape, 0, 2)
     modes_b, out = together((modes_b, out))
 
-    return finish(modes_b, across, inverse, out, adj_modes.shape, 2)
+    return finish(modes_b, across, shared, inverse, out, adj_modes.shape, 2)
 
 
 def solution(mesh):

time: 897 us -> 884 us (0.986)
  Pallas kernels: 258 us -> 240 us
    pallas_call x2 -> x1, Pallas kernels: 34.3 us -> 16.5 us  [finish(): pl.pallas_call(kernel, grid=(s_n + outs,), in_specs=[smem] * 3 + [pl.Bloc...]
  transfers between devices with their start and end apart: 16 -> 16, of which waited for: 12 -> 12; matrix products, arithmetic and copies ran while one was open for 36% -> 36% of each run, Pallas kernels for 25% -> 26%
where the time goes in v8:
time: 884 us; the launch traced here: 868 us
  waiting for transfers between devices  243 us (27%)
  Pallas kernels  240 us (27%)
  other arithmetic  161 us (18%)
  local copies, waits for them, and re-layouts  160 us (18%)
  starting transfers between devices  60.6 us (7%)
    all_to_all x5, waiting for transfers between devices, exchange(): return lax.all_to_all(x, 'four', split_axis=0, concat_axis=0, tiled=True)  230 us
    gather x1, local copies, waits for them, and re-layouts, inverse_mass(): return (1.0 / summed[ids]).reshape(mass.shape)  90.5 us
    scatter-add x1, other arithmetic, inverse_mass(): summed = jnp.zeros((UNIQUE,), jnp.float32).at[ids].add(mass.reshape(-1))  85.8 us
    all_to_all x5, starting transfers between devices, exchange(): return lax.all_to_all(x, 'four', split_axis=0, concat_axis=0, tiled=True)  43 us
    pallas_call x4, Pallas kernels, derivative(): pl.pallas_call(kernel, grid=(c_n, m_n // rows), in_specs=[pl.BlockSpec(bl...  42.5 us
    sort x2, other arithmetic, grouped(): lax.sort((jnp.concatenate([group.astype(jnp.int32), spare_group]), jnp.co...  34.5 us
    pallas_call x1, Pallas kernels, forcing_modes(): pl.pallas_call(kernel, grid=(c_n, l_n), in_specs=[whole, whole, pl.BlockS...  32.8 us
    pallas_call x1, Pallas kernels, base_products(): pl.pallas_call(kernel, grid=(l_n,), in_specs=[pl.BlockSpec((2 * p_n, 3 *...  30.6 us
  transfers between devices with their start and end apart: 16, of which 12 were waited for; matrix products, arithmetic and copies ran while one was open for 36% of the time, Pallas kernels for 26%

profile of v8, /device:TPU:9, one launch (start us, length us, event | category | flops | bytes accessed | tf_op | source)
XLA Modules:
  0.0 868.5 jit_solution(15196332228844782093)
XLA Ops:
  4.8 4.9 all-to-all-start
  9.7 13.8 %node_major.2.x_ref.u_ref = f32[4,3,16,64,256]{4,3,2,1,0:T(8,128)} custom-call(f32[3,64,64,256]{3,2,1,0:T(8,128)} %x_ref), custom_call_target="tpu_custom_call" | custom-call | flops 3145728 | bytes 25165824 | tf_op jit(solution)/shard_map/node_major/pallas_call | solution.py:91
  23.5 7.7 slice.104
  31.2 7.6 line_derivative.5
  38.8 13.7 %line_derivative.4 = f32[4,2,16,64,256]{4,3,2,1,0:T(8,128)} custom-call(f32[4,3,16,64,256]{4,3,2,1,0:T(8,128)} %node_major.2.x_ref.u_ref), custom_call_target="tpu_custom_call" | custom-call | flops 33554432 | bytes 16777216 | tf_op jit(solution)/shard_map/line_derivative/pallas_call | solution.py:120
  52.5 11.7 %pad_maximum_fusion = f32[4,4,16,64,256]{4,3,2,1,0:T(8,128)} fusion(f32[4,2,16,64,256]{4,3,2,1,0:T(8,128)} %line_derivative.4, f32[4,2,16,64,256]{4,3,2,1,0:T(8,128)} %slice.104), kind=kLoop, calls=%fused_computation.10 | loop fusion | flops 4194304 | bytes 33554432 | tf_op jit(solution)/shard_map/concatenate | solution.py:726
  64.2 34.8 %all-to-all-done.x_ref = f32[4,64,16,256]{3,2,1,0:T(8,128)} async-done(((f32[4,64,16,256]{3,2,1,0:T(8,128)}), f32[4,64,16,256]{3,2,1,0:T(8,128)}, u32[]{:S(2)}, u32[]{:S(2)}) %all-to-all-start) | async-done | bytes 4194336 | tf_op jit(solution)/shard_map/all_to_all | solution.py:701
  99.0 10.4 %all-to-all-start.1 = ((f32[4,4,16,64,256]{4,3,2,1,0:T(8,128)}), f32[4,4,16,64,256]{4,3,2,1,0:T(8,128)}, u32[]{:S(2)}, u32[]{:S(2)}) async-start(f32[4,4,16,64,256]{4,3,2,1,0:T(8,128)} %pad_maximum_fusion), calls=%async_computation.1 | async-start | bytes 33554432 | tf_op jit(solution)/shard_map/all_to_all | solution.py:701
  109.9 4.1 compare_reduce_fusion
  117.2 7.1 sort.61
  141.4 85.8 %scatter_custom_fusion = f32[12825]{0:T(1024)S(1)} fusion(s32[16384]{0:T(1024)S(1)} %bitcast.147, f32[16384]{0:T(1024)S(1)} %bitcast.151, f32[]{:T(128)} %constant.171.clone.1), kind=kCustom, calls=%fused_computation.94 | custom fusion | flops 16384 | bytes 51304 | tf_op jit(solution)/shard_map/scatter-add | solution.py:694
  232.6 17.2 %sort.62 = (s32[16448]{0:T(1024)}, s32[16448]{0:T(1024)S(1)}, s32[16448]{0:T(1024)}) sort(s32[16448]{0:T(1024)S(1)} %get-tuple-element.131, s32[16448]{0:T(1024)S(1)} %concatenate.58, s32[16448]{0:T(1024)S(1)} %iota.179), dimensions={0}, to_apply=%region_3.4 | sort | flops 246720 | bytes 394752 | tf_op jit(solution)/shard_map/sort | solution.py:608
  249.8 17.2 %sort.63 = (s32[16448]{0:T(1024)}, s32[16448]{0:T(1024)S(1)}, s32[16448]{0:T(1024)}) sort(s32[16448]{0:T(1024)S(1)} %get-tuple-element.130, s32[16448]{0:T(1024)S(1)} %concatenate.58, s32[16448]{0:T(1024)S(1)} %iota.187), dimensions={0}, to_apply=%region_16.17 | sort | flops 246720 | bytes 394752 | tf_op jit(solution)/shard_map/sort | solution.py:608
  274.2 10.5 %node_major.3 = f32[1,4,16,64,256]{4,3,2,1,0:T(8,128)} custom-call(f32[4,64,16,256]{3,2,1,0:T(8,128)} %all-to-all-done.x_ref), custom_call_target="tpu_custom_call" | custom-call | flops 1048576 | bytes 8388608 | tf_op jit(solution)/shard_map/node_major/pallas_call | solution.py:91
  284.7 7.5 line_derivative.6.usa_ref
  302.4 23.3 %copy.68 = bf16[12,256,16,256]{3,1,2,0:T(8,128)(2,1)} copy(bf16[12,256,16,256]{3,2,1,0:T(8,128)(2,1)} %param.12) | data formatting | bytes 50331648 | tf_op jit(solution)/shard_map/optimization_barrier | solution.py:727
  329.1 90.5 %gather_fusion.3 = f32[16384]{0:T(1024)S(1)} fusion(f32[12825]{0:T(1024)S(1)} %scatter_fusion, s32[16384]{0:T(1024)S(1)} %broadcast_clamp_fusion), kind=kCustom, calls=%fused_computation.3 | custom fusion | bytes 196608 | tf_op jit(solution)/shard_map/gather | solution.py:697
  433.1 34.7 %all-to-all-done.1.x_ref.ub_ref.ur_ref.u_ref = f32[4,4,16,64,256]{4,3,2,1,0:T(8,128)} async-done(((f32[4,4,16,64,256]{4,3,2,1,0:T(8,128)}), f32[4,4,16,64,256]{4,3,2,1,0:T(8,128)}, u32[]{:S(2)}, u32[]{:S(2)}) %all-to-all-start.1) | async-done | bytes 16777248 | tf_op jit(solution)/shard_map/all_to_all | solution.py:701
  467.8 9.2 %all-to-all-start.2 = ((f32[4,1,16,64,256]{4,3,2,1,0:T(8,128)}), f32[4,1,16,64,256]{4,3,2,1,0:T(8,128)}, u32[]{:S(2)}, u32[]{:S(2)}) async-start(f32[4,1,16,64,256]{4,3,2,1,0:T(8,128)} %line_derivative.5), calls=%async_computation.2 | async-start | bytes 8388608 | tf_op jit(solution)/shard_map/all_to_all | solution.py:701
  478.2 13.7 %line_derivative.7.usb_ref = f32[4,2,16,64,256]{4,3,2,1,0:T(8,128)} custom-call(f32[4,4,16,64,256]{4,3,2,1,0:T(8,128)} %all-to-all-done.1.x_ref.ub_ref.ur_ref.u_ref), custom_call_target="tpu_custom_call" | custom-call | flops 33554432 | bytes 16777216 | tf_op jit(solution)/shard_map/line_derivative/pallas_call | solution.py:120
  491.9 30.6 %base_products.1 = (f32[16,256,256]{2,1,0:T(8,128)}, f32[3,16,256,256]{3,2,1,0:T(8,128)}) custom-call(bf16[512,768]{1,0:T(8,128)(2,1)} %constant.177.clone.both_ref, bf16[256,768]{1,0:T(8,128)(2,1)} %constant.178.clone.synth_ref, f32[4,1,16,64,256]{4,3,2,1,0:T(8,128)} %bitcast.140, f32[4,4,16,64,256]{4,3,2,1,0:T(8,128)} %all-to-all-done.1.x_ref.ub_ref.ur_ref.u_ref, ...), custom_call_target="tpu_custom_call" | custom-call | flops 14495514624 | bytes 67108864 | tf_op jit(solution)/shard_map/base_products/pallas_call | solution.py:177
  522.5 32.8 %forcing_modes.1 = f32[4,2,16,64,256]{4,3,2,1,0:T(8,128)} custom-call(bf16[256,768]{1,0:T(8,128)(2,1)} %constant.178.clone.synth_ref, bf16[256,768]{1,0:T(8,128)(2,1)} %constant.179.clone.analysis_ref, f32[4,4,16,64,256]{4,3,2,1,0:T(8,128)} %all-to-all-done.1.x_ref.ub_ref.ur_ref.u_ref, f32[16,256,256]{2,1,0:T(8,128)} %get-tuple-element.76.vr_ref, ...), custom_call_target="tpu_custom_call" | custom-call | flops 6442450944 | bytes 33554432 | tf_op jit(solution)/shard_map/forcing_modes/pallas_call | solution.py:219
  555.3 10.3 %all-to-all-done.2.ur_ref = f32[4,1,16,64,256]{4,3,2,1,0:T(8,128)} async-done(((f32[4,1,16,64,256]{4,3,2,1,0:T(8,128)}), f32[4,1,16,64,256]{4,3,2,1,0:T(8,128)}, u32[]{:S(2)}, u32[]{:S(2)}) %all-to-all-start.2) | async-done | bytes 4194336 | tf_op jit(solution)/shard_map/all_to_all | solution.py:701
  565.6 9.7 %all-to-all-start.3 = ((f32[4,2,16,64,256]{4,3,2,1,0:T(8,128)}), f32[4,2,16,64,256]{4,3,2,1,0:T(8,128)}, u32[]{:S(2)}, u32[]{:S(2)}) async-start(f32[4,2,16,64,256]{4,3,2,1,0:T(8,128)} %forcing_modes.1), calls=%async_computation.3 | async-start | bytes 16777216 | tf_op jit(solution)/shard_map/all_to_all | solution.py:701
  576.8 20.7 %forcing_and_rims.1 = (f32[4,1,16,64,256]{4,3,2,1,0:T(8,128)}, f32[480,256]{1,0:T(8,128)}) custom-call(bf16[256,768]{1,0:T(8,128)(2,1)} %constant.178.clone.synth_ref, bf16[256,768]{1,0:T(8,128)(2,1)} %constant.179.clone.analysis_ref, f32[4,1,16,64,256]{4,3,2,1,0:T(8,128)} %all-to-all-done.2.ur_ref, ...), custom_call_target="tpu_custom_call" | custom-call | flops 6442450944 | bytes 20971520 | tf_op jit(solution)/shard_map/forcing_and_rims/pallas_call | solution.py:274
  610.4 30.3 %own_sums.1 = f32[4,1,16,64,256]{4,3,2,1,0:T(8,128)} custom-call(f32[4,1,16,64,256]{4,3,2,1,0:T(8,128)} %get-tuple-element.81.f_ref, f32[4,4,16,64,256]{4,3,2,1,0:T(8,128)} %all-to-all-done.1.x_ref.ub_ref.ur_ref.u_ref, f32[16,256]{1,0:T(8,128)} %constant_dynamic-slice_fusion.1.mass_ref, s32[16,256]{1,0:T(8,128)} %constant_dynamic-slice_fusion.conn_ref, ...), custom_call_target="tpu_custom_call" | custom-call | flops 17179869184 | bytes 12582912 | tf_op jit(solution)/shard_map/own_sums/pallas_call | solution.py:334
  640.7 113.2 %all-to-all-done.3.f_ref = f32[4,2,16,64,256]{4,3,2,1,0:T(8,128)} async-done(((f32[4,2,16,64,256]{4,3,2,1,0:T(8,128)}), f32[4,2,16,64,256]{4,3,2,1,0:T(8,128)}, u32[]{:S(2)}, u32[]{:S(2)}) %all-to-all-start.3) | async-done | bytes 8388640 | tf_op jit(solution)/shard_map/all_to_all | solution.py:701
  753.9 8.8 %all-to-all-start.4 = ((f32[4,1,16,64,256]{4,3,2,1,0:T(8,128)}), f32[4,1,16,64,256]{4,3,2,1,0:T(8,128)}, u32[]{:S(2)}, u32[]{:S(2)}) async-start(f32[4,1,16,64,256]{4,3,2,1,0:T(8,128)} %own_sums.1), calls=%async_computation.4 | async-start | bytes 8388608 | tf_op jit(solution)/shard_map/all_to_all | solution.py:701
  762.8 22.7 %local_sums.1 = (f32[16392,128]{1,0:T(8,128)}, f32[240,128]{1,0:T(8,128)}, f32[240,128]{1,0:T(8,128)}) custom-call(s32[3648]{0:T(1024)} %get-tuple-element.87.codes, s32[10]{0:T(128)} %reshape.1055.bnd, s32[2,240]{1,0:T(2,128)} %get-tuple-element.89.er, f32[4,2,16,64,256]{4,3,2,1,0:T(8,128)} %all-to-all-done.3.f_ref, ...), custom_call_target="tpu_custom_call" | custom-call | flops 838860800 | bytes 25165824 | tf_op jit(solution)/shard_map/local_sums/pallas_call | solution.py:515
  794.4 19.7 %spread.1._ = f32[3,64,64,256]{3,2,1,0:T(8,128)} custom-call(s32[3648]{0:T(1024)} %get-tuple-element.87.codes, s32[10]{0:T(128)} %reshape.1055.bnd, s32[2,240]{1,0:T(2,128)} %get-tuple-element.89.er, f32[16392,128]{1,0:T(8,128)} %get-tuple-element.92.t_ref, f32[240,128]{1,0:T(8,128)} %copy-done.4, f32[240,128]{1,0:T(8,128)} %copy-done.5, f32[64,256]{1,0:T(8,128)} %div.82.inv_ref), custom_call_target="tpu_custom_call" | custom-call | flops 838860800 | bytes 25165824 | tf_op jit(solution)/shard_map/spread/pallas_call | solution.py:581
  814.1 37.3 %all-to-all-done.4.f_ref.again_ref = f32[4,1,16,64,256]{4,3,2,1,0:T(8,128)} async-done(((f32[4,1,16,64,256]{4,3,2,1,0:T(8,128)}), f32[4,1,16,64,256]{4,3,2,1,0:T(8,128)}, u32[]{:S(2)}, u32[]{:S(2)}) %all-to-all-start.4) | async-done | bytes 4194336 | tf_op jit(solution)/shard_map/all_to_all | solution.py:701
  851.5 16.5 %finish.1 = f32[3,64,64,256]{3,2,1,0:T(8,128)} custom-call(s32[3648]{0:T(1024)} %get-tuple-element.69.codes, s32[12]{0:T(128)} %reshape.1060.bnd, s32[8]{0:T(128)} %convert_element_type.105.mark, f32[4,1,16,64,256]{4,3,2,1,0:T(8,128)} %all-to-all-done.4.f_ref.again_ref, ...), custom_call_target="tpu_custom_call", output_to_operand_aliasing={{}: (6, {})} | custom-call | flops 838860800 | bytes 12582912 | tf_op jit(solution)/shard_map/finish/pallas_call | solution.py:453
  (150 shorter events, 86.6 us)
Async XLA Ops:
  0.0 477.0 %copy-start = (f32[4,64,256]{2,1,0:T(8,128)S(1)}, f32[4,64,256]{2,1,0:T(8,128)}, u32[]{:S(2)}) copy-start(f32[4,64,256]{2,1,0:T(8,128)} %param.13) | copy-start | bytes 786436
  0.0 2.3 slice-start
  4.8 94.2 %all-to-all-start = ((f32[4,64,16,256]{3,2,1,0:T(8,128)}), f32[4,64,16,256]{3,2,1,0:T(8,128)}, u32[]{:S(2)}, u32[]{:S(2)}) async-start(f32[4,64,16,256]{3,2,1,0:T(8,128)} %bitcast.142), calls=%async_computation | async-start | bytes 8388608 | tf_op jit(solution)/shard_map/all_to_all | solution.py:701
  64.2 45.4 %copy-start.6 = (s32[1,2,225]{2,1,0:T(2,128)S(1)}, s32[1,2,225]{2,1,0:T(2,128)}, u32[]{:S(2)}) copy-start(s32[1,2,225]{2,1,0:T(2,128)} %param.16) | copy-start | bytes 5404
  64.2 45.5 %copy-start.2 = (s32[64,256]{1,0:T(8,128)S(1)}, s32[64,256]{1,0:T(8,128)}, u32[]{:S(2)}) copy-start(s32[64,256]{1,0:T(8,128)} %param.15) | copy-start | bytes 196612
  64.2 77.1 %copy-start.3 = (f32[64,256]{1,0:T(8,128)S(1)}, f32[64,256]{1,0:T(8,128)}, u32[]{:S(2)}) copy-start(f32[64,256]{1,0:T(8,128)} %mass_ref) | copy-start | bytes 196612
  99.0 368.7 %all-to-all-start.1 = ((f32[4,4,16,64,256]{4,3,2,1,0:T(8,128)}), f32[4,4,16,64,256]{4,3,2,1,0:T(8,128)}, u32[]{:S(2)}, u32[]{:S(2)}) async-start(f32[4,4,16,64,256]{4,3,2,1,0:T(8,128)} %pad_maximum_fusion), calls=%async_computation.1 | async-start | bytes 33554432 | tf_op jit(solution)/shard_map/all_to_all | solution.py:701
  114.0 306.4 %collective-permute-start.5 = (f32[4,240]{1,0:T(4,128)S(1)}, f32[4,240]{1,0:T(4,128)S(1)}, u32[]{:S(2)}, u32[]{:S(2)}) collective-permute-start(f32[4,240]{1,0:T(4,128)S(1)} %get-tuple-element.122), channel_id=1, source_target_pairs={{0,4},{4,8},{8,12},{12,16},{16,20},{20,24},{24,28},{28,0},{1,5},{5... | collective-permute-start | bytes 11528 | tf_op jit(solution)/shard_map/ppermute | solution.py:660
  116.9 303.4 %collective-permute-start.6 = (f32[4,240]{1,0:T(4,128)S(1)}, f32[4,240]{1,0:T(4,128)S(1)}, u32[]{:S(2)}, u32[]{:S(2)}) collective-permute-start(f32[4,240]{1,0:T(4,128)S(1)} %get-tuple-element.123), channel_id=1, source_target_pairs={{0,28},{4,0},{8,4},{12,8},{16,12},{20,16},{24,20},{28,24},{1,29},{... | collective-permute-start | bytes 11528 | tf_op jit(solution)/shard_map/ppermute | solution.py:660
  229.0 96.8 %collective-permute-start.3 = (f32[225]{0:T(256)S(1)}, f32[225]{0:T(256)S(1)}, u32[]{:S(2)}, u32[]{:S(2)}) collective-permute-start(f32[225]{0:T(256)S(1)} %gather_fusion.1), channel_id=1, source_target_pairs={{0,4},{4,8},{8,12},{12,16},{16,20},{20,24},{24,28},{28,0},{1,5},{5... | collective-permute-start | bytes 2708 | tf_op jit(solution)/shard_map/ppermute | solution.py:660
  232.5 93.3 %collective-permute-start.4 = (f32[225]{0:T(256)S(1)}, f32[225]{0:T(256)S(1)}, u32[]{:S(2)}, u32[]{:S(2)}) collective-permute-start(f32[225]{0:T(256)S(1)} %gather_fusion.2), channel_id=1, source_target_pairs={{0,28},{4,0},{8,4},{12,8},{16,12},{20,16},{24,20},{28,24},{1,29},{... | collective-permute-start | bytes 2708 | tf_op jit(solution)/shard_map/ppermute | solution.py:660
  274.2 22.4 %copy-start.7 = (pred[3648]{0:T(1024)(128)(4,1)S(1)}, pred[3648]{0:T(1024)(128)(4,1)}, u32[]{:S(2)}) copy-start(pred[3648]{0:T(1024)(128)(4,1)} %constant.146.clone.1) | copy-start | bytes 10948
  421.0 3.2 collective-permute-start.7
  425.5 3.3 collective-permute-start.8
  429.4 2.4 collective-permute-start.9
  467.8 97.9 %all-to-all-start.2 = ((f32[4,1,16,64,256]{4,3,2,1,0:T(8,128)}), f32[4,1,16,64,256]{4,3,2,1,0:T(8,128)}, u32[]{:S(2)}, u32[]{:S(2)}) async-start(f32[4,1,16,64,256]{4,3,2,1,0:T(8,128)} %line_derivative.5), calls=%async_computation.2 | async-start | bytes 8388608 | tf_op jit(solution)/shard_map/all_to_all | solution.py:701
  565.6 188.3 %all-to-all-start.3 = ((f32[4,2,16,64,256]{4,3,2,1,0:T(8,128)}), f32[4,2,16,64,256]{4,3,2,1,0:T(8,128)}, u32[]{:S(2)}, u32[]{:S(2)}) async-start(f32[4,2,16,64,256]{4,3,2,1,0:T(8,128)} %forcing_modes.1), calls=%async_computation.3 | async-start | bytes 16777216 | tf_op jit(solution)/shard_map/all_to_all | solution.py:701
  598.6 7.0 collective-permute-start.10
  601.5 7.8 collective-permute-start.11
  753.9 97.5 %all-to-all-start.4 = ((f32[4,1,16,64,256]{4,3,2,1,0:T(8,128)}), f32[4,1,16,64,256]{4,3,2,1,0:T(8,128)}, u32[]{:S(2)}, u32[]{:S(2)}) async-start(f32[4,1,16,64,256]{4,3,2,1,0:T(8,128)} %own_sums.1), calls=%async_computation.4 | async-start | bytes 8388608 | tf_op jit(solution)/shard_map/all_to_all | solution.py:701
  785.4 5.1 collective-permute-start.12
  788.3 5.4 collective-permute-start.13
  790.5 3.2 copy-start.4
  793.7 0.7 copy-start.5
  851.5 16.6 %copy-start.1 = (f32[4,64,256]{2,1,0:T(8,128)S(1)}, f32[4,64,256]{2,1,0:T(8,128)}, u32[]{:S(2)}) copy-start(f32[4,64,256]{2,1,0:T(8,128)} %param.13) | copy-start | bytes 786436

commit v9 on v8

--- a/solution.py
+++ b/solution.py
@@ -14,9 +14,10 @@
 UNIQUE = 12825
 STEP_SIZE = 0.1
 LANES = 128
-BATCH = 16
+BATCH = 32
 CLASSES = 4
 PACK = 15
+BITS = 14
 VMEM_LIMIT = 56 * 1024 * 1024
 
 
@@ -311,10 +312,13 @@
 
         @pl.when(l == 0)
         def _():
-            for k in range(l_n):
-                weighted = f_ref[:, 0, k] + mass_ref[k : k + 1, :] * u_ref[:, 0, k]
+            def hold(k, _):
+                weighted = f_ref[:, 0, k] + mass_ref[pl.ds(k, 1), :] * u_ref[:, 0, k]
                 high, low = split(weighted.reshape(coefs, e_n))
                 held[k] = jnp.concatenate([high, low], axis=1)
+                return 0
+
+            lax.fori_loop(0, l_n, hold, 0)
 
         mine = conn_ref[pl.ds(l, 1), :]
 
@@ -324,8 +328,7 @@
 
         high, low = split(rim_ref[...])
         total = product(jnp.concatenate([high, low], axis=1), same(id_ref[...]))
-        for k in range(l_n):
-            total = total + product(held[k], same(turned_ref[k]))
+        total = lax.fori_loop(0, l_n, lambda k, t: t + product(held[k], same(turned_ref[k])), total)
         o_ref[:, 0, 0] = total.reshape(s_n, m_n, e_n)
 
     def whole(*shape):
@@ -602,29 +605,28 @@
 
 def grouped(group, classes, member, rep, pairs_n):
     rows_n = group.shape[0]
-    assert rows_n < 1 << PACK
+    assert rows_n <= 1 << BITS and classes < 8
+    ones = (1 << 2 * BITS) - 1
     nobody = rows_n * (1 << PACK) + rows_n
-    spare_group = jnp.arange(CLASSES * BATCH, dtype=jnp.int32) // BATCH
-    _, codes = lax.sort(
-        (
-            jnp.concatenate([group.astype(jnp.int32), spare_group]),
-            jnp.concatenate([member * (1 << PACK) + rep, jnp.full((CLASSES * BATCH,), nobody, jnp.int32)]),
-        ),
-        num_keys=1,
-        is_stable=True,
-    )
+    spare = (jnp.arange(CLASSES * BATCH, dtype=jnp.int32) // BATCH) * (ones + 1) + ones
+    keys = group.astype(jnp.int32) * (ones + 1) + member * (1 << BITS) + rep
+    length = pairs_n + CLASSES * BATCH
+    keys = lax.sort(jnp.concatenate([keys, spare]), is_stable=False)[:length] & ones
+    codes = jnp.where(keys == ones, nobody, (keys >> BITS) * (1 << PACK) + (keys & (1 << BITS) - 1))
     spares = BATCH * jnp.minimum(jnp.arange(classes, dtype=jnp.int32), CLASSES)
-    numbers = jnp.stack([jnp.sum(group == k, dtype=jnp.int32) for k in range(classes)])
-    starts = jnp.cumsum(numbers) - numbers + spares
+    numbers = jnp.sum(group[None, :] == jnp.arange(classes, dtype=jnp.int32)[:, None], axis=1, dtype=jnp.int32)
+    lower = jnp.tri(classes, k=-1, dtype=jnp.int32)
+    starts = jnp.sum(lower * numbers[None, :], axis=1) + spares
     bounds = jnp.stack([starts, numbers], axis=1).reshape(-1).astype(jnp.int32)
-    length = pairs_n + CLASSES * BATCH
-    return jnp.pad(codes[:length], (0, BATCH + -length % BATCH), constant_values=nobody), bounds
+    return jnp.pad(codes, (0, BATCH + -length % BATCH), constant_values=nobody), bounds
 
 
 def pair_lists(ids, edges, parts, nodes_n):
     rows_n = ids.shape[0]
     place = jnp.arange(rows_n, dtype=jnp.int32)
-    ids_sorted, member = lax.sort((ids, place), num_keys=1, is_stable=True)
+    assert rows_n <= 1 << BITS and UNIQUE <= 1 << BITS
+    keys = lax.sort(ids * (1 << BITS) + place, is_stable=False)
+    ids_sorted, member = keys >> BITS, keys & (1 << BITS) - 1
     yes = jnp.ones((1,), bool)
     head = jnp.concatenate([yes, ids_sorted[1:] != ids_sorted[:-1]])
     last = jnp.concatenate([head[1:], yes])

time: 884 us -> 886 us (level)
  Pallas kernels: 240 us -> 308 us
  waiting for transfers between devices: 243 us -> 208 us
  other arithmetic: 161 us -> 142 us
  local copies, waits for them, and re-layouts: 160 us -> 147 us
    pallas_call x1, Pallas kernels: 30.3 us -> 92.9 us  [own_sums(): pl.pallas_call(kernel, grid=(l_n,), in_specs=[whole(s_n, 1, l_n, m_n, e_n...]
    all_to_all x5, waiting for transfers between devices: 230 us -> 195 us  [exchange(): return lax.all_to_all(x, 'four', split_axis=0, concat_axis=0, tiled=True)]
    sort x3, other arithmetic: 41.6 us -> 24 us  [the longest x2 17.7 us: grouped(): lax.sort(jnp.concatenate([keys, spare]), is_stable=False)[:length] & ones]
    another operation x16 -> x10, local copies, waits for them, and re-layouts: 14.9 us -> 0.78 us  [the longest x4 14.1 us: grouped(): jnp.stack([jnp.sum(group == k, dtype=jnp.int32) for k in range(classes)])]
  transfers between devices with their start and end apart: 16 -> 16, of which waited for: 12 -> 12; matrix products, arithmetic and copies ran while one was open for 36% -> 33% of each run, Pallas kernels for 26% -> 33%
where the time goes in v9:
time: 886 us; the launch traced here: 870 us
  Pallas kernels  308 us (35%)
  waiting for transfers between devices  208 us (23%)
  local copies, waits for them, and re-layouts  147 us (17%)
  other arithmetic  142 us (16%)
  starting transfers between devices  61.1 us (7%)
    all_to_all x5, waiting for transfers between devices, exchange(): return lax.all_to_all(x, 'four', split_axis=0, concat_axis=0, tiled=True)  195 us
    pallas_call x1, Pallas kernels, own_sums(): pl.pallas_call(kernel, grid=(l_n,), in_specs=[whole(s_n, 1, l_n, m_n, e_n...  92.9 us
    gather x1, local copies, waits for them, and re-layouts, inverse_mass(): return (1.0 / summed[ids]).reshape(mass.shape)  90.5 us
    scatter-add x1, other arithmetic, inverse_mass(): summed = jnp.zeros((UNIQUE,), jnp.float32).at[ids].add(mass.reshape(-1))  85.8 us
    all_to_all x5, starting transfers between devices, exchange(): return lax.all_to_all(x, 'four', split_axis=0, concat_axis=0, tiled=True)  43 us
    pallas_call x4, Pallas kernels, derivative(): pl.pallas_call(kernel, grid=(c_n, m_n // rows), in_specs=[pl.BlockSpec(bl...  42.5 us
    pallas_call x1, Pallas kernels, forcing_modes(): pl.pallas_call(kernel, grid=(c_n, l_n), in_specs=[whole, whole, pl.BlockS...  32.8 us
    pallas_call x1, Pallas kernels, base_products(): pl.pallas_call(kernel, grid=(l_n,), in_specs=[pl.BlockSpec((2 * p_n, 3 *...  30.6 us
  transfers between devices with their start and end apart: 16, of which 12 were waited for; matrix products, arithmetic and copies ran while one was open for 33% of the time, Pallas kernels for 33%

profile of v9, /device:TPU:9, one launch (start us, length us, event | category | flops | bytes accessed | tf_op | source)
XLA Modules:
  0.0 870.1 jit_solution(5067330603363316543)
XLA Ops:
  4.8 4.9 all-to-all-start
  9.7 13.8 %node_major.2.x_ref.u_ref = f32[4,3,16,64,256]{4,3,2,1,0:T(8,128)} custom-call(f32[3,64,64,256]{3,2,1,0:T(8,128)} %x_ref), custom_call_target="tpu_custom_call" | custom-call | flops 3145728 | bytes 25165824 | tf_op jit(solution)/shard_map/node_major/pallas_call | solution.py:92
  23.5 7.7 slice.102
  31.2 7.6 line_derivative.5
  38.8 13.7 %line_derivative.4 = f32[4,2,16,64,256]{4,3,2,1,0:T(8,128)} custom-call(f32[4,3,16,64,256]{4,3,2,1,0:T(8,128)} %node_major.2.x_ref.u_ref), custom_call_target="tpu_custom_call" | custom-call | flops 33554432 | bytes 16777216 | tf_op jit(solution)/shard_map/line_derivative/pallas_call | solution.py:121
  52.5 11.7 %pad_maximum_fusion = f32[4,4,16,64,256]{4,3,2,1,0:T(8,128)} fusion(f32[4,2,16,64,256]{4,3,2,1,0:T(8,128)} %line_derivative.4, f32[4,2,16,64,256]{4,3,2,1,0:T(8,128)} %slice.102), kind=kLoop, calls=%fused_computation.10 | loop fusion | flops 4194304 | bytes 33554432 | tf_op jit(solution)/shard_map/concatenate | solution.py:728
  64.2 34.8 %all-to-all-done.x_ref = f32[4,64,16,256]{3,2,1,0:T(8,128)} async-done(((f32[4,64,16,256]{3,2,1,0:T(8,128)}), f32[4,64,16,256]{3,2,1,0:T(8,128)}, u32[]{:S(2)}, u32[]{:S(2)}) %all-to-all-start) | async-done | bytes 4194336 | tf_op jit(solution)/shard_map/all_to_all | solution.py:703
  99.0 10.4 %all-to-all-start.1 = ((f32[4,4,16,64,256]{4,3,2,1,0:T(8,128)}), f32[4,4,16,64,256]{4,3,2,1,0:T(8,128)}, u32[]{:S(2)}, u32[]{:S(2)}) async-start(f32[4,4,16,64,256]{4,3,2,1,0:T(8,128)} %pad_maximum_fusion), calls=%async_computation.1 | async-start | bytes 33554432 | tf_op jit(solution)/shard_map/all_to_all | solution.py:703
  109.7 4.3 compare_reduce_fusion
  117.5 6.3 sort.21
  131.9 8.9 %sort.22 = s32[16512]{0:T(1024)S(1)} sort(s32[16512]{0:T(1024)S(1)} %get-tuple-element.108), dimensions={0}, to_apply=%region_3.4 | sort | flops 247680 | bytes 132096 | tf_op jit(solution)/shard_map/sort | solution.py:614
  140.8 8.8 %sort.23 = s32[16512]{0:T(1024)S(1)} sort(s32[16512]{0:T(1024)S(1)} %get-tuple-element.107), dimensions={0}, to_apply=%region_12.13 | sort | flops 247680 | bytes 132096 | tf_op jit(solution)/shard_map/sort | solution.py:614
  149.8 85.8 %scatter_custom_fusion = f32[12825]{0:T(1024)S(1)} fusion(s32[16384]{0:T(1024)S(1)} %bitcast.132, f32[16384]{0:T(1024)S(1)} %bitcast.136, f32[]{:T(128)} %constant.167.clone.1), kind=kCustom, calls=%fused_computation.85 | custom fusion | flops 16384 | bytes 51304 | tf_op jit(solution)/shard_map/scatter-add | solution.py:696
  241.1 10.5 %node_major.3 = f32[1,4,16,64,256]{4,3,2,1,0:T(8,128)} custom-call(f32[4,64,16,256]{3,2,1,0:T(8,128)} %all-to-all-done.x_ref), custom_call_target="tpu_custom_call" | custom-call | flops 1048576 | bytes 8388608 | tf_op jit(solution)/shard_map/node_major/pallas_call | solution.py:92
  256.7 7.6 line_derivative.6.usa_ref
  270.6 23.3 %copy.68 = bf16[12,256,16,256]{3,1,2,0:T(8,128)(2,1)} copy(bf16[12,256,16,256]{3,2,1,0:T(8,128)(2,1)} %param.12) | data formatting | bytes 50331648 | tf_op jit(solution)/shard_map/optimization_barrier | solution.py:729
  297.3 90.5 %gather_fusion.3 = f32[16384]{0:T(1024)S(1)} fusion(f32[12825]{0:T(1024)S(1)} %scatter_fusion, s32[16384]{0:T(1024)S(1)} %broadcast_clamp_fusion), kind=kCustom, calls=%fused_computation.3 | custom fusion | bytes 196608 | tf_op jit(solution)/shard_map/gather | solution.py:699
  401.2 66.5 %all-to-all-done.1.x_ref.ub_ref.ur_ref.u_ref = f32[4,4,16,64,256]{4,3,2,1,0:T(8,128)} async-done(((f32[4,4,16,64,256]{4,3,2,1,0:T(8,128)}), f32[4,4,16,64,256]{4,3,2,1,0:T(8,128)}, u32[]{:S(2)}, u32[]{:S(2)}) %all-to-all-start.1) | async-done | bytes 16777248 | tf_op jit(solution)/shard_map/all_to_all | solution.py:703
  467.8 8.9 %all-to-all-start.2 = ((f32[4,1,16,64,256]{4,3,2,1,0:T(8,128)}), f32[4,1,16,64,256]{4,3,2,1,0:T(8,128)}, u32[]{:S(2)}, u32[]{:S(2)}) async-start(f32[4,1,16,64,256]{4,3,2,1,0:T(8,128)} %line_derivative.5), calls=%async_computation.2 | async-start | bytes 8388608 | tf_op jit(solution)/shard_map/all_to_all | solution.py:703
  477.9 13.7 %line_derivative.7.usb_ref = f32[4,2,16,64,256]{4,3,2,1,0:T(8,128)} custom-call(f32[4,4,16,64,256]{4,3,2,1,0:T(8,128)} %all-to-all-done.1.x_ref.ub_ref.ur_ref.u_ref), custom_call_target="tpu_custom_call" | custom-call | flops 33554432 | bytes 16777216 | tf_op jit(solution)/shard_map/line_derivative/pallas_call | solution.py:121
  491.6 30.6 %base_products.1 = (f32[16,256,256]{2,1,0:T(8,128)}, f32[3,16,256,256]{3,2,1,0:T(8,128)}) custom-call(bf16[512,768]{1,0:T(8,128)(2,1)} %constant.174.clone.both_ref, bf16[256,768]{1,0:T(8,128)(2,1)} %constant.175.clone.synth_ref, f32[4,1,16,64,256]{4,3,2,1,0:T(8,128)} %bitcast.126, f32[4,4,16,64,256]{4,3,2,1,0:T(8,128)} %all-to-all-done.1.x_ref.ub_ref.ur_ref.u_ref, ...), custom_call_target="tpu_custom_call" | custom-call | flops 14495514624 | bytes 67108864 | tf_op jit(solution)/shard_map/base_products/pallas_call | solution.py:178
  522.2 32.8 %forcing_modes.1 = f32[4,2,16,64,256]{4,3,2,1,0:T(8,128)} custom-call(bf16[256,768]{1,0:T(8,128)(2,1)} %constant.175.clone.synth_ref, bf16[256,768]{1,0:T(8,128)(2,1)} %constant.176.clone.analysis_ref, f32[4,4,16,64,256]{4,3,2,1,0:T(8,128)} %all-to-all-done.1.x_ref.ub_ref.ur_ref.u_ref, f32[16,256,256]{2,1,0:T(8,128)} %get-tuple-element.64.vr_ref, ...), custom_call_target="tpu_custom_call" | custom-call | flops 6442450944 | bytes 33554432 | tf_op jit(solution)/shard_map/forcing_modes/pallas_call | solution.py:220
  555.0 10.4 %all-to-all-done.2.ur_ref = f32[4,1,16,64,256]{4,3,2,1,0:T(8,128)} async-done(((f32[4,1,16,64,256]{4,3,2,1,0:T(8,128)}), f32[4,1,16,64,256]{4,3,2,1,0:T(8,128)}, u32[]{:S(2)}, u32[]{:S(2)}) %all-to-all-start.2) | async-done | bytes 4194336 | tf_op jit(solution)/shard_map/all_to_all | solution.py:703
  565.4 9.9 %all-to-all-start.3 = ((f32[4,2,16,64,256]{4,3,2,1,0:T(8,128)}), f32[4,2,16,64,256]{4,3,2,1,0:T(8,128)}, u32[]{:S(2)}, u32[]{:S(2)}) async-start(f32[4,2,16,64,256]{4,3,2,1,0:T(8,128)} %forcing_modes.1), calls=%async_computation.3 | async-start | bytes 16777216 | tf_op jit(solution)/shard_map/all_to_all | solution.py:703
  576.8 20.8 %forcing_and_rims.1 = (f32[4,1,16,64,256]{4,3,2,1,0:T(8,128)}, f32[512,256]{1,0:T(8,128)}) custom-call(bf16[256,768]{1,0:T(8,128)(2,1)} %constant.175.clone.synth_ref, bf16[256,768]{1,0:T(8,128)(2,1)} %constant.176.clone.analysis_ref, f32[4,1,16,64,256]{4,3,2,1,0:T(8,128)} %all-to-all-done.2.ur_ref, ...), custom_call_target="tpu_custom_call" | custom-call | flops 6442450944 | bytes 20971520 | tf_op jit(solution)/shard_map/forcing_and_rims/pallas_call | solution.py:275
  610.9 92.9 %own_sums.1 = f32[4,1,16,64,256]{4,3,2,1,0:T(8,128)} custom-call(f32[4,1,16,64,256]{4,3,2,1,0:T(8,128)} %get-tuple-element.69.f_ref, f32[4,4,16,64,256]{4,3,2,1,0:T(8,128)} %all-to-all-done.1.x_ref.ub_ref.ur_ref.u_ref, f32[16,256]{1,0:T(8,128)} %constant_dynamic-slice_fusion.1.mass_ref, s32[16,256]{1,0:T(8,128)} %constant_dynamic-slice_fusion.conn_ref, ...), custom_call_target="tpu_custom_call" | custom-call | flops 17179869184 | bytes 12582912 | tf_op jit(solution)/shard_map/own_sums/pallas_call | solution.py:337
  703.8 50.1 %all-to-all-done.3.f_ref = f32[4,2,16,64,256]{4,3,2,1,0:T(8,128)} async-done(((f32[4,2,16,64,256]{4,3,2,1,0:T(8,128)}), f32[4,2,16,64,256]{4,3,2,1,0:T(8,128)}, u32[]{:S(2)}, u32[]{:S(2)}) %all-to-all-start.3) | async-done | bytes 8388640 | tf_op jit(solution)/shard_map/all_to_all | solution.py:703
  753.9 8.8 %all-to-all-start.4 = ((f32[4,1,16,64,256]{4,3,2,1,0:T(8,128)}), f32[4,1,16,64,256]{4,3,2,1,0:T(8,128)}, u32[]{:S(2)}, u32[]{:S(2)}) async-start(f32[4,1,16,64,256]{4,3,2,1,0:T(8,128)} %own_sums.1), calls=%async_computation.4 | async-start | bytes 8388608 | tf_op jit(solution)/shard_map/all_to_all | solution.py:703
  762.8 24.9 %local_sums.1 = (f32[16392,128]{1,0:T(8,128)}, f32[256,128]{1,0:T(8,128)}, f32[256,128]{1,0:T(8,128)}) custom-call(s32[3744]{0:T(1024)} %pad.14.codes, s32[10]{0:T(128)} %reshape.417.bnd, s32[2,256]{1,0:T(2,128)} %get-tuple-element.77.er, f32[4,2,16,64,256]{4,3,2,1,0:T(8,128)} %all-to-all-done.3.f_ref, f32[4,3,16,64,256]{4,3,2,1,0:T(8,128)} %node_major.2.x_ref.u_ref, ...), custom_call_target="tpu_custom_call" | custom-call | flops 838860800 | bytes 25165824 | tf_op jit(solution)/shard_map/local_sums/pallas_call | solution.py:518
  796.8 21.0 %spread.1._ = f32[3,64,64,256]{3,2,1,0:T(8,128)} custom-call(s32[3744]{0:T(1024)} %pad.14.codes, s32[10]{0:T(128)} %reshape.417.bnd, s32[2,256]{1,0:T(2,128)} %get-tuple-element.77.er, f32[16392,128]{1,0:T(8,128)} %get-tuple-element.80.t_ref, f32[256,128]{1,0:T(8,128)} %copy-done.4, f32[256,128]{1,0:T(8,128)} %copy-done.5, f32[64,256]{1,0:T(8,128)} %div.79.inv_ref), custom_call_target="tpu_custom_call" | custom-call | flops 838860800 | bytes 25165824 | tf_op jit(solution)/shard_map/spread/pallas_call | solution.py:584
  817.8 33.6 %all-to-all-done.4.f_ref.again_ref = f32[4,1,16,64,256]{4,3,2,1,0:T(8,128)} async-done(((f32[4,1,16,64,256]{4,3,2,1,0:T(8,128)}), f32[4,1,16,64,256]{4,3,2,1,0:T(8,128)}, u32[]{:S(2)}, u32[]{:S(2)}) %all-to-all-start.4) | async-done | bytes 4194336 | tf_op jit(solution)/shard_map/all_to_all | solution.py:703
  851.5 18.3 %finish.1 = f32[3,64,64,256]{3,2,1,0:T(8,128)} custom-call(s32[3744]{0:T(1024)} %pad.15.codes, s32[12]{0:T(128)} %reshape.421.bnd, s32[8]{0:T(128)} %convert_element_type.27.mark, f32[4,1,16,64,256]{4,3,2,1,0:T(8,128)} %all-to-all-done.4.f_ref.again_ref, f32[4,1,16,64,256]{4,3,2,1,0:T(8,128)} %all-to-all-done.4.f_ref.again_ref, ...), custom_call_target="tpu_custom_call", output_to_operand_aliasing={{}: (6, {})} | custom-call | flops 838860800 | bytes 12582912 | tf_op jit(solution)/shard_map/finish/pallas_call | solution.py:456
  (146 shorter events, 72.6 us)
Async XLA Ops:
  0.0 476.7 %copy-start = (f32[4,64,256]{2,1,0:T(8,128)S(1)}, f32[4,64,256]{2,1,0:T(8,128)}, u32[]{:S(2)}) copy-start(f32[4,64,256]{2,1,0:T(8,128)} %param.13) | copy-start | bytes 786436
  0.0 2.3 slice-start
  4.8 94.2 %all-to-all-start = ((f32[4,64,16,256]{3,2,1,0:T(8,128)}), f32[4,64,16,256]{3,2,1,0:T(8,128)}, u32[]{:S(2)}, u32[]{:S(2)}) async-start(f32[4,64,16,256]{3,2,1,0:T(8,128)} %bitcast.128), calls=%async_computation | async-start | bytes 8388608 | tf_op jit(solution)/shard_map/all_to_all | solution.py:703
  64.2 45.3 %copy-start.6 = (s32[1,2,225]{2,1,0:T(2,128)S(1)}, s32[1,2,225]{2,1,0:T(2,128)}, u32[]{:S(2)}) copy-start(s32[1,2,225]{2,1,0:T(2,128)} %param.16) | copy-start | bytes 5404
  64.2 45.4 %copy-start.2 = (s32[64,256]{1,0:T(8,128)S(1)}, s32[64,256]{1,0:T(8,128)}, u32[]{:S(2)}) copy-start(s32[64,256]{1,0:T(8,128)} %param.15) | copy-start | bytes 196612
  64.2 85.5 %copy-start.3 = (f32[64,256]{1,0:T(8,128)S(1)}, f32[64,256]{1,0:T(8,128)}, u32[]{:S(2)}) copy-start(f32[64,256]{1,0:T(8,128)} %mass_ref) | copy-start | bytes 196612
  99.0 368.7 %all-to-all-start.1 = ((f32[4,4,16,64,256]{4,3,2,1,0:T(8,128)}), f32[4,4,16,64,256]{4,3,2,1,0:T(8,128)}, u32[]{:S(2)}, u32[]{:S(2)}) async-start(f32[4,4,16,64,256]{4,3,2,1,0:T(8,128)} %pad_maximum_fusion), calls=%async_computation.1 | async-start | bytes 33554432 | tf_op jit(solution)/shard_map/all_to_all | solution.py:703
  114.0 274.5 %collective-permute-start.5 = (f32[4,256]{1,0:T(4,128)S(1)}, f32[4,256]{1,0:T(4,128)S(1)}, u32[]{:S(2)}, u32[]{:S(2)}) collective-permute-start(f32[4,256]{1,0:T(4,128)S(1)} %get-tuple-element.100), channel_id=1, source_target_pairs={{0,4},{4,8},{8,12},{12,16},{16,20},{20,24},{24,28},{28,0},{1,5},{5... | collective-permute-start | bytes 12296 | tf_op jit(solution)/shard_map/ppermute | solution.py:662
  117.0 271.6 %collective-permute-start.6 = (f32[4,256]{1,0:T(4,128)S(1)}, f32[4,256]{1,0:T(4,128)S(1)}, u32[]{:S(2)}, u32[]{:S(2)}) collective-permute-start(f32[4,256]{1,0:T(4,128)S(1)} %get-tuple-element.101), channel_id=1, source_target_pairs={{0,28},{4,0},{8,4},{12,8},{16,12},{20,16},{24,20},{28,24},{1,29},{... | collective-permute-start | bytes 12296 | tf_op jit(solution)/shard_map/ppermute | solution.py:662
  237.4 56.6 %collective-permute-start.3 = (f32[225]{0:T(256)S(1)}, f32[225]{0:T(256)S(1)}, u32[]{:S(2)}, u32[]{:S(2)}) collective-permute-start(f32[225]{0:T(256)S(1)} %gather_fusion.1), channel_id=1, source_target_pairs={{0,4},{4,8},{8,12},{12,16},{16,20},{20,24},{24,28},{28,0},{1,5},{5... | collective-permute-start | bytes 2708 | tf_op jit(solution)/shard_map/ppermute | solution.py:662
  240.9 53.1 %collective-permute-start.4 = (f32[225]{0:T(256)S(1)}, f32[225]{0:T(256)S(1)}, u32[]{:S(2)}, u32[]{:S(2)}) collective-permute-start(f32[225]{0:T(256)S(1)} %gather_fusion.2), channel_id=1, source_target_pairs={{0,28},{4,0},{8,4},{12,8},{16,12},{20,16},{24,20},{28,24},{1,29},{... | collective-permute-start | bytes 2708 | tf_op jit(solution)/shard_map/ppermute | solution.py:662
  389.2 3.2 collective-permute-start.7
  393.7 3.3 collective-permute-start.8
  397.6 2.4 collective-permute-start.9
  467.8 97.6 %all-to-all-start.2 = ((f32[4,1,16,64,256]{4,3,2,1,0:T(8,128)}), f32[4,1,16,64,256]{4,3,2,1,0:T(8,128)}, u32[]{:S(2)}, u32[]{:S(2)}) async-start(f32[4,1,16,64,256]{4,3,2,1,0:T(8,128)} %line_derivative.5), calls=%async_computation.2 | async-start | bytes 8388608 | tf_op jit(solution)/shard_map/all_to_all | solution.py:703
  565.4 188.5 %all-to-all-start.3 = ((f32[4,2,16,64,256]{4,3,2,1,0:T(8,128)}), f32[4,2,16,64,256]{4,3,2,1,0:T(8,128)}, u32[]{:S(2)}, u32[]{:S(2)}) async-start(f32[4,2,16,64,256]{4,3,2,1,0:T(8,128)} %forcing_modes.1), calls=%async_computation.3 | async-start | bytes 16777216 | tf_op jit(solution)/shard_map/all_to_all | solution.py:703
  598.7 7.3 collective-permute-start.10
  601.6 8.2 collective-permute-start.11
  753.9 97.6 %all-to-all-start.4 = ((f32[4,1,16,64,256]{4,3,2,1,0:T(8,128)}), f32[4,1,16,64,256]{4,3,2,1,0:T(8,128)}, u32[]{:S(2)}, u32[]{:S(2)}) async-start(f32[4,1,16,64,256]{4,3,2,1,0:T(8,128)} %own_sums.1), calls=%async_computation.4 | async-start | bytes 8388608 | tf_op jit(solution)/shard_map/all_to_all | solution.py:703
  787.7 5.1 collective-permute-start.12
  790.5 5.6 collective-permute-start.13
  792.8 3.3 copy-start.4
  796.1 0.7 copy-start.5
  851.5 18.3 %copy-start.1 = (f32[4,64,256]{2,1,0:T(8,128)S(1)}, f32[4,64,256]{2,1,0:T(8,128)}, u32[]{:S(2)}) copy-start(f32[4,64,256]{2,1,0:T(8,128)} %param.13) | copy-start | bytes 786436

commit v10 on v9

--- a/solution.py
+++ b/solution.py
@@ -14,7 +14,7 @@
 UNIQUE = 12825
 STEP_SIZE = 0.1
 LANES = 128
-BATCH = 32
+BATCH = 8
 CLASSES = 4
 PACK = 15
 BITS = 14
@@ -328,7 +328,8 @@
 
         high, low = split(rim_ref[...])
         total = product(jnp.concatenate([high, low], axis=1), same(id_ref[...]))
-        total = lax.fori_loop(0, l_n, lambda k, t: t + product(held[k], same(turned_ref[k])), total)
+        for k in range(l_n):
+            total = total + product(held[k], same(turned_ref[k]))
         o_ref[:, 0, 0] = total.reshape(s_n, m_n, e_n)
 
     def whole(*shape):

time: 886 us -> 884 us (level)
  Pallas kernels: 308 us -> 240 us
  waiting for transfers between devices: 208 us -> 276 us
    all_to_all x5, waiting for transfers between devices: 195 us -> 264 us  [exchange(): return lax.all_to_all(x, 'four', split_axis=0, concat_axis=0, tiled=True)]
    pallas_call x1, Pallas kernels: 92.9 us -> 30.4 us  [own_sums(): pl.pallas_call(kernel, grid=(l_n,), in_specs=[whole(s_n, 1, l_n, m_n, e_n...]
  transfers between devices with their start and end apart: 16 -> 16, of which waited for: 12 -> 12; matrix products, arithmetic and copies ran while one was open for 33% -> 33% of each run, Pallas kernels for 33% -> 26%
where the time goes in v10:
time: 884 us; the launch traced here: 868 us
  waiting for transfers between devices  276 us (31%)
  Pallas kernels  240 us (27%)
  local copies, waits for them, and re-layouts  147 us (17%)
  other arithmetic  141 us (16%)
  starting transfers between devices  60.8 us (7%)
    all_to_all x5, waiting for transfers between devices, exchange(): return lax.all_to_all(x, 'four', split_axis=0, concat_axis=0, tiled=True)  264 us
    gather x1, local copies, waits for them, and re-layouts, inverse_mass(): return (1.0 / summed[ids]).reshape(mass.shape)  90.5 us
    scatter-add x1, other arithmetic, inverse_mass(): summed = jnp.zeros((UNIQUE,), jnp.float32).at[ids].add(mass.reshape(-1))  85.8 us
    all_to_all x5, starting transfers between devices, exchange(): return lax.all_to_all(x, 'four', split_axis=0, concat_axis=0, tiled=True)  43 us
    pallas_call x4, Pallas kernels, derivative(): pl.pallas_call(kernel, grid=(c_n, m_n // rows), in_specs=[pl.BlockSpec(bl...  42.5 us
    pallas_call x1, Pallas kernels, forcing_modes(): pl.pallas_call(kernel, grid=(c_n, l_n), in_specs=[whole, whole, pl.BlockS...  32.8 us
    pallas_call x1, Pallas kernels, base_products(): pl.pallas_call(kernel, grid=(l_n,), in_specs=[pl.BlockSpec((2 * p_n, 3 *...  30.6 us
    pallas_call x1, Pallas kernels, own_sums(): pl.pallas_call(kernel, grid=(l_n,), in_specs=[whole(s_n, 1, l_n, m_n, e_n...  30.4 us
  transfers between devices with their start and end apart: 16, of which 12 were waited for; matrix products, arithmetic and copies ran while one was open for 33% of the time, Pallas kernels for 26%

profile of v10, /device:TPU:9, one launch (start us, length us, event | category | flops | bytes accessed | tf_op | source)
XLA Modules:
  0.0 868.3 jit_solution(17468364782633775737)
XLA Ops:
  4.8 4.9 all-to-all-start
  9.7 13.8 %node_major.2.x_ref.u_ref = f32[4,3,16,64,256]{4,3,2,1,0:T(8,128)} custom-call(f32[3,64,64,256]{3,2,1,0:T(8,128)} %x_ref), custom_call_target="tpu_custom_call" | custom-call | flops 3145728 | bytes 25165824 | tf_op jit(solution)/shard_map/node_major/pallas_call | solution.py:92
  23.5 7.7 slice.102
  31.2 7.6 line_derivative.5
  38.8 13.7 %line_derivative.4 = f32[4,2,16,64,256]{4,3,2,1,0:T(8,128)} custom-call(f32[4,3,16,64,256]{4,3,2,1,0:T(8,128)} %node_major.2.x_ref.u_ref), custom_call_target="tpu_custom_call" | custom-call | flops 33554432 | bytes 16777216 | tf_op jit(solution)/shard_map/line_derivative/pallas_call | solution.py:121
  52.5 11.7 %pad_maximum_fusion = f32[4,4,16,64,256]{4,3,2,1,0:T(8,128)} fusion(f32[4,2,16,64,256]{4,3,2,1,0:T(8,128)} %line_derivative.4, f32[4,2,16,64,256]{4,3,2,1,0:T(8,128)} %slice.102), kind=kLoop, calls=%fused_computation.10 | loop fusion | flops 4194304 | bytes 33554432 | tf_op jit(solution)/shard_map/concatenate | solution.py:729
  64.2 34.8 %all-to-all-done.x_ref = f32[4,64,16,256]{3,2,1,0:T(8,128)} async-done(((f32[4,64,16,256]{3,2,1,0:T(8,128)}), f32[4,64,16,256]{3,2,1,0:T(8,128)}, u32[]{:S(2)}, u32[]{:S(2)}) %all-to-all-start) | async-done | bytes 4194336 | tf_op jit(solution)/shard_map/all_to_all | solution.py:704
  99.0 10.4 %all-to-all-start.1 = ((f32[4,4,16,64,256]{4,3,2,1,0:T(8,128)}), f32[4,4,16,64,256]{4,3,2,1,0:T(8,128)}, u32[]{:S(2)}, u32[]{:S(2)}) async-start(f32[4,4,16,64,256]{4,3,2,1,0:T(8,128)} %pad_maximum_fusion), calls=%async_computation.1 | async-start | bytes 33554432 | tf_op jit(solution)/shard_map/all_to_all | solution.py:704
  109.8 3.9 compare_reduce_fusion
  117.0 6.3 sort.21
  131.4 8.9 %sort.22 = s32[16416]{0:T(1024)S(1)} sort(s32[16416]{0:T(1024)S(1)} %get-tuple-element.107), dimensions={0}, to_apply=%region_3.4 | sort | flops 246240 | bytes 131328 | tf_op jit(solution)/shard_map/sort | solution.py:615
  140.3 8.3 sort.23
  148.8 85.8 %scatter_custom_fusion = f32[12825]{0:T(1024)S(1)} fusion(s32[16384]{0:T(1024)S(1)} %bitcast.122, f32[16384]{0:T(1024)S(1)} %bitcast.126, f32[]{:T(128)} %constant.167.clone.1), kind=kCustom, calls=%fused_computation.85 | custom fusion | flops 16384 | bytes 51304 | tf_op jit(solution)/shard_map/scatter-add | solution.py:697
  240.1 10.5 %node_major.3 = f32[1,4,16,64,256]{4,3,2,1,0:T(8,128)} custom-call(f32[4,64,16,256]{3,2,1,0:T(8,128)} %all-to-all-done.x_ref), custom_call_target="tpu_custom_call" | custom-call | flops 1048576 | bytes 8388608 | tf_op jit(solution)/shard_map/node_major/pallas_call | solution.py:92
  250.6 7.5 line_derivative.6.usa_ref
  269.6 23.3 %copy.66 = bf16[12,256,16,256]{3,1,2,0:T(8,128)(2,1)} copy(bf16[12,256,16,256]{3,2,1,0:T(8,128)(2,1)} %param.12) | data formatting | bytes 50331648 | tf_op jit(solution)/shard_map/optimization_barrier | solution.py:730
  296.3 90.5 %gather_fusion.3 = f32[16384]{0:T(1024)S(1)} fusion(f32[12825]{0:T(1024)S(1)} %scatter_fusion, s32[16384]{0:T(1024)S(1)} %broadcast_clamp_fusion), kind=kCustom, calls=%fused_computation.3 | custom fusion | bytes 196608 | tf_op jit(solution)/shard_map/gather | solution.py:700
  400.3 67.5 %all-to-all-done.1.x_ref.ub_ref.ur_ref.u_ref = f32[4,4,16,64,256]{4,3,2,1,0:T(8,128)} async-done(((f32[4,4,16,64,256]{4,3,2,1,0:T(8,128)}), f32[4,4,16,64,256]{4,3,2,1,0:T(8,128)}, u32[]{:S(2)}, u32[]{:S(2)}) %all-to-all-start.1) | async-done | bytes 16777248 | tf_op jit(solution)/shard_map/all_to_all | solution.py:704
  467.8 8.9 %all-to-all-start.2 = ((f32[4,1,16,64,256]{4,3,2,1,0:T(8,128)}), f32[4,1,16,64,256]{4,3,2,1,0:T(8,128)}, u32[]{:S(2)}, u32[]{:S(2)}) async-start(f32[4,1,16,64,256]{4,3,2,1,0:T(8,128)} %line_derivative.5), calls=%async_computation.2 | async-start | bytes 8388608 | tf_op jit(solution)/shard_map/all_to_all | solution.py:704
  477.9 13.7 %line_derivative.7.usb_ref = f32[4,2,16,64,256]{4,3,2,1,0:T(8,128)} custom-call(f32[4,4,16,64,256]{4,3,2,1,0:T(8,128)} %all-to-all-done.1.x_ref.ub_ref.ur_ref.u_ref), custom_call_target="tpu_custom_call" | custom-call | flops 33554432 | bytes 16777216 | tf_op jit(solution)/shard_map/line_derivative/pallas_call | solution.py:121
  491.6 30.6 %base_products.1 = (f32[16,256,256]{2,1,0:T(8,128)}, f32[3,16,256,256]{3,2,1,0:T(8,128)}) custom-call(bf16[512,768]{1,0:T(8,128)(2,1)} %constant.174.clone.both_ref, bf16[256,768]{1,0:T(8,128)(2,1)} %constant.175.clone.synth_ref, f32[4,1,16,64,256]{4,3,2,1,0:T(8,128)} %bitcast.116, f32[4,4,16,64,256]{4,3,2,1,0:T(8,128)} %all-to-all-done.1.x_ref.ub_ref.ur_ref.u_ref, ...), custom_call_target="tpu_custom_call" | custom-call | flops 14495514624 | bytes 67108864 | tf_op jit(solution)/shard_map/base_products/pallas_call | solution.py:178
  522.2 32.8 %forcing_modes.1 = f32[4,2,16,64,256]{4,3,2,1,0:T(8,128)} custom-call(bf16[256,768]{1,0:T(8,128)(2,1)} %constant.175.clone.synth_ref, bf16[256,768]{1,0:T(8,128)(2,1)} %constant.176.clone.analysis_ref, f32[4,4,16,64,256]{4,3,2,1,0:T(8,128)} %all-to-all-done.1.x_ref.ub_ref.ur_ref.u_ref, f32[16,256,256]{2,1,0:T(8,128)} %get-tuple-element.64.vr_ref, ...), custom_call_target="tpu_custom_call" | custom-call | flops 6442450944 | bytes 33554432 | tf_op jit(solution)/shard_map/forcing_modes/pallas_call | solution.py:220
  555.0 10.4 %all-to-all-done.2.ur_ref = f32[4,1,16,64,256]{4,3,2,1,0:T(8,128)} async-done(((f32[4,1,16,64,256]{4,3,2,1,0:T(8,128)}), f32[4,1,16,64,256]{4,3,2,1,0:T(8,128)}, u32[]{:S(2)}, u32[]{:S(2)}) %all-to-all-start.2) | async-done | bytes 4194336 | tf_op jit(solution)/shard_map/all_to_all | solution.py:704
  565.4 9.9 %all-to-all-start.3 = ((f32[4,2,16,64,256]{4,3,2,1,0:T(8,128)}), f32[4,2,16,64,256]{4,3,2,1,0:T(8,128)}, u32[]{:S(2)}, u32[]{:S(2)}) async-start(f32[4,2,16,64,256]{4,3,2,1,0:T(8,128)} %forcing_modes.1), calls=%async_computation.3 | async-start | bytes 16777216 | tf_op jit(solution)/shard_map/all_to_all | solution.py:704
  576.8 20.6 %forcing_and_rims.1 = (f32[4,1,16,64,256]{4,3,2,1,0:T(8,128)}, f32[464,256]{1,0:T(8,128)}) custom-call(bf16[256,768]{1,0:T(8,128)(2,1)} %constant.175.clone.synth_ref, bf16[256,768]{1,0:T(8,128)(2,1)} %constant.176.clone.analysis_ref, f32[4,1,16,64,256]{4,3,2,1,0:T(8,128)} %all-to-all-done.2.ur_ref, ...), custom_call_target="tpu_custom_call" | custom-call | flops 6442450944 | bytes 20971520 | tf_op jit(solution)/shard_map/forcing_and_rims/pallas_call | solution.py:275
  610.1 30.4 %own_sums.1 = f32[4,1,16,64,256]{4,3,2,1,0:T(8,128)} custom-call(f32[4,1,16,64,256]{4,3,2,1,0:T(8,128)} %get-tuple-element.69.f_ref, f32[4,4,16,64,256]{4,3,2,1,0:T(8,128)} %all-to-all-done.1.x_ref.ub_ref.ur_ref.u_ref, f32[16,256]{1,0:T(8,128)} %constant_dynamic-slice_fusion.1.mass_ref, s32[16,256]{1,0:T(8,128)} %constant_dynamic-slice_fusion.conn_ref, ...), custom_call_target="tpu_custom_call" | custom-call | flops 17179869184 | bytes 12582912 | tf_op jit(solution)/shard_map/own_sums/pallas_call | solution.py:338
  640.5 113.4 %all-to-all-done.3.f_ref = f32[4,2,16,64,256]{4,3,2,1,0:T(8,128)} async-done(((f32[4,2,16,64,256]{4,3,2,1,0:T(8,128)}), f32[4,2,16,64,256]{4,3,2,1,0:T(8,128)}, u32[]{:S(2)}, u32[]{:S(2)}) %all-to-all-start.3) | async-done | bytes 8388640 | tf_op jit(solution)/shard_map/all_to_all | solution.py:704
  753.9 8.8 %all-to-all-start.4 = ((f32[4,1,16,64,256]{4,3,2,1,0:T(8,128)}), f32[4,1,16,64,256]{4,3,2,1,0:T(8,128)}, u32[]{:S(2)}, u32[]{:S(2)}) async-start(f32[4,1,16,64,256]{4,3,2,1,0:T(8,128)} %own_sums.1), calls=%async_computation.4 | async-start | bytes 8388608 | tf_op jit(solution)/shard_map/all_to_all | solution.py:704
  762.7 23.5 %local_sums.1 = (f32[16392,128]{1,0:T(8,128)}, f32[232,128]{1,0:T(8,128)}, f32[232,128]{1,0:T(8,128)}) custom-call(s32[3600]{0:T(1024)} %pad.14.codes, s32[10]{0:T(128)} %reshape.417.bnd, s32[2,232]{1,0:T(2,128)} %get-tuple-element.77.er, f32[4,2,16,64,256]{4,3,2,1,0:T(8,128)} %all-to-all-done.3.f_ref, f32[4,3,16,64,256]{4,3,2,1,0:T(8,128)} %node_major.2.x_ref.u_ref, ...), custom_call_target="tpu_custom_call" | custom-call | flops 838860800 | bytes 25165824 | tf_op jit(solution)/shard_map/local_sums/pallas_call | solution.py:519
  795.0 18.6 %spread.1._ = f32[3,64,64,256]{3,2,1,0:T(8,128)} custom-call(s32[3600]{0:T(1024)} %pad.14.codes, s32[10]{0:T(128)} %reshape.417.bnd, s32[2,232]{1,0:T(2,128)} %get-tuple-element.77.er, f32[16392,128]{1,0:T(8,128)} %get-tuple-element.80.t_ref, f32[232,128]{1,0:T(8,128)} %copy-done.4, f32[232,128]{1,0:T(8,128)} %copy-done.5, f32[64,256]{1,0:T(8,128)} %div.79.inv_ref), custom_call_target="tpu_custom_call" | custom-call | flops 838860800 | bytes 25165824 | tf_op jit(solution)/shard_map/spread/pallas_call | solution.py:585
  813.6 37.8 %all-to-all-done.4.f_ref.again_ref = f32[4,1,16,64,256]{4,3,2,1,0:T(8,128)} async-done(((f32[4,1,16,64,256]{4,3,2,1,0:T(8,128)}), f32[4,1,16,64,256]{4,3,2,1,0:T(8,128)}, u32[]{:S(2)}, u32[]{:S(2)}) %all-to-all-start.4) | async-done | bytes 4194336 | tf_op jit(solution)/shard_map/all_to_all | solution.py:704
  851.4 16.6 %finish.1 = f32[3,64,64,256]{3,2,1,0:T(8,128)} custom-call(s32[3600]{0:T(1024)} %pad.15.codes, s32[12]{0:T(128)} %reshape.421.bnd, s32[8]{0:T(128)} %convert_element_type.27.mark, f32[4,1,16,64,256]{4,3,2,1,0:T(8,128)} %all-to-all-done.4.f_ref.again_ref, f32[4,1,16,64,256]{4,3,2,1,0:T(8,128)} %all-to-all-done.4.f_ref.again_ref, ...), custom_call_target="tpu_custom_call", output_to_operand_aliasing={{}: (6, {})} | custom-call | flops 838860800 | bytes 12582912 | tf_op jit(solution)/shard_map/finish/pallas_call | solution.py:457
  (146 shorter events, 71.8 us)
Async XLA Ops:
  0.0 476.7 %copy-start = (f32[4,64,256]{2,1,0:T(8,128)S(1)}, f32[4,64,256]{2,1,0:T(8,128)}, u32[]{:S(2)}) copy-start(f32[4,64,256]{2,1,0:T(8,128)} %param.13) | copy-start | bytes 786436
  0.0 2.3 slice-start
  4.8 94.2 %all-to-all-start = ((f32[4,64,16,256]{3,2,1,0:T(8,128)}), f32[4,64,16,256]{3,2,1,0:T(8,128)}, u32[]{:S(2)}, u32[]{:S(2)}) async-start(f32[4,64,16,256]{3,2,1,0:T(8,128)} %bitcast.118), calls=%async_computation | async-start | bytes 8388608 | tf_op jit(solution)/shard_map/all_to_all | solution.py:704
  64.2 45.3 %copy-start.6 = (s32[1,2,225]{2,1,0:T(2,128)S(1)}, s32[1,2,225]{2,1,0:T(2,128)}, u32[]{:S(2)}) copy-start(s32[1,2,225]{2,1,0:T(2,128)} %param.16) | copy-start | bytes 5404
  64.2 45.4 %copy-start.2 = (s32[64,256]{1,0:T(8,128)S(1)}, s32[64,256]{1,0:T(8,128)}, u32[]{:S(2)}) copy-start(s32[64,256]{1,0:T(8,128)} %param.15) | copy-start | bytes 196612
  64.2 84.5 %copy-start.3 = (f32[64,256]{1,0:T(8,128)S(1)}, f32[64,256]{1,0:T(8,128)}, u32[]{:S(2)}) copy-start(f32[64,256]{1,0:T(8,128)} %mass_ref) | copy-start | bytes 196612
  99.0 368.7 %all-to-all-start.1 = ((f32[4,4,16,64,256]{4,3,2,1,0:T(8,128)}), f32[4,4,16,64,256]{4,3,2,1,0:T(8,128)}, u32[]{:S(2)}, u32[]{:S(2)}) async-start(f32[4,4,16,64,256]{4,3,2,1,0:T(8,128)} %pad_maximum_fusion), calls=%async_computation.1 | async-start | bytes 33554432 | tf_op jit(solution)/shard_map/all_to_all | solution.py:704
  113.7 273.8 %collective-permute-start.5 = (f32[4,232]{1,0:T(4,128)S(1)}, f32[4,232]{1,0:T(4,128)S(1)}, u32[]{:S(2)}, u32[]{:S(2)}) collective-permute-start(f32[4,232]{1,0:T(4,128)S(1)} %get-tuple-element.100), channel_id=1, source_target_pairs={{0,4},{4,8},{8,12},{12,16},{16,20},{20,24},{24,28},{28,0},{1,5},{5... | collective-permute-start | bytes 11144 | tf_op jit(solution)/shard_map/ppermute | solution.py:663
  116.7 270.9 %collective-permute-start.6 = (f32[4,232]{1,0:T(4,128)S(1)}, f32[4,232]{1,0:T(4,128)S(1)}, u32[]{:S(2)}, u32[]{:S(2)}) collective-permute-start(f32[4,232]{1,0:T(4,128)S(1)} %get-tuple-element.101), channel_id=1, source_target_pairs={{0,28},{4,0},{8,4},{12,8},{16,12},{20,16},{24,20},{28,24},{1,29},{... | collective-permute-start | bytes 11144 | tf_op jit(solution)/shard_map/ppermute | solution.py:663
  236.4 56.6 %collective-permute-start.3 = (f32[225]{0:T(256)S(1)}, f32[225]{0:T(256)S(1)}, u32[]{:S(2)}, u32[]{:S(2)}) collective-permute-start(f32[225]{0:T(256)S(1)} %gather_fusion.1), channel_id=1, source_target_pairs={{0,4},{4,8},{8,12},{12,16},{16,20},{20,24},{24,28},{28,0},{1,5},{5... | collective-permute-start | bytes 2708 | tf_op jit(solution)/shard_map/ppermute | solution.py:663
  239.9 53.1 %collective-permute-start.4 = (f32[225]{0:T(256)S(1)}, f32[225]{0:T(256)S(1)}, u32[]{:S(2)}, u32[]{:S(2)}) collective-permute-start(f32[225]{0:T(256)S(1)} %gather_fusion.2), channel_id=1, source_target_pairs={{0,28},{4,0},{8,4},{12,8},{16,12},{20,16},{24,20},{28,24},{1,29},{... | collective-permute-start | bytes 2708 | tf_op jit(solution)/shard_map/ppermute | solution.py:663
  388.2 3.2 collective-permute-start.7
  392.6 3.3 collective-permute-start.8
  396.6 2.4 collective-permute-start.9
  467.8 97.6 %all-to-all-start.2 = ((f32[4,1,16,64,256]{4,3,2,1,0:T(8,128)}), f32[4,1,16,64,256]{4,3,2,1,0:T(8,128)}, u32[]{:S(2)}, u32[]{:S(2)}) async-start(f32[4,1,16,64,256]{4,3,2,1,0:T(8,128)} %line_derivative.5), calls=%async_computation.2 | async-start | bytes 8388608 | tf_op jit(solution)/shard_map/all_to_all | solution.py:704
  565.4 188.5 %all-to-all-start.3 = ((f32[4,2,16,64,256]{4,3,2,1,0:T(8,128)}), f32[4,2,16,64,256]{4,3,2,1,0:T(8,128)}, u32[]{:S(2)}, u32[]{:S(2)}) async-start(f32[4,2,16,64,256]{4,3,2,1,0:T(8,128)} %forcing_modes.1), calls=%async_computation.3 | async-start | bytes 16777216 | tf_op jit(solution)/shard_map/all_to_all | solution.py:704
  598.5 6.8 collective-permute-start.10
  601.4 7.7 collective-permute-start.11
  753.9 97.6 %all-to-all-start.4 = ((f32[4,1,16,64,256]{4,3,2,1,0:T(8,128)}), f32[4,1,16,64,256]{4,3,2,1,0:T(8,128)}, u32[]{:S(2)}, u32[]{:S(2)}) async-start(f32[4,1,16,64,256]{4,3,2,1,0:T(8,128)} %own_sums.1), calls=%async_computation.4 | async-start | bytes 8388608 | tf_op jit(solution)/shard_map/all_to_all | solution.py:704
  786.2 5.0 collective-permute-start.12
  789.1 5.3 collective-permute-start.13
  791.2 3.2 copy-start.4
  794.4 0.7 copy-start.5
  851.4 16.6 %copy-start.1 = (f32[4,64,256]{2,1,0:T(8,128)S(1)}, f32[4,64,256]{2,1,0:T(8,128)}, u32[]{:S(2)}) copy-start(f32[4,64,256]{2,1,0:T(8,128)} %param.13) | copy-start | bytes 786436
